TPU v7x, 256 devices: a whole 4x4x8 slice. The times are simulated.
256 devices in a mesh: tm: 4 (over z_hi), feed: 64 (over y, z_lo, x, core).
Axes of the slice: x: 4, y: 4, z: 8 (z_hi: 4, z_lo: 2; z = z_hi * 2 + z_lo), core: 2. Of those that a mesh axis runs over, the one named last changes fastest.
Arguments:
- voltages: int32 [1024, 524288], P('feed', 'tm'), may hold values from -128 to 127
- window: float32 [4, 2048], replicated, may hold values from -0.04 to 0.04
- first_channel: int32 [1], replicated, may hold values from 0 to 512
Outputs:
- visibility: bfloat16 [1024, 512, 1024], P('tm', 'feed')
Inputs may be any that keep to these rules, and one draw needn't show every extreme that they name: first_channel[0] + 512 <= 1024.
All inputs are finite; a program needn't handle non-finite values.
Results may differ from a plain program's by a relative error of at most 0.0071.
Values may be sent and summed in bfloat16 or wider, within the bound.
No kernel may reach another device: no remote copies, remote signals or barrier semaphores. Data moves between devices by JAX's collectives and lax.ppermute only.
A program may use at most 128 MiB of HBM per device.

v0:
```python
import math

import jax
import jax.numpy as jnp
from jax import lax
from jax.sharding import PartitionSpec as P

CH_DEV = 8


def passed_along(x, axis, by):
    length = lax.axis_size(axis)
    pairs = [(i, i + by) for i in range(length) if 0 <= i + by < length]
    return lax.ppermute(x, axis, pairs)


def make_table(first_channel, frame_len, chan_count):
    sample_idx = lax.iota(jnp.int32, frame_len)
    chan_idx = first_channel[0] + lax.iota(jnp.int32, chan_count)
    phase_index = sample_idx[:, None] * chan_idx[None, :] % frame_len
    angles = phase_index.astype(jnp.float32) * jnp.float32(2.0 * math.pi / frame_len)
    norm_scale = jnp.float32(1.0 / math.sqrt(frame_len))
    return jnp.concatenate([jnp.cos(angles) * norm_scale, -jnp.sin(angles) * norm_scale], 1).astype(
        jnp.bfloat16
    )


def correlate(spectra_block, start_row, row_count):
    input_count = spectra_block.shape[2]
    row_block = lax.dynamic_slice_in_dim(spectra_block, start_row, row_count, 2)
    swapped = jnp.concatenate([row_block[:, :, :, 1:2], -row_block[:, :, :, 0:1]], 3)
    real_part = jnp.einsum(
        "tcirs,tcjrs->icj", row_block, spectra_block, preferred_element_type=jnp.float32
    )
    imag_part = jnp.einsum(
        "tcirs,tcjrs->icj", swapped, spectra_block, preferred_element_type=jnp.float32
    )
    row_ids = start_row + lax.iota(jnp.int32, row_count)
    lower_mask = row_ids[:, None, None] >= lax.iota(jnp.int32, input_count)[None, None, :]
    return jnp.where(lower_mask, real_part, imag_part)


def per_device(voltages, window, first_channel):
    inp_dev = voltages.shape[0]
    tap_count, frame_len = window.shape
    spec_dev = voltages.shape[1] // frame_len
    n_tm = lax.axis_size("tm")
    n_feed = lax.axis_size("feed")
    chan_count = CH_DEV * n_feed
    input_count = inp_dev * n_feed
    samples = voltages.astype(jnp.float32).reshape(inp_dev, spec_dev, frame_len)
    zero_frames = jnp.zeros((inp_dev, tap_count - 1, frame_len), jnp.float32)
    front_pad = jnp.concatenate([zero_frames, samples], 1)
    back_pad = jnp.concatenate([samples, zero_frames], 1)
    own_sum = jnp.zeros((inp_dev, spec_dev, frame_len), jnp.float32)
    for tap_index in range(tap_count):
        own_sum = (
            own_sum
            + window[tap_index][None, None, :]
            * front_pad[:, tap_count - 1 - tap_index : tap_count - 1 - tap_index + spec_dev]
        )
    carried = jnp.zeros((inp_dev, tap_count - 1, frame_len), jnp.float32)
    for tap_index in range(1, tap_count):
        carried = (
            carried
            + window[tap_index][None, None, :]
            * back_pad[:, spec_dev - tap_index : spec_dev - tap_index + tap_count - 1]
        )
    arrived = passed_along(carried.astype(jnp.bfloat16), "tm", 1)
    head_rows = own_sum[:, : tap_count - 1] + arrived.astype(jnp.float32)
    filtered = jnp.concatenate([head_rows, own_sum[:, tap_count - 1 :]], 1).astype(jnp.bfloat16)
    dft_table = make_table(first_channel, frame_len, chan_count).reshape(frame_len, 2, chan_count)
    spectra = jnp.einsum("nrc,isn->cirs", dft_table, filtered, preferred_element_type=jnp.float32)
    spectra = spectra.astype(jnp.bfloat16).reshape(1, chan_count, inp_dev * 2 * spec_dev)
    row_count = input_count // n_tm
    first_row = lax.axis_index("tm") * row_count
    norm_count = jnp.float32(spec_dev * n_tm)
    all_times = lax.all_gather(spectra, "tm", axis=0, tiled=True)
    turned = lax.all_to_all(all_times, "feed", split_axis=1, concat_axis=2, tiled=True)
    shaped = turned.reshape(n_tm, CH_DEV, input_count, 2, spec_dev)
    summed = correlate(shaped, first_row, row_count)
    return (summed / norm_count).astype(jnp.bfloat16)


def solution(mesh):
    in_specs = (P("feed", "tm"), P(), P())
    out_specs = P("tm", "feed", None)
    return jax.shard_map(
        per_device, mesh=mesh, in_specs=in_specs, out_specs=out_specs, check_vma=False
    )
```

profile of v0, /device:TPU:1, one launch (start us, length us, event | category | flops | bytes accessed | tf_op | source)
XLA Modules:
  0.0 471.8 jit_solution(6325245082160685162)
XLA Ops:
  6.5 0.0 all-gather.2.cloned.1.call-start
  6.5 0.9 fusion.34
  7.5 3.9 convert_element_type.32
  11.4 4.9 %copy.22 = f32[2,8,64,2048]{3,2,1,0:T(8,128)S(1)} copy(f32[2,8,64,2048]{3,1,2,0:T(8,128)S(1)} %bitcast.51) | data formatting | bytes 16777216
  16.3 0.4 fusion.30
  16.7 6.0 %collective-permute-start = (bf16[16,3,2048]{2,1,0:T(4,128)(2,1)S(1)}, bf16[16,3,2048]{2,1,0:T(4,128)(2,1)S(1)}, u32[]{:S(2)}, u32[]{:S(2)}) collective-permute-start(bf16[16,3,2048]{2,1,0:T(4,128)(2,1)S(1)} %fusion.30), channel_id=1, source_target_pairs={{0,64},{64,128},{128,192},{1,65},{65,129},{129,193},{2,66},{66,130... | collective-permute-start | bytes 589832 | tf_op jit(solution)/shard_map/ppermute | solution.py:14
  22.7 5.6 %fusion.3 = f32[16,64,2048]{2,1,0:T(8,128)} fusion(f32[16,64,2048]{2,1,0:T(8,128)S(1)} %bitcast.49, f32[2048]{0:T(1024)S(1)} %bitcast.56, f32[2048]{0:T(1024)S(1)} %bitcast.58, f32[2048]{0:T(1024)S(1)} %bitcast.54, f32[2048]{0:T(1024)S(1)} %bitcast.59), kind=kLoop, calls=%fused_computation.8 | loop fusion | flops 14680064 | bytes 16809984 | tf_op jit(solution)/shard_map/add | solution.py:58
  29.0 17.1 %multiply_convert_fusion.1 = (bf16[2048,1,512]{2,0,1:T(8,128)(2,1)S(1)}, bf16[2048,1,512]{2,0,1:T(8,128)(2,1)S(1)}) fusion(s32[512]{0:T(512)S(1)} %iota_add_fusion), kind=kLoop, calls=%fused_computation.30 | loop fusion | flops 19922944 | bytes 4196352 | tf_op jit(solution)/shard_map/convert
  46.1 4.6 slice.107
  50.7 0.0 collective-permute-done
  50.7 1.4 fusion.29
  52.1 4.5 fusion.24
  56.6 2.4 copy.11
  59.0 0.0 all-gather.2.cloned.1.call-update
  59.0 156.9 %all-gather.2.cloned.1.call-done = bf16[4,512,2048]{2,1,0:T(8,128)(2,1)} async-done(((bf16[1,512,2048]{2,1,0:T(8,128)(2,1)}), bf16[4,512,2048]{2,1,0:T(8,128)(2,1)}) %all-gather.2.cloned.1.call-update) | async-done | bytes 8388624 | tf_op jit(solution)/shard_map/all_gather | solution.py:78
  215.9 12.1 %copy.12 = bf16[4,512,2048]{2,0,1:T(4,128)(2,1)} copy(bf16[4,512,2048]{2,1,0:T(8,128)(2,1)} %all-gather.2.cloned.1.call-done) | data formatting | bytes 16777216 | tf_op jit(solution)/shard_map/all_gather | solution.py:78
  228.0 9.6 %all-to-all-start = ((bf16[4,512,2048]{2,0,1:T(4,128)(2,1)}), bf16[4,512,2048]{2,0,1:T(4,128)(2,1)}, u32[]{:S(2)}, u32[]{:S(2)}) async-start(bf16[4,512,2048]{2,0,1:T(4,128)(2,1)} %copy.12), calls=%async_computation | async-start | bytes 16777216 | tf_op jit(solution)/shard_map/all_to_all | solution.py:79
  237.7 0.2 iota_compare_fusion
  237.8 105.7 %all-to-all-done = bf16[4,512,2048]{2,0,1:T(4,128)(2,1)} async-done(((bf16[4,512,2048]{2,0,1:T(4,128)(2,1)}), bf16[4,512,2048]{2,0,1:T(4,128)(2,1)}, u32[]{:S(2)}, u32[]{:S(2)}) %all-to-all-start) | async-done | bytes 8388640 | tf_op jit(solution)/shard_map/all_to_all | solution.py:79
  343.6 11.2 %copy.24 = bf16[4,512,2048]{2,1,0:T(8,128)(2,1)} copy(bf16[4,512,2048]{2,0,1:T(4,128)(2,1)} %all-to-all-done) | data formatting | bytes 16777216 | tf_op jit(solution)/shard_map/all_to_all | solution.py:79
  354.8 11.4 %copy.14 = bf16[4,8,64,2048]{3,2,1,0:T(8,128)(2,1)} copy(bf16[4,8,64,2048]{3,1,2,0:T(8,128)(2,1)} %bitcast.50) | data formatting | bytes 16777216 | tf_op jit(solution)/shard_map/all_to_all | solution.py:79
  366.2 29.9 %reshape.115 = bf16[4,8,1024,2,64]{4,3,2,1,0:T(2,128)(2,1)} reshape(bf16[4,8,64,2048]{3,2,1,0:T(8,128)(2,1)} %copy.14) | data formatting | bytes 16777216 | tf_op jit(solution)/shard_map/reshape | solution.py:80
  396.1 39.3 %copy.16 = bf16[4,8,1024,2,64]{2,4,0,3,1:T(8,128)(2,1)} copy(bf16[4,8,1024,2,64]{4,3,2,1,0:T(2,128)(2,1)} %reshape.115) | data formatting | bytes 16777216 | tf_op jit(solution)/shard_map/reshape | solution.py:80
  435.4 9.9 %fusion.22 = f32[8,1024,256,1,1]{2,1,4,3,0:T(8,128)} fusion(bf16[4,8,1024,2,64]{2,4,0,3,1:T(8,128)(2,1)} %copy.16, s32[]{:T(128)S(6)} %select_n.23), kind=kOutput, calls=%fused_computation.37 | convolution fusion | flops 2147483648 | bytes 18874372 | tf_op jit(solution)/shard_map/tcirs,tcjrs->icj/dot_general | solution.py:32
  445.4 1.9 constant_dynamic-slice_fusion
  447.3 10.8 %fusion.7 = bf16[256,8,1024]{0,2,1:T(8,128)(2,1)} fusion(f32[8,1024,256,1,1]{2,1,4,3,0:T(8,128)} %fusion.22, pred[256,1024]{0,1:T(8,128)(4,1)S(1)} %iota_compare_fusion, bf16[4,8,1024,2,64]{2,4,0,3,1:T(8,128)(2,1)} %copy.16, bf16[4,8,256,1,64]{2,4,0,3,1:T(8,128)(2,1)S(1)} %get-tuple-element.6, bf16[4,8,256,1,64]{2,4,0,3,1:T(8,128)(2,1)S(1)} %get-tuple-element.5), kind=kOutput, calls=%fused_computation.14 | convolution fusion | flops 2154823680 | bytes 23330816 | tf_op jit(solution)/shard_map/tcirs,tcjrs->icj/dot_general | solution.py:35
  458.1 6.7 %copy.18 = bf16[256,8,1024]{2,1,0:T(8,128)(2,1)} copy(bf16[256,8,1024]{0,2,1:T(8,128)(2,1)} %fusion.7) | data formatting | bytes 8388608 | tf_op jit(solution)/shard_map/convert_element_type | solution.py:82
  (2 shorter events, 0.0 us)
Async XLA Ops:
  6.5 209.4 %all-gather.2.cloned.1.call-start = ((), (), s32[]{:S(2)}) async-start(), calls=%async_computation.1 | async-start | bytes 10485760 | tf_op jit(solution)/shard_map/all_gather | solution.py:78
  16.7 34.0 %collective-permute-start = (bf16[16,3,2048]{2,1,0:T(4,128)(2,1)S(1)}, bf16[16,3,2048]{2,1,0:T(4,128)(2,1)S(1)}, u32[]{:S(2)}, u32[]{:S(2)}) collective-permute-start(bf16[16,3,2048]{2,1,0:T(4,128)(2,1)S(1)} %fusion.30), channel_id=1, source_target_pairs={{0,64},{64,128},{128,192},{1,65},{65,129},{129,193},{2,66},{66,130... | collective-permute-start | bytes 589832 | tf_op jit(solution)/shard_map/ppermute | solution.py:14
  228.0 115.5 %all-to-all-start = ((bf16[4,512,2048]{2,0,1:T(4,128)(2,1)}), bf16[4,512,2048]{2,0,1:T(4,128)(2,1)}, u32[]{:S(2)}, u32[]{:S(2)}) async-start(bf16[4,512,2048]{2,0,1:T(4,128)(2,1)} %copy.12), calls=%async_computation | async-start | bytes 16777216 | tf_op jit(solution)/shard_map/all_to_all | solution.py:79
Sparse Core Ops, SparseCore 0:
  59.2 156.6 all-gather.1
where the time goes:
time: 479 us; the launch traced here: 472 us
  waiting for transfers between devices  263 us (55%)
  local copies, waits for them, and re-layouts  123 us (26%)
  other arithmetic  30.6 us (6%)
  matrix products  25.3 us (5%)
  starting transfers between devices  15.6 us (3%)
  between operations  14.3 us (3%)
    all_gather x1, waiting for transfers between devices, per_device(): all_times = lax.all_gather(spectra, 'tm', axis=0, tiled=True)  157 us
    all_to_all x1, waiting for transfers between devices, per_device(): lax.all_to_all(all_times, 'feed', split_axis=1, concat_axis=2, tiled=True)  106 us
    reshape x2, local copies, waits for them, and re-layouts, per_device(): shaped = turned.reshape(n_tm, CH_DEV, input_count, 2, spec_dev)  69.2 us
    all_to_all x2, local copies, waits for them, and re-layouts, per_device(): lax.all_to_all(all_times, 'feed', split_axis=1, concat_axis=2, tiled=True)  22.6 us
    another operation x2, other arithmetic  18.5 us
    all_gather x1, local copies, waits for them, and re-layouts, per_device(): all_times = lax.all_gather(spectra, 'tm', axis=0, tiled=True)  12.1 us
    dot_general x1, matrix products, correlate(): jnp.einsum('tcirs,tcjrs->icj', swapped, spectra_block, preferred_element_...  10.8 us
    dot_general x1, matrix products, correlate(): jnp.einsum('tcirs,tcjrs->icj', row_block, spectra_block, preferred_elemen...  9.91 us
  transfers between devices with their start and end apart: 3, of which 2 were waited for; matrix products, arithmetic and copies ran while one was open for 6% of the time, Pallas kernels for 0%

commit v1 on v0

v1 whole, which is shorter than its diff:
```python
import functools
import math

import jax
import jax.numpy as jnp
from jax import lax
from jax.experimental import pallas as pl
from jax.experimental.pallas import tpu as pltpu
from jax.sharding import PartitionSpec as P

FRAME = 2048
TAPS = 4
INP = 16
SPEC = 64
INPUTS = 1024
N_TM = 4
N_FEED = 64
CH_DEV = 8
FRAME_BLOCK = 8
LANES = 256
COARSE = 32
FINE = FRAME // COARSE
ROWS = INPUTS // N_TM
PIECE = 2 * SPEC
MIB = 1 << 20


def params(mib):
    return pltpu.CompilerParams(vmem_limit_bytes=mib * MIB)


def ring(by):
    return [(i, (i + by) % N_TM) for i in range(N_TM)]


def to_right(x):
    return lax.ppermute(x, "tm", ring(1))


def to_left(x):
    return lax.ppermute(x, "tm", ring(-1))


def carry_kernel(v_ref, w_ref, out_ref):
    for head in range(TAPS - 1):
        for start in range(0, FRAME, LANES):
            total = jnp.zeros((INP, LANES), jnp.float32)
            for tap in range(head + 1, TAPS):
                at = (4 + head - tap) * FRAME + start
                total = total + w_ref[tap : tap + 1, start : start + LANES] * v_ref[
                    :, at : at + LANES
                ].astype(jnp.float32)
            out_ref[head * INP : (head + 1) * INP, start : start + LANES] = total.astype(jnp.bfloat16)


def carry(voltages, window):
    last = voltages.shape[1] // (4 * FRAME) - 1
    return pl.pallas_call(
        carry_kernel,
        grid=(1,),
        in_specs=[
            pl.BlockSpec((INP, 4 * FRAME), lambda g: (0, last)),
            pl.BlockSpec((TAPS, FRAME), lambda g: (0, 0)),
        ],
        out_specs=pl.BlockSpec(((TAPS - 1) * INP, FRAME), lambda g: (0, 0)),
        out_shape=jax.ShapeDtypeStruct(((TAPS - 1) * INP, FRAME), jnp.bfloat16),
        compiler_params=params(32),
        name="carry",
    )(voltages, window)


def filter_kernel(v_ref, w_ref, out_ref, head_ref, past):
    step = pl.program_id(0)

    @pl.when(step == 0)
    def _():
        past[...] = jnp.zeros_like(past)

    for start in range(0, FRAME, LANES):
        cols = slice(start, start + LANES)
        taps = [
            jnp.broadcast_to(w_ref[p : p + 1, cols], (INP, LANES)) for p in range(TAPS)
        ]
        seen = [past[p, :, cols] for p in range(TAPS - 1)]
        for k in range(FRAME_BLOCK):
            now = v_ref[:, k * FRAME + start : k * FRAME + start + LANES].astype(jnp.float32)
            total = taps[0] * now
            for p in range(1, TAPS):
                total = total + taps[p] * seen[p - 1]
            out_ref[k * INP : (k + 1) * INP, cols] = total.astype(jnp.bfloat16)
            if k < TAPS - 1:

                @pl.when(step == 0)
                def _():
                    head_ref[k * INP : (k + 1) * INP, cols] = total

            seen = [now] + seen[:-1]
        for p in range(TAPS - 1):
            past[p, :, cols] = seen[p]


def filter_own(voltages, window):
    steps = SPEC // FRAME_BLOCK
    head_rows = (TAPS - 1) * INP
    return pl.pallas_call(
        filter_kernel,
        grid=(steps,),
        in_specs=[
            pl.BlockSpec((INP, FRAME_BLOCK * FRAME), lambda g: (0, g)),
            pl.BlockSpec((TAPS, FRAME), lambda g: (0, 0)),
        ],
        out_specs=[
            pl.BlockSpec((FRAME_BLOCK * INP, FRAME), lambda g: (g, 0)),
            pl.BlockSpec((head_rows, FRAME), lambda g: (0, 0)),
        ],
        out_shape=[
            jax.ShapeDtypeStruct((SPEC * INP, FRAME), jnp.bfloat16),
            jax.ShapeDtypeStruct((head_rows, FRAME), jnp.float32),
        ],
        scratch_shapes=[pltpu.VMEM((TAPS - 1, INP, FRAME), jnp.float32)],
        compiler_params=params(32),
        name="own_filter",
    )(voltages, window)


def table_kernel(coarse_cos, coarse_sin, fine_cos, fine_sin, out_ref):
    half = fine_cos.shape[1] // 2
    for piece in range(2):
        cols = slice(piece * half, (piece + 1) * half)
        for a in range(COARSE):
            ac, as_ = coarse_cos[a : a + 1, cols], coarse_sin[a : a + 1, cols]
            bc, bs = fine_cos[:, cols], fine_sin[:, cols]
            rows = slice(a * FINE, (a + 1) * FINE)
            out_ref[piece, rows, :half] = (ac * bc - as_ * bs).astype(jnp.bfloat16)
            out_ref[piece, rows, half:] = (-(as_ * bc) - ac * bs).astype(jnp.bfloat16)


def table(first_channel, position, which):
    column = lax.iota(jnp.int32, N_FEED * N_TM)
    group = (position + column % N_TM) % N_TM
    channel = first_channel[0] + column // N_TM * CH_DEV + 2 * group + which

    def waves(samples):
        phase = samples[:, None] * channel[None, :] % FRAME
        angle = phase.astype(jnp.float32) * jnp.float32(2.0 * math.pi / FRAME)
        return jnp.cos(angle), jnp.sin(angle)

    scale = jnp.float32(1.0 / math.sqrt(FRAME))
    coarse = waves(FINE * lax.iota(jnp.int32, COARSE))
    fine = waves(lax.iota(jnp.int32, FINE))
    return pl.pallas_call(
        table_kernel,
        out_shape=jax.ShapeDtypeStruct((2, FRAME, N_FEED * N_TM), jnp.bfloat16),
        compiler_params=params(32),
        name="dft_table",
    )(coarse[0], coarse[1], fine[0] * scale, fine[1] * scale)


def dft_kernel(f_ref, head_ref, arrived_ref, t_ref, out_ref, fixed, wide, turned):
    head_rows = head_ref.shape[0]

    @pl.when(pl.program_id(0) == 0)
    def _():
        fixed[...] = (head_ref[...] + arrived_ref[...].astype(jnp.float32)).astype(jnp.bfloat16)

    first = jnp.dot(fixed[...], t_ref[0], preferred_element_type=jnp.float32)
    rest = jnp.dot(f_ref[head_rows:, :], t_ref[0], preferred_element_type=jnp.float32)
    for r in range(2):
        wide[r, :head_rows, :] = first[:, r * 128 : (r + 1) * 128]
        wide[r, head_rows:, :] = rest[:, r * 128 : (r + 1) * 128]
    for i in range(INP):
        rows = pl.ds(i, SPEC, stride=INP)
        both = jnp.concatenate([wide[0, rows, :], wide[1, rows, :]], 0)
        turned[pl.ds(i, 128, stride=INP), :] = both.T
    out_ref[...] = turned[...].astype(jnp.bfloat16).reshape(out_ref.shape)


def dft(filtered, head, arrived, dft_table):
    steps = dft_table.shape[0]
    whole = lambda g: (0, 0)
    return pl.pallas_call(
        dft_kernel,
        grid=(steps,),
        in_specs=[
            pl.BlockSpec(filtered.shape, whole),
            pl.BlockSpec(head.shape, whole),
            pl.BlockSpec(arrived.shape, whole),
            pl.BlockSpec((1, FRAME, 256), lambda g: (g, 0, 0)),
        ],
        out_specs=pl.BlockSpec((128, INP, PIECE), lambda g: (g, 0, 0)),
        out_shape=jax.ShapeDtypeStruct((steps * 128, INP, PIECE), jnp.bfloat16),
        scratch_shapes=[
            pltpu.VMEM(head.shape, jnp.bfloat16),
            pltpu.VMEM((2, SPEC * INP, 128), jnp.float32),
            pltpu.VMEM((128 * INP, PIECE), jnp.float32),
        ],
        compiler_params=params(48),
        name="dft",
    )(filtered, head, arrived, dft_table)


def correlate_kernel(row_ref, *refs):
    pieces, out_ref = refs[:N_TM], refs[N_TM]
    block = row_ref[0]
    at = pl.ds(pl.multiple_of(block * ROWS, ROWS), ROWS)
    mine = [piece[at, :] for piece in pieces]
    plain = jnp.concatenate(mine, 1)
    crossed = jnp.concatenate(
        [x for m in mine for x in (m[:, SPEC:], -m[:, :SPEC])], 1
    )
    scale = jnp.float32(1.0 / (SPEC * N_TM))
    contract = (((1,), (1,)), ((), ()))
    for other in range(N_TM):
        cols = slice(other * ROWS, (other + 1) * ROWS)
        left = jnp.where(other <= block, plain, crossed)
        right = jnp.concatenate([piece[cols, :] for piece in pieces], 1)
        part = lax.dot_general(left, right, contract, preferred_element_type=jnp.float32)
        out_ref[:, cols] = (part * scale).astype(jnp.bfloat16)
    part = lax.dot_general(crossed, plain, contract, preferred_element_type=jnp.float32)
    lower = lax.broadcasted_iota(jnp.int32, (ROWS, ROWS), 0) >= lax.broadcasted_iota(
        jnp.int32, (ROWS, ROWS), 1
    )
    both = jnp.where(lower, out_ref[:, at].astype(jnp.float32), part * scale)
    out_ref[:, at] = both.astype(jnp.bfloat16)


def correlate(block, pieces):
    vmem = pl.BlockSpec(memory_space=pltpu.VMEM)
    return pl.pallas_call(
        correlate_kernel,
        in_specs=[pl.BlockSpec(memory_space=pltpu.SMEM)] + [vmem] * N_TM,
        out_specs=vmem,
        out_shape=jax.ShapeDtypeStruct((ROWS, INPUTS), jnp.bfloat16),
        compiler_params=params(32),
        name="correlate",
    )(block.astype(jnp.int32).reshape(1), *pieces)


def gather_kernel(position_ref, *refs):
    planes, out_ref, wide = refs[:CH_DEV], refs[CH_DEV], refs[CH_DEV + 1]
    rows = planes[0].shape[0]
    for place in range(CH_DEV):
        channel = 2 * lax.rem(position_ref[0] + place // 2, N_TM) + place % 2
        for part in range(INPUTS // 128):
            cols = slice(part * 128, (part + 1) * 128)
            wide[part, pl.ds(channel, rows, stride=CH_DEV), :] = planes[place][:, cols].astype(
                jnp.float32
            )
    for part in range(INPUTS // 128):
        cols = slice(part * 128, (part + 1) * 128)
        out_ref[:, :, cols] = wide[part].astype(jnp.bfloat16).reshape(rows, CH_DEV, 128)


def gather_planes(position, planes):
    block = 64
    return pl.pallas_call(
        gather_kernel,
        grid=(ROWS // block,),
        in_specs=[pl.BlockSpec(memory_space=pltpu.SMEM)]
        + [pl.BlockSpec((block, INPUTS), lambda g: (g, 0))] * CH_DEV,
        out_specs=pl.BlockSpec((block, CH_DEV, INPUTS), lambda g: (g, 0, 0)),
        out_shape=jax.ShapeDtypeStruct((ROWS, CH_DEV, INPUTS), jnp.bfloat16),
        scratch_shapes=[pltpu.VMEM((INPUTS // 128, block * CH_DEV, 128), jnp.float32)],
        compiler_params=params(32),
        name="gather_planes",
    )(position.astype(jnp.int32).reshape(1), *planes)


def per_device(voltages, window, first_channel):
    position = lax.axis_index("tm")
    after, before = (position + 1) % N_TM, (position + N_TM - 1) % N_TM
    arrived = lax.ppermute(carry(voltages, window), "tm", [(i, i + 1) for i in range(N_TM - 1)])
    tables = [table(first_channel, position, which) for which in range(2)]
    filtered, head = filter_own(voltages, window)
    planes = [None] * CH_DEV
    for which in range(2):
        spectra = dft(filtered, head, arrived, tables[which])
        turned = lax.all_to_all(spectra, "feed", split_axis=0, concat_axis=0, tiled=True)
        turned = turned.reshape(N_FEED, N_TM, INP, PIECE)
        own = [turned[:, p].reshape(INPUTS, PIECE) for p in range(N_TM)]
        left_1, right_2 = to_right(own[1]), to_left(own[2])
        left_0, right_3 = to_right(own[0]), to_left(own[3])
        far_right, far_left = to_left(right_2), to_right(left_1)
        here = [own[0], left_1, right_3, far_right]
        there = [own[3], left_0, right_2, far_left]
        from_right = to_left(correlate(before, here))
        from_left = to_right(correlate(after, there))
        planes[0 + which] = correlate(position, here)
        planes[2 + which] = from_right
        planes[4 + which] = from_left
        planes[6 + which] = correlate(position, there)
    return gather_planes(position, planes)


def solution(mesh):
    in_specs = (P("feed", "tm"), P(), P())
    out_specs = P("tm", "feed", None)
    return jax.shard_map(
        per_device, mesh=mesh, in_specs=in_specs, out_specs=out_specs, check_vma=False
    )
```

time: 479 us -> 209 us (0.44); the launches traced: 472 us -> 208 us
  waiting for transfers between devices: 263 us -> 94.7 us
  local copies, waits for them, and re-layouts: 123 us -> 7.21 us
  starting transfers between devices: 15.6 us -> 72.7 us
  Pallas kernels: 0 us -> 31.9 us
  other arithmetic: 30.6 us -> 0.91 us
  matrix products: 25.3 us -> 0 us
  between operations: 14.3 us -> 0.84 us
    all_gather x1 -> x0, waiting for transfers between devices: 157 us -> none  [per_device(): all_times = lax.all_gather(spectra, 'tm', axis=0, tiled=True)]
    all_to_all x1 -> x2, waiting for transfers between devices: 106 us -> 24.1 us  [per_device(): lax.all_to_all(spectra, 'feed', split_axis=0, concat_axis=0, tiled=True)]
    reshape x3 -> x0, local copies, waits for them, and re-layouts: 71.6 us -> none  [the longest x2 69.2 us: per_device(): shaped = turned.reshape(n_tm, CH_DEV, input_count, 2, spec_dev)]
    ppermute x1 -> x17, waiting for transfers between devices: 0.01 us -> 70.6 us  [the longest x8 40.6 us: to_right(): return lax.ppermute(x, 'tm', ring(1))]
    ppermute x1 -> x17, starting transfers between devices: 5.99 us -> 58.1 us  [the longest x8 36.6 us: to_right(): return lax.ppermute(x, 'tm', ring(1))]
    pallas_call x0 -> x15, Pallas kernels: none -> 31.9 us  [the longest x2 13.9 us: dft(): pl.pallas_call(dft_kernel, grid=(steps,), in_specs=[pl.BlockSpec(filtered...]
    dot_general x3 -> x0, matrix products: 25.3 us -> none  [the longest x1 10.8 us: correlate(): jnp.einsum('tcirs,tcjrs->icj', swapped, spectra_block, preferred_element_...]
    all_to_all x2 -> x0, local copies, waits for them, and re-layouts: 22.6 us -> none  [per_device(): lax.all_to_all(all_times, 'feed', split_axis=1, concat_axis=2, tiled=True)]
  transfers between devices with their start and end apart: 3 -> 19, of which waited for: 2 -> 12; matrix products, arithmetic and copies ran while one was open for 6% -> 1% of each run, Pallas kernels for 0% -> 10%
where the time goes in v1:
time: 209 us; the launch traced here: 208 us
  waiting for transfers between devices  94.7 us (45%)
  starting transfers between devices  72.7 us (35%)
  Pallas kernels  31.9 us (15%)
  local copies, waits for them, and re-layouts  7.21 us (3%)
    ppermute x8, waiting for transfers between devices, to_right(): return lax.ppermute(x, 'tm', ring(1))  40.6 us
    ppermute x8, starting transfers between devices, to_right(): return lax.ppermute(x, 'tm', ring(1))  36.6 us
    ppermute x8, waiting for transfers between devices, to_left(): return lax.ppermute(x, 'tm', ring(-1))  30 us
    all_to_all x2, waiting for transfers between devices, per_device(): lax.all_to_all(spectra, 'feed', split_axis=0, concat_axis=0, tiled=True)  24.1 us
    ppermute x8, starting transfers between devices, to_left(): return lax.ppermute(x, 'tm', ring(-1))  15.8 us
    all_to_all x2, starting transfers between devices, per_device(): lax.all_to_all(spectra, 'feed', split_axis=0, concat_axis=0, tiled=True)  14.6 us
    pallas_call x2, Pallas kernels, dft(): pl.pallas_call(dft_kernel, grid=(steps,), in_specs=[pl.BlockSpec(filtered...  13.9 us
    pallas_call x8, Pallas kernels, correlate(): pl.pallas_call(correlate_kernel, in_specs=[pl.BlockSpec(memory_space=pltp...  9.03 us
  transfers between devices with their start and end apart: 19, of which 12 were waited for; matrix products, arithmetic and copies ran while one was open for 1% of the time, Pallas kernels for 10%

profile of v1, /device:TPU:1, one launch (start us, length us, event | category | flops | bytes accessed | tf_op | source)
XLA Modules:
  0.0 208.2 jit_solution(13756879864308818721)
XLA Ops:
  0.0 3.4 %copy-done = s32[16,131072]{1,0:T(8,128)S(1)} copy-done((s32[16,131072]{1,0:T(8,128)S(1)}, s32[16,131072]{1,0:T(8,128)}, u32[]{:S(2)}) %copy-start) | copy-done | bytes 8388632
  4.2 5.7 %collective-permute-start = (bf16[48,2048]{1,0:T(8,128)(2,1)S(1)}, bf16[48,2048]{1,0:T(8,128)(2,1)S(1)}, u32[]{:S(2)}, u32[]{:S(2)}) collective-permute-start(bf16[48,2048]{1,0:T(8,128)(2,1)S(1)} %carry.1), channel_id=1, source_target_pairs={{0,64},{64,128},{128,192},{1,65},{65,129},{129,193},{2,66},{66,130... | collective-permute-start | bytes 589832 | tf_op jit(solution)/shard_map/ppermute | solution.py:272
  10.0 3.8 %own_filter.1 = (bf16[1024,2048]{1,0:T(8,128)(2,1)S(1)}, f32[48,2048]{1,0:T(8,128)S(1)}) custom-call(s32[16,131072]{1,0:T(8,128)S(1)} %copy-done, f32[4,2048]{1,0:T(4,128)S(1)} %copy-done.2), custom_call_target="tpu_custom_call" | custom-call | tf_op jit(solution)/shard_map/own_filter/pallas_call | solution.py:105
  17.7 6.9 %dft.3 = bf16[256,16,128]{2,1,0:T(8,128)(2,1)} custom-call(bf16[1024,2048]{1,0:T(8,128)(2,1)} %copy-done.1, f32[48,2048]{1,0:T(8,128)S(1)} %get-tuple-element.8.head_ref, bf16[48,2048]{1,0:T(8,128)(2,1)S(1)} %collective-permute-done.arrived_ref, bf16[2,2048,256]{2,1,0:T(8,128)(2,1)S(1)} %dft_table.3.t_ref), custom_call_target="tpu_custom_call" | custom-call | tf_op jit(solution)/shard_map/dft/pallas_call | solution.py:181
  24.6 10.0 %all-to-all-start.1 = ((bf16[256,16,128]{2,1,0:T(8,128)(2,1)}), bf16[256,16,128]{2,1,0:T(8,128)(2,1)S(1)}, u32[]{:S(2)}, u32[]{:S(2)}) async-start(bf16[256,16,128]{2,1,0:T(8,128)(2,1)} %dft.3), calls=%async_computation.1 | async-start | bytes 2097152 | tf_op jit(solution)/shard_map/all_to_all | solution.py:278
  35.5 6.9 %dft.2 = bf16[256,16,128]{2,1,0:T(8,128)(2,1)} custom-call(bf16[1024,2048]{1,0:T(8,128)(2,1)} %copy-done.1, f32[48,2048]{1,0:T(8,128)S(1)} %get-tuple-element.8.head_ref, bf16[48,2048]{1,0:T(8,128)(2,1)S(1)} %collective-permute-done.arrived_ref, bf16[2,2048,256]{2,1,0:T(8,128)(2,1)S(1)} %dft_table.2.t_ref), custom_call_target="tpu_custom_call" | custom-call | tf_op jit(solution)/shard_map/dft/pallas_call | solution.py:181
  42.4 10.1 %all-to-all-done.1 = bf16[256,16,128]{2,1,0:T(8,128)(2,1)S(1)} async-done(((bf16[256,16,128]{2,1,0:T(8,128)(2,1)}), bf16[256,16,128]{2,1,0:T(8,128)(2,1)S(1)}, u32[]{:S(2)}, u32[]{:S(2)}) %all-to-all-start.1) | async-done | bytes 1048608 | tf_op jit(solution)/shard_map/all_to_all | solution.py:278
  52.5 4.7 %all-to-all-start = ((bf16[256,16,128]{2,1,0:T(8,128)(2,1)}), bf16[256,16,128]{2,1,0:T(8,128)(2,1)S(1)}, u32[]{:S(2)}, u32[]{:S(2)}) async-start(bf16[256,16,128]{2,1,0:T(8,128)(2,1)} %dft.2), calls=%async_computation | async-start | bytes 2097152 | tf_op jit(solution)/shard_map/all_to_all | solution.py:278
  58.1 3.2 %collective-permute-start.5 = (bf16[1024,128]{1,0:T(8,128)(2,1)}, bf16[1024,128]{1,0:T(8,128)(2,1)S(1)}, u32[]{:S(2)}, u32[]{:S(2)}) collective-permute-start(bf16[1024,128]{1,0:T(8,128)(2,1)} %bitcast.9), channel_id=1, source_target_pairs={{0,64},{64,128},{128,192},{192,0},{1,65},{65,129},{129,193},{193,1... | collective-permute-start | bytes 786440 | tf_op jit(solution)/shard_map/ppermute | solution.py:37
  61.3 4.3 %collective-permute-start.14 = (bf16[1024,128]{1,0:T(8,128)(2,1)S(1)}, bf16[1024,128]{1,0:T(8,128)(2,1)S(1)}, u32[]{:S(2)}, u32[]{:S(2)}) collective-permute-start(bf16[1024,128]{1,0:T(8,128)(2,1)S(1)} %bitcast.31), channel_id=1, source_target_pairs={{0,64},{64,128},{128,192},{192,0},{1,65},{65,129},{129,193},{193,1... | collective-permute-start | bytes 786440 | tf_op jit(solution)/shard_map/ppermute | solution.py:37
  65.6 14.0 %all-to-all-done = bf16[256,16,128]{2,1,0:T(8,128)(2,1)S(1)} async-done(((bf16[256,16,128]{2,1,0:T(8,128)(2,1)}), bf16[256,16,128]{2,1,0:T(8,128)(2,1)S(1)}, u32[]{:S(2)}, u32[]{:S(2)}) %all-to-all-start) | async-done | bytes 1048608 | tf_op jit(solution)/shard_map/all_to_all | solution.py:278
  79.8 3.3 %collective-permute-start.1 = (bf16[1024,128]{1,0:T(8,128)(2,1)S(1)}, bf16[1024,128]{1,0:T(8,128)(2,1)S(1)}, u32[]{:S(2)}, u32[]{:S(2)}) collective-permute-start(bf16[1024,128]{1,0:T(8,128)(2,1)S(1)} %bitcast.47), channel_id=1, source_target_pairs={{0,64},{64,128},{128,192},{192,0},{1,65},{65,129},{129,193},{193,1... | collective-permute-start | bytes 786440 | tf_op jit(solution)/shard_map/ppermute | solution.py:37
  83.1 2.2 %collective-permute-start.7 = (bf16[1024,128]{1,0:T(8,128)(2,1)S(1)}, bf16[1024,128]{1,0:T(8,128)(2,1)S(1)}, u32[]{:S(2)}, u32[]{:S(2)}) collective-permute-start(bf16[1024,128]{1,0:T(8,128)(2,1)S(1)} %bitcast.45), channel_id=1, source_target_pairs={{0,192},{64,0},{128,64},{192,128},{1,193},{65,1},{129,65},{193,129... | collective-permute-start | bytes 786440 | tf_op jit(solution)/shard_map/ppermute | solution.py:41
  85.3 2.1 collective-permute-start.11
  87.4 3.9 %collective-permute-done.5.refs_1_ = bf16[1024,128]{1,0:T(8,128)(2,1)S(1)} collective-permute-done((bf16[1024,128]{1,0:T(8,128)(2,1)}, bf16[1024,128]{1,0:T(8,128)(2,1)S(1)}, u32[]{:S(2)}, u32[]{:S(2)}) %collective-permute-start.5) | collective-permute-done | bytes 262176 | tf_op jit(solution)/shard_map/ppermute | solution.py:37
  91.3 2.2 %collective-permute-start.3 = (bf16[1024,128]{1,0:T(8,128)(2,1)S(1)}, bf16[1024,128]{1,0:T(8,128)(2,1)S(1)}, u32[]{:S(2)}, u32[]{:S(2)}) collective-permute-start(bf16[1024,128]{1,0:T(8,128)(2,1)S(1)} %bitcast.46), channel_id=1, source_target_pairs={{0,192},{64,0},{128,64},{192,128},{1,193},{65,1},{129,65},{193,129... | collective-permute-start | bytes 786440 | tf_op jit(solution)/shard_map/ppermute | solution.py:41
  93.5 3.6 %collective-permute-done.14.refs_1_ = bf16[1024,128]{1,0:T(8,128)(2,1)S(1)} collective-permute-done((bf16[1024,128]{1,0:T(8,128)(2,1)S(1)}, bf16[1024,128]{1,0:T(8,128)(2,1)S(1)}, u32[]{:S(2)}, u32[]{:S(2)}) %collective-permute-start.14) | collective-permute-done | bytes 262176 | tf_op jit(solution)/shard_map/ppermute | solution.py:37
  97.1 5.7 %collective-permute-done.1.refs_1_ = bf16[1024,128]{1,0:T(8,128)(2,1)S(1)} collective-permute-done((bf16[1024,128]{1,0:T(8,128)(2,1)S(1)}, bf16[1024,128]{1,0:T(8,128)(2,1)S(1)}, u32[]{:S(2)}, u32[]{:S(2)}) %collective-permute-start.1) | collective-permute-done | bytes 262176 | tf_op jit(solution)/shard_map/ppermute | solution.py:37
  102.7 3.6 %collective-permute-start.6 = (bf16[1024,128]{1,0:T(8,128)(2,1)S(1)}, bf16[1024,128]{1,0:T(8,128)(2,1)S(1)}, u32[]{:S(2)}, u32[]{:S(2)}) collective-permute-start(bf16[1024,128]{1,0:T(8,128)(2,1)S(1)} %bitcast.34), channel_id=1, source_target_pairs={{0,192},{64,0},{128,64},{192,128},{1,193},{65,1},{129,65},{193,129... | collective-permute-start | bytes 786440 | tf_op jit(solution)/shard_map/ppermute | solution.py:41
  106.3 2.1 %collective-permute-done.11.refs_1_ = bf16[1024,128]{1,0:T(8,128)(2,1)S(1)} collective-permute-done((bf16[1024,128]{1,0:T(8,128)(2,1)S(1)}, bf16[1024,128]{1,0:T(8,128)(2,1)S(1)}, u32[]{:S(2)}, u32[]{:S(2)}) %collective-permute-start.11) | collective-permute-done | bytes 262176 | tf_op jit(solution)/shard_map/ppermute | solution.py:37
  108.4 2.1 %collective-permute-start.8 = (bf16[1024,128]{1,0:T(8,128)(2,1)S(1)}, bf16[1024,128]{1,0:T(8,128)(2,1)}, u32[]{:S(2)}, u32[]{:S(2)}) collective-permute-start(bf16[1024,128]{1,0:T(8,128)(2,1)S(1)} %collective-permute-done.7.refs_2_), channel_id=1, source_target_pairs={{0,192},{64,0},{128,64},{192,128},{1,193},{65,1},{129,65},{193,129... | collective-permute-start | bytes 786440 | tf_op jit(solution)/shard_map/ppermute | solution.py:41
  110.6 3.5 %collective-permute-done.15.refs_3_ = bf16[1024,128]{1,0:T(8,128)(2,1)S(1)} collective-permute-done((bf16[1024,128]{1,0:T(8,128)(2,1)S(1)}, bf16[1024,128]{1,0:T(8,128)(2,1)S(1)}, u32[]{:S(2)}, u32[]{:S(2)}) %collective-permute-start.15) | collective-permute-done | bytes 262176 | tf_op jit(solution)/shard_map/ppermute | solution.py:37
  114.1 2.1 %collective-permute-start.4 = (bf16[1024,128]{1,0:T(8,128)(2,1)S(1)}, bf16[1024,128]{1,0:T(8,128)(2,1)}, u32[]{:S(2)}, u32[]{:S(2)}) collective-permute-start(bf16[1024,128]{1,0:T(8,128)(2,1)S(1)} %collective-permute-done.3.refs_2_), channel_id=1, source_target_pairs={{0,192},{64,0},{128,64},{192,128},{1,193},{65,1},{129,65},{193,129... | collective-permute-start | bytes 786440 | tf_op jit(solution)/shard_map/ppermute | solution.py:41
  116.8 2.9 %collective-permute-done.12.refs_3_ = bf16[1024,128]{1,0:T(8,128)(2,1)S(1)} collective-permute-done((bf16[1024,128]{1,0:T(8,128)(2,1)S(1)}, bf16[1024,128]{1,0:T(8,128)(2,1)S(1)}, u32[]{:S(2)}, u32[]{:S(2)}) %collective-permute-start.12) | collective-permute-done | bytes 262176 | tf_op jit(solution)/shard_map/ppermute | solution.py:37
  119.7 19.1 %collective-permute-start.16 = (bf16[256,1024]{1,0:T(8,128)(2,1)S(1)}, bf16[256,1024]{1,0:T(8,128)(2,1)S(1)}, u32[]{:S(2)}, u32[]{:S(2)}) collective-permute-start(bf16[256,1024]{1,0:T(8,128)(2,1)S(1)} %correlate.13), channel_id=1, source_target_pairs={{0,64},{64,128},{128,192},{192,0},{1,65},{65,129},{129,193},{193,1... | collective-permute-start | bytes 1572872 | tf_op jit(solution)/shard_map/ppermute | solution.py:37
  139.5 4.6 %collective-permute-start.13 = (bf16[256,1024]{1,0:T(8,128)(2,1)S(1)}, bf16[256,1024]{1,0:T(8,128)(2,1)S(1)}, u32[]{:S(2)}, u32[]{:S(2)}) collective-permute-start(bf16[256,1024]{1,0:T(8,128)(2,1)S(1)} %correlate.12), channel_id=1, source_target_pairs={{0,64},{64,128},{128,192},{192,0},{1,65},{65,129},{129,193},{193,1... | collective-permute-start | bytes 1572872 | tf_op jit(solution)/shard_map/ppermute | solution.py:37
  148.2 2.7 %collective-permute-start.9 = (bf16[256,1024]{1,0:T(8,128)(2,1)S(1)}, bf16[256,1024]{1,0:T(8,128)(2,1)S(1)}, u32[]{:S(2)}, u32[]{:S(2)}) collective-permute-start(bf16[256,1024]{1,0:T(8,128)(2,1)S(1)} %correlate.10), channel_id=1, source_target_pairs={{0,192},{64,0},{128,64},{192,128},{1,193},{65,1},{129,65},{193,129... | collective-permute-start | bytes 1572872 | tf_op jit(solution)/shard_map/ppermute | solution.py:41
  155.4 4.5 %collective-permute-done.16.refs_5_ = bf16[256,1024]{1,0:T(8,128)(2,1)S(1)} collective-permute-done((bf16[256,1024]{1,0:T(8,128)(2,1)S(1)}, bf16[256,1024]{1,0:T(8,128)(2,1)S(1)}, u32[]{:S(2)}, u32[]{:S(2)}) %collective-permute-start.16) | collective-permute-done | bytes 524320 | tf_op jit(solution)/shard_map/ppermute | solution.py:37
  159.9 14.4 %collective-permute-done.13.refs_4_ = bf16[256,1024]{1,0:T(8,128)(2,1)S(1)} collective-permute-done((bf16[256,1024]{1,0:T(8,128)(2,1)S(1)}, bf16[256,1024]{1,0:T(8,128)(2,1)S(1)}, u32[]{:S(2)}, u32[]{:S(2)}) %collective-permute-start.13) | collective-permute-done | bytes 524320 | tf_op jit(solution)/shard_map/ppermute | solution.py:37
  174.4 18.7 %collective-permute-done.10.refs_3_ = bf16[256,1024]{1,0:T(8,128)(2,1)S(1)} collective-permute-done((bf16[256,1024]{1,0:T(8,128)(2,1)S(1)}, bf16[256,1024]{1,0:T(8,128)(2,1)S(1)}, u32[]{:S(2)}, u32[]{:S(2)}) %collective-permute-start.10) | collective-permute-done | bytes 524320 | tf_op jit(solution)/shard_map/ppermute | solution.py:41
  193.1 11.2 %collective-permute-done.9.refs_2_ = bf16[256,1024]{1,0:T(8,128)(2,1)S(1)} collective-permute-done((bf16[256,1024]{1,0:T(8,128)(2,1)S(1)}, bf16[256,1024]{1,0:T(8,128)(2,1)S(1)}, u32[]{:S(2)}, u32[]{:S(2)}) %collective-permute-start.9) | collective-permute-done | bytes 524320 | tf_op jit(solution)/shard_map/ppermute | solution.py:41
  204.3 3.9 %gather_planes.1 = bf16[256,8,1024]{2,1,0:T(8,128)(2,1)} custom-call(s32[1]{0:T(128)} %bitcast.row_ref.position_ref, bf16[256,1024]{1,0:T(8,128)(2,1)S(1)} %correlate.8.refs_0_, bf16[256,1024]{1,0:T(8,128)(2,1)S(1)} %correlate.9.refs_1_, bf16[256,1024]{1,0:T(8,128)(2,1)S(1)} %collective-permute-done.9.refs_2_, ...), custom_call_target="tpu_custom_call" | custom-call | tf_op jit(solution)/shard_map/gather_planes/pallas_call | solution.py:256
  (34 shorter events, 16.0 us)
Async XLA Ops:
  0.0 3.4 %copy-start = (s32[16,131072]{1,0:T(8,128)S(1)}, s32[16,131072]{1,0:T(8,128)}, u32[]{:S(2)}) copy-start(s32[16,131072]{1,0:T(8,128)} %v_ref.3) | copy-start | bytes 25165828
  3.4 0.8 copy-start.2
  4.2 13.5 %collective-permute-start = (bf16[48,2048]{1,0:T(8,128)(2,1)S(1)}, bf16[48,2048]{1,0:T(8,128)(2,1)S(1)}, u32[]{:S(2)}, u32[]{:S(2)}) collective-permute-start(bf16[48,2048]{1,0:T(8,128)(2,1)S(1)} %carry.1), channel_id=1, source_target_pairs={{0,64},{64,128},{128,192},{1,65},{65,129},{129,193},{2,66},{66,130... | collective-permute-start | bytes 589832 | tf_op jit(solution)/shard_map/ppermute | solution.py:272
  13.7 2.0 copy-start.1
  24.6 27.9 %all-to-all-start.1 = ((bf16[256,16,128]{2,1,0:T(8,128)(2,1)}), bf16[256,16,128]{2,1,0:T(8,128)(2,1)S(1)}, u32[]{:S(2)}, u32[]{:S(2)}) async-start(bf16[256,16,128]{2,1,0:T(8,128)(2,1)} %dft.3), calls=%async_computation.1 | async-start | bytes 2097152 | tf_op jit(solution)/shard_map/all_to_all | solution.py:278
  52.5 27.1 %all-to-all-start = ((bf16[256,16,128]{2,1,0:T(8,128)(2,1)}), bf16[256,16,128]{2,1,0:T(8,128)(2,1)S(1)}, u32[]{:S(2)}, u32[]{:S(2)}) async-start(bf16[256,16,128]{2,1,0:T(8,128)(2,1)} %dft.2), calls=%async_computation | async-start | bytes 2097152 | tf_op jit(solution)/shard_map/all_to_all | solution.py:278
  58.1 33.2 %collective-permute-start.5 = (bf16[1024,128]{1,0:T(8,128)(2,1)}, bf16[1024,128]{1,0:T(8,128)(2,1)S(1)}, u32[]{:S(2)}, u32[]{:S(2)}) collective-permute-start(bf16[1024,128]{1,0:T(8,128)(2,1)} %bitcast.9), channel_id=1, source_target_pairs={{0,64},{64,128},{128,192},{192,0},{1,65},{65,129},{129,193},{193,1... | collective-permute-start | bytes 786440 | tf_op jit(solution)/shard_map/ppermute | solution.py:37
  61.3 35.7 %collective-permute-start.14 = (bf16[1024,128]{1,0:T(8,128)(2,1)S(1)}, bf16[1024,128]{1,0:T(8,128)(2,1)S(1)}, u32[]{:S(2)}, u32[]{:S(2)}) collective-permute-start(bf16[1024,128]{1,0:T(8,128)(2,1)S(1)} %bitcast.31), channel_id=1, source_target_pairs={{0,64},{64,128},{128,192},{192,0},{1,65},{65,129},{129,193},{193,1... | collective-permute-start | bytes 786440 | tf_op jit(solution)/shard_map/ppermute | solution.py:37
  79.8 22.9 %collective-permute-start.1 = (bf16[1024,128]{1,0:T(8,128)(2,1)S(1)}, bf16[1024,128]{1,0:T(8,128)(2,1)S(1)}, u32[]{:S(2)}, u32[]{:S(2)}) collective-permute-start(bf16[1024,128]{1,0:T(8,128)(2,1)S(1)} %bitcast.47), channel_id=1, source_target_pairs={{0,64},{64,128},{128,192},{192,0},{1,65},{65,129},{129,193},{193,1... | collective-permute-start | bytes 786440 | tf_op jit(solution)/shard_map/ppermute | solution.py:37
  83.1 19.7 %collective-permute-start.7 = (bf16[1024,128]{1,0:T(8,128)(2,1)S(1)}, bf16[1024,128]{1,0:T(8,128)(2,1)S(1)}, u32[]{:S(2)}, u32[]{:S(2)}) collective-permute-start(bf16[1024,128]{1,0:T(8,128)(2,1)S(1)} %bitcast.45), channel_id=1, source_target_pairs={{0,192},{64,0},{128,64},{192,128},{1,193},{65,1},{129,65},{193,129... | collective-permute-start | bytes 786440 | tf_op jit(solution)/shard_map/ppermute | solution.py:41
  85.3 23.1 %collective-permute-start.11 = (bf16[1024,128]{1,0:T(8,128)(2,1)S(1)}, bf16[1024,128]{1,0:T(8,128)(2,1)S(1)}, u32[]{:S(2)}, u32[]{:S(2)}) collective-permute-start(bf16[1024,128]{1,0:T(8,128)(2,1)S(1)} %bitcast.37), channel_id=1, source_target_pairs={{0,64},{64,128},{128,192},{192,0},{1,65},{65,129},{129,193},{193,1... | collective-permute-start | bytes 786440 | tf_op jit(solution)/shard_map/ppermute | solution.py:37
  91.3 19.2 %collective-permute-start.3 = (bf16[1024,128]{1,0:T(8,128)(2,1)S(1)}, bf16[1024,128]{1,0:T(8,128)(2,1)S(1)}, u32[]{:S(2)}, u32[]{:S(2)}) collective-permute-start(bf16[1024,128]{1,0:T(8,128)(2,1)S(1)} %bitcast.46), channel_id=1, source_target_pairs={{0,192},{64,0},{128,64},{192,128},{1,193},{65,1},{129,65},{193,129... | collective-permute-start | bytes 786440 | tf_op jit(solution)/shard_map/ppermute | solution.py:41
  97.1 17.0 %collective-permute-start.15 = (bf16[1024,128]{1,0:T(8,128)(2,1)S(1)}, bf16[1024,128]{1,0:T(8,128)(2,1)S(1)}, u32[]{:S(2)}, u32[]{:S(2)}) collective-permute-start(bf16[1024,128]{1,0:T(8,128)(2,1)S(1)} %collective-permute-done.5.refs_1_), channel_id=1, source_target_pairs={{0,64},{64,128},{128,192},{192,0},{1,65},{65,129},{129,193},{193,1... | collective-permute-start | bytes 786440 | tf_op jit(solution)/shard_map/ppermute | solution.py:37
  102.7 17.0 %collective-permute-start.12 = (bf16[1024,128]{1,0:T(8,128)(2,1)S(1)}, bf16[1024,128]{1,0:T(8,128)(2,1)S(1)}, u32[]{:S(2)}, u32[]{:S(2)}) collective-permute-start(bf16[1024,128]{1,0:T(8,128)(2,1)S(1)} %collective-permute-done.1.refs_1_), channel_id=1, source_target_pairs={{0,64},{64,128},{128,192},{192,0},{1,65},{65,129},{129,193},{193,1... | collective-permute-start | bytes 786440 | tf_op jit(solution)/shard_map/ppermute | solution.py:37
  102.7 36.8 %collective-permute-start.6 = (bf16[1024,128]{1,0:T(8,128)(2,1)S(1)}, bf16[1024,128]{1,0:T(8,128)(2,1)S(1)}, u32[]{:S(2)}, u32[]{:S(2)}) collective-permute-start(bf16[1024,128]{1,0:T(8,128)(2,1)S(1)} %bitcast.34), channel_id=1, source_target_pairs={{0,192},{64,0},{128,64},{192,128},{1,193},{65,1},{129,65},{193,129... | collective-permute-start | bytes 786440 | tf_op jit(solution)/shard_map/ppermute | solution.py:41
  108.4 35.7 %collective-permute-start.8 = (bf16[1024,128]{1,0:T(8,128)(2,1)S(1)}, bf16[1024,128]{1,0:T(8,128)(2,1)}, u32[]{:S(2)}, u32[]{:S(2)}) collective-permute-start(bf16[1024,128]{1,0:T(8,128)(2,1)S(1)} %collective-permute-done.7.refs_2_), channel_id=1, source_target_pairs={{0,192},{64,0},{128,64},{192,128},{1,193},{65,1},{129,65},{193,129... | collective-permute-start | bytes 786440 | tf_op jit(solution)/shard_map/ppermute | solution.py:41
  110.5 36.0 %collective-permute-start.2 = (bf16[1024,128]{1,0:T(8,128)(2,1)S(1)}, bf16[1024,128]{1,0:T(8,128)(2,1)}, u32[]{:S(2)}, u32[]{:S(2)}) collective-permute-start(bf16[1024,128]{1,0:T(8,128)(2,1)S(1)} %bitcast.40), channel_id=1, source_target_pairs={{0,192},{64,0},{128,64},{192,128},{1,193},{65,1},{129,65},{193,129... | collective-permute-start | bytes 786440 | tf_op jit(solution)/shard_map/ppermute | solution.py:41
  114.1 32.4 %collective-permute-start.4 = (bf16[1024,128]{1,0:T(8,128)(2,1)S(1)}, bf16[1024,128]{1,0:T(8,128)(2,1)}, u32[]{:S(2)}, u32[]{:S(2)}) collective-permute-start(bf16[1024,128]{1,0:T(8,128)(2,1)S(1)} %collective-permute-done.3.refs_2_), channel_id=1, source_target_pairs={{0,192},{64,0},{128,64},{192,128},{1,193},{65,1},{129,65},{193,129... | collective-permute-start | bytes 786440 | tf_op jit(solution)/shard_map/ppermute | solution.py:41
  119.7 40.2 %collective-permute-start.16 = (bf16[256,1024]{1,0:T(8,128)(2,1)S(1)}, bf16[256,1024]{1,0:T(8,128)(2,1)S(1)}, u32[]{:S(2)}, u32[]{:S(2)}) collective-permute-start(bf16[256,1024]{1,0:T(8,128)(2,1)S(1)} %correlate.13), channel_id=1, source_target_pairs={{0,64},{64,128},{128,192},{192,0},{1,65},{65,129},{129,193},{193,1... | collective-permute-start | bytes 1572872 | tf_op jit(solution)/shard_map/ppermute | solution.py:37
  139.5 34.9 %collective-permute-start.13 = (bf16[256,1024]{1,0:T(8,128)(2,1)S(1)}, bf16[256,1024]{1,0:T(8,128)(2,1)S(1)}, u32[]{:S(2)}, u32[]{:S(2)}) collective-permute-start(bf16[256,1024]{1,0:T(8,128)(2,1)S(1)} %correlate.12), channel_id=1, source_target_pairs={{0,64},{64,128},{128,192},{192,0},{1,65},{65,129},{129,193},{193,1... | collective-permute-start | bytes 1572872 | tf_op jit(solution)/shard_map/ppermute | solution.py:37
  145.7 47.4 %collective-permute-start.10 = (bf16[256,1024]{1,0:T(8,128)(2,1)S(1)}, bf16[256,1024]{1,0:T(8,128)(2,1)S(1)}, u32[]{:S(2)}, u32[]{:S(2)}) collective-permute-start(bf16[256,1024]{1,0:T(8,128)(2,1)S(1)} %correlate.11), channel_id=1, source_target_pairs={{0,192},{64,0},{128,64},{192,128},{1,193},{65,1},{129,65},{193,129... | collective-permute-start | bytes 1572872 | tf_op jit(solution)/shard_map/ppermute | solution.py:41
  148.2 56.1 %collective-permute-start.9 = (bf16[256,1024]{1,0:T(8,128)(2,1)S(1)}, bf16[256,1024]{1,0:T(8,128)(2,1)S(1)}, u32[]{:S(2)}, u32[]{:S(2)}) collective-permute-start(bf16[256,1024]{1,0:T(8,128)(2,1)S(1)} %correlate.10), channel_id=1, source_target_pairs={{0,192},{64,0},{128,64},{192,128},{1,193},{65,1},{129,65},{193,129... | collective-permute-start | bytes 1572872 | tf_op jit(solution)/shard_map/ppermute | solution.py:41

commit v2 on v1

v2 whole, which is shorter than its diff:
```python
import functools
import math

import jax
import jax.numpy as jnp
from jax import lax
from jax.experimental import pallas as pl
from jax.experimental.pallas import tpu as pltpu
from jax.sharding import PartitionSpec as P

FRAME = 2048
TAPS = 4
INP = 16
SPEC = 64
INPUTS = 1024
N_TM = 4
N_FEED = 64
N_Z = 8
N_D = 32
CH_DEV = 8
FRAME_BLOCK = 8
DEPTH = 4
LANES = 256
COARSE = 32
FINE = FRAME // COARSE
ROWS = INPUTS // N_TM
PIECE = 2 * SPEC
BLOCK = (N_TM, N_D // N_TM, INP, PIECE)
EARLY = (2, 0, 5)
LATE = (1, 3, 4, 6, 7)
FAR = 2 * len(LATE)
MIB = 1 << 20


def in_hbm(x):
    return pltpu.with_memory_space_constraint(x, pltpu.HBM)


def params(mib):
    return pltpu.CompilerParams(vmem_limit_bytes=mib * MIB)


def place_of(tm, z_lo, d):
    return tm * N_FEED + (d // 8 * 2 + z_lo) * 8 + d % 8


def along_z(x, by):
    pairs = []
    for z in range(N_Z):
        to = (z + by) % N_Z
        for d in range(N_D):
            pairs.append((place_of(z // 2, z % 2, d), place_of(to // 2, to % 2, d)))
    return lax.ppermute(x, ("tm", "feed"), pairs)


def both_ways(left, right, by):
    return lax.optimization_barrier((along_z(left, -by), along_z(right, by)))


def turn(x):
    groups = [[place_of(0, z_lo, d) for d in range(N_D)] for z_lo in range(2)]
    return lax.all_to_all(
        x, "feed", split_axis=0, concat_axis=0, tiled=True, axis_index_groups=groups
    )


def carry_kernel(v_ref, w_ref, out_ref, held, sem):
    at = v_ref.shape[1] - (TAPS - 1) * FRAME
    copy = pltpu.make_async_copy(v_ref.at[:, pl.ds(at, (TAPS - 1) * FRAME)], held, sem)
    copy.start()
    copy.wait()
    for head in range(TAPS - 1):
        for start in range(0, FRAME, LANES):
            total = jnp.zeros((INP, LANES), jnp.float32)
            for tap in range(head + 1, TAPS):
                at = (TAPS - 1 + head - tap) * FRAME + start
                total = total + w_ref[tap : tap + 1, start : start + LANES] * held[
                    :, at : at + LANES
                ].astype(jnp.float32)
            out_ref[head * INP : (head + 1) * INP, start : start + LANES] = total.astype(jnp.bfloat16)


def carry(voltages, window):
    return pl.pallas_call(
        carry_kernel,
        in_specs=[
            pl.BlockSpec(memory_space=pltpu.HBM),
            pl.BlockSpec(memory_space=pltpu.VMEM),
        ],
        out_specs=pl.BlockSpec(memory_space=pltpu.VMEM),
        out_shape=jax.ShapeDtypeStruct(((TAPS - 1) * INP, FRAME), jnp.bfloat16),
        scratch_shapes=[
            pltpu.VMEM((INP, (TAPS - 1) * FRAME), jnp.int32),
            pltpu.SemaphoreType.DMA,
        ],
        compiler_params=params(8),
        name="carry",
    )(in_hbm(voltages), window)


def filter_kernel(v_ref, w_ref, out_ref, head_ref, held, past, sems):
    width = FRAME_BLOCK * FRAME
    steps = SPEC // FRAME_BLOCK

    def fetch(step):
        return pltpu.make_async_copy(
            v_ref.at[:, pl.ds(step * width, width)], held.at[step % DEPTH], sems.at[step % DEPTH]
        )

    for step in range(DEPTH - 1):
        fetch(step).start()
    past[...] = jnp.zeros_like(past)
    for step in range(steps):
        if step + DEPTH - 1 < steps:
            fetch(step + DEPTH - 1).start()
        fetch(step).wait()
        for start in range(0, FRAME, LANES):
            cols = slice(start, start + LANES)
            taps = [
                jnp.broadcast_to(w_ref[p : p + 1, cols], (INP, LANES)) for p in range(TAPS)
            ]
            seen = [past[p, :, cols] for p in range(TAPS - 1)]
            for k in range(FRAME_BLOCK):
                now = held[step % DEPTH, :, k * FRAME + start : k * FRAME + start + LANES].astype(
                    jnp.float32
                )
                total = taps[0] * now
                for p in range(1, TAPS):
                    total = total + taps[p] * seen[p - 1]
                row = (step * FRAME_BLOCK + k) * INP
                out_ref[row : row + INP, cols] = total.astype(jnp.bfloat16)
                if row < head_ref.shape[0]:
                    head_ref[row : row + INP, cols] = total
                seen = [now] + seen[:-1]
            for p in range(TAPS - 1):
                past[p, :, cols] = seen[p]


def filter_own(voltages, window):
    head_rows = (TAPS - 1) * INP
    vmem = pl.BlockSpec(memory_space=pltpu.VMEM)
    return pl.pallas_call(
        filter_kernel,
        in_specs=[pl.BlockSpec(memory_space=pltpu.HBM), vmem],
        out_specs=[vmem, vmem],
        out_shape=[
            jax.ShapeDtypeStruct((SPEC * INP, FRAME), jnp.bfloat16),
            jax.ShapeDtypeStruct((head_rows, FRAME), jnp.float32),
        ],
        scratch_shapes=[
            pltpu.VMEM((DEPTH, INP, FRAME_BLOCK * FRAME), jnp.int32),
            pltpu.VMEM((TAPS - 1, INP, FRAME), jnp.float32),
            pltpu.SemaphoreType.DMA((DEPTH,)),
        ],
        compiler_params=params(14),
        name="own_filter",
    )(in_hbm(voltages), window)


def table_kernel(coarse_cos, coarse_sin, fine_cos, fine_sin, out_ref):
    half = out_ref.shape[2] // 2
    for part in range(out_ref.shape[0]):
        cols = slice(part * half, (part + 1) * half)
        for a in range(COARSE):
            ac, as_ = coarse_cos[a : a + 1, cols], coarse_sin[a : a + 1, cols]
            bc, bs = fine_cos[:, cols], fine_sin[:, cols]
            rows = slice(a * FINE, (a + 1) * FINE)
            out_ref[part, rows, :half] = (ac * bc - as_ * bs).astype(jnp.bfloat16)
            out_ref[part, rows, half:] = (-(as_ * bc) - ac * bs).astype(jnp.bfloat16)


def table(first_channel, z):
    column = lax.iota(jnp.int32, N_D * FAR)
    runs = jnp.repeat(jnp.arange(2 * len(EARLY), dtype=jnp.int32), N_D)
    early, late = jnp.array(EARLY, jnp.int32), jnp.array(LATE, jnp.int32)
    d = jnp.concatenate([column // FAR, lax.iota(jnp.int32, N_D * 2 * len(EARLY)) % N_D])
    delta = jnp.concatenate([late[column % len(LATE)], early[runs // 2]])
    which = jnp.concatenate([column % FAR // len(LATE), runs % 2])
    group = (z + N_Z - delta) % N_Z
    feed = (d // 8 * 2 + group % 2) * 8 + d % 8
    channel = first_channel[0] + feed * CH_DEV + group // 2 * 2 + which

    def waves(samples):
        phase = samples[:, None] * channel[None, :] % FRAME
        angle = phase.astype(jnp.float32) * jnp.float32(2.0 * math.pi / FRAME)
        return jnp.cos(angle), jnp.sin(angle)

    scale = jnp.float32(1.0 / math.sqrt(FRAME))
    coarse = waves(FINE * lax.iota(jnp.int32, COARSE))
    fine = waves(lax.iota(jnp.int32, FINE))
    return pl.pallas_call(
        table_kernel,
        out_shape=jax.ShapeDtypeStruct((4, FRAME, N_D * N_Z), jnp.bfloat16),
        compiler_params=params(16),
        name="dft_table",
    )(coarse[0], coarse[1], fine[0] * scale, fine[1] * scale)


def dft_kernel(dests, f_ref, head_ref, arrived_ref, t_ref, *refs):
    outs, (fixed, wide, turned) = refs[:-3], refs[-3:]
    head_rows = head_ref.shape[0]
    fixed[...] = (head_ref[...] + arrived_ref[...].astype(jnp.float32)).astype(jnp.bfloat16)
    for part in range(t_ref.shape[0]):
        first = jnp.dot(fixed[...], t_ref[part], preferred_element_type=jnp.float32)
        rest = jnp.dot(f_ref[head_rows:, :], t_ref[part], preferred_element_type=jnp.float32)
        for r in range(2):
            wide[part, r, :head_rows, :] = first[:, r * 128 : (r + 1) * 128]
            wide[part, r, head_rows:, :] = rest[:, r * 128 : (r + 1) * 128]
    for part in range(t_ref.shape[0]):
        for i in range(INP):
            rows = pl.ds(i, SPEC, stride=INP)
            both = jnp.concatenate([wide[part, 0, rows, :], wide[part, 1, rows, :]], 0)
            turned[part, pl.ds(i, 128, stride=INP), :] = both.T
        for run in range(4):
            rows = slice(run * N_D * INP, (run + 1) * N_D * INP)
            block = turned[part, rows, :].astype(jnp.bfloat16).reshape(BLOCK)
            for n, (which, at) in enumerate(dests[part * 4 + run]):
                if outs[which].shape[0] == at + 2:
                    outs[which][at:] = block[2 * n : 2 * n + 2]
                else:
                    outs[which][at : at + 4] = block


def dft(filtered, head, arrived, dft_table, counts, dests):
    parts = dft_table.shape[0]
    vmem = pl.BlockSpec(memory_space=pltpu.VMEM)
    return pl.pallas_call(
        functools.partial(dft_kernel, dests),
        in_specs=[vmem] * 4,
        out_specs=[vmem] * len(counts),
        out_shape=[jax.ShapeDtypeStruct((count, *BLOCK[1:]), jnp.bfloat16) for count in counts],
        scratch_shapes=[
            pltpu.VMEM(head.shape, jnp.bfloat16),
            pltpu.VMEM((parts, 2, SPEC * INP, 128), jnp.float32),
            pltpu.VMEM((parts, 128 * INP, PIECE), jnp.float32),
        ],
        compiler_params=params(24),
        name="dft",
    )(filtered, head, arrived, dft_table)


def move_kernel(moves, n_in, *refs):
    ins, outs, sems = refs[:n_in], refs[n_in:-1], refs[-1]
    copies = [
        pltpu.make_async_copy(ins[i].at[src], outs[o].at[dst], sems.at[n])
        for n, (i, src, o, dst) in enumerate(moves)
    ]
    for copy in copies:
        copy.start()
    for copy in copies:
        copy.wait()


def move(arrays, shapes, moves):
    return pl.pallas_call(
        functools.partial(move_kernel, moves, len(arrays)),
        in_specs=[pl.BlockSpec(memory_space=pltpu.HBM)] * len(arrays),
        out_specs=[pl.BlockSpec(memory_space=pltpu.VMEM)] * len(shapes),
        out_shape=[jax.ShapeDtypeStruct(shape, jnp.bfloat16) for shape in shapes],
        scratch_shapes=[pltpu.SemaphoreType.DMA((len(moves),))],
        compiler_params=params(4),
        name="move",
    )(*[in_hbm(x) for x in arrays])


def correlate_kernel(layout, where_ref, *refs):
    arrays, (out_ref, x, sems) = refs[:-3], refs[-3:]
    z_lo = where_ref[1]
    copies = []
    for delta, parts in enumerate(layout):
        step, odd = divmod(delta, 2)
        half = lax.rem(z_lo + odd, 2)
        slot = lax.rem(step + z_lo * odd, N_TM)
        for which, at, to, count in parts:
            if len(arrays[which].shape) == 5:
                source = arrays[which].at[:, :, at]
            else:
                source = arrays[which].at[pl.ds(at, count)]
            goal = x.at[slot, pl.ds(to, count), half]
            copies.append(pltpu.make_async_copy(source, goal, sems.at[len(copies)]))
    for copy in copies:
        copy.start()
    for copy in copies:
        copy.wait()
    scale = jnp.float32(1.0 / (SPEC * N_TM))
    contract = (((1,), (1,)), ((), ()))
    lower = lax.broadcasted_iota(jnp.int32, (ROWS, ROWS), 0) >= lax.broadcasted_iota(
        jnp.int32, (ROWS, ROWS), 1
    )
    block = where_ref[0]
    mine = [x[slot, block].reshape(ROWS, PIECE) for slot in range(N_TM)]
    plain = jnp.concatenate(mine, 1)
    crossed = jnp.concatenate([x for m in mine for x in (m[:, SPEC:], -m[:, :SPEC])], 1)
    for other in range(N_TM):
        cols = slice(other * ROWS, (other + 1) * ROWS)
        left = jnp.where(other <= block, plain, crossed)
        right = jnp.concatenate(
            [x[slot, other].reshape(ROWS, PIECE) for slot in range(N_TM)], 1
        )
        part = lax.dot_general(left, right, contract, preferred_element_type=jnp.float32)
        out_ref[:, cols] = (part * scale).astype(jnp.bfloat16)
    part = lax.dot_general(crossed, plain, contract, preferred_element_type=jnp.float32)
    at = pl.ds(pl.multiple_of(block * ROWS, ROWS), ROWS)
    both = jnp.where(lower, out_ref[:, at].astype(jnp.float32), part * scale)
    out_ref[:, at] = both.astype(jnp.bfloat16)


def correlate(block, z_lo, layout, arrays):
    used = sorted({part[0] for parts in layout for part in parts})
    layout = [[(used.index(part[0]), *part[1:]) for part in parts] for parts in layout]
    arrays = [in_hbm(arrays[which]) for which in used]
    vmem = pl.BlockSpec(memory_space=pltpu.VMEM)
    where = jnp.stack([block, z_lo]).astype(jnp.int32)
    return pl.pallas_call(
        functools.partial(correlate_kernel, layout),
        in_specs=[pl.BlockSpec(memory_space=pltpu.SMEM)]
        + [pl.BlockSpec(memory_space=pltpu.HBM)] * len(arrays),
        out_specs=vmem,
        out_shape=jax.ShapeDtypeStruct((ROWS, INPUTS), jnp.bfloat16),
        scratch_shapes=[
            pltpu.VMEM((N_TM, N_TM, 2, *BLOCK[1:]), jnp.bfloat16),
            pltpu.SemaphoreType.DMA((N_Z + 1,)),
        ],
        compiler_params=params(12),
        name="correlate",
    )(where, *arrays)


def gather_kernel(position_ref, *refs):
    planes, out_ref, wide = refs[:CH_DEV], refs[CH_DEV], refs[CH_DEV + 1]
    rows = planes[0].shape[0]
    for place in range(CH_DEV):
        channel = 2 * lax.rem(position_ref[0] + place // 2, N_TM) + place % 2
        for part in range(INPUTS // 128):
            cols = slice(part * 128, (part + 1) * 128)
            wide[part, pl.ds(channel, rows, stride=CH_DEV), :] = planes[place][:, cols].astype(
                jnp.float32
            )
    for part in range(INPUTS // 128):
        cols = slice(part * 128, (part + 1) * 128)
        out_ref[:, :, cols] = wide[part].astype(jnp.bfloat16).reshape(rows, CH_DEV, 128)


def gather_planes(position, planes):
    block = 64
    return pl.pallas_call(
        gather_kernel,
        grid=(ROWS // block,),
        in_specs=[pl.BlockSpec(memory_space=pltpu.SMEM)]
        + [pl.BlockSpec((block, INPUTS), lambda g: (g, 0))] * CH_DEV,
        out_specs=pl.BlockSpec((block, CH_DEV, INPUTS), lambda g: (g, 0, 0)),
        out_shape=jax.ShapeDtypeStruct((ROWS, CH_DEV, INPUTS), jnp.bfloat16),
        scratch_shapes=[pltpu.VMEM((INPUTS // 128, block * CH_DEV, 128), jnp.float32)],
        compiler_params=params(32),
        name="gather_planes",
    )(position.astype(jnp.int32).reshape(1), *planes)


def places(which):
    at, early = 4 * which, 6 * which
    here = [(0, early), (1, 8 + at), (0, early + 1), (5, 0), (5, 4), (0, early + 2), (4, at), (2, at)]
    there = [(0, early + 3), (2, 8 + at), (0, early + 4), (1, at), (3, at), (0, early + 5), (6, 4), (6, 0)]
    return [[[(*place, 0, 4)] for place in side] for side in (here, there)]


def per_device(voltages, window, first_channel):
    position = lax.axis_index("tm")
    z_lo = lax.axis_index("feed") // 8 % 2
    z = 2 * position + z_lo
    after, before = (position + 1) % N_TM, (position + N_TM - 1) % N_TM
    carried, first_channel = lax.optimization_barrier((carry(voltages, window), first_channel))
    arrived = lax.ppermute(carried, "tm", [(i, i + 1) for i in range(N_TM - 1)])
    dft_table, window = lax.optimization_barrier((table(first_channel, z), window))
    filtered, head = filter_own(voltages, window)
    planes = [None] * CH_DEV

    dests = [[(0, 4 * i)] for i in range(FAR)]
    dests += [[(1 + i // 2, i % 2 * 4)] for i in range(2 * N_Z - FAR)]
    spectra, twos, zeros, fives = dft(filtered, head, arrived, dft_table, (4 * FAR, 8, 8, 8), dests)
    turned = turn(spectra.reshape(-1, INP, PIECE)).reshape(*BLOCK[:2], FAR, *BLOCK[2:])
    left_5, right_5 = both_ways(fives, fives, 3)
    left_2, right_0 = both_ways(twos, zeros, 2)
    early = [zeros, left_2, right_5, right_0, twos, left_5]
    everything = slice(None)
    (packed,) = move(
        early,
        [(*BLOCK[:2], 2 * len(early), *BLOCK[2:])],
        [
            (n, (pl.ds(4 * which, 4),), 0, (everything, everything, len(early) * which + n))
            for which in range(2)
            for n in range(len(early))
        ],
    )
    packed = turn(packed.reshape(-1, INP, PIECE)).reshape(packed.shape)
    sent = ((3, 1), (7, 1), (4,), (6,))
    sent_31, sent_71, sent_4, sent_6 = move(
        [turned],
        [(8 * len(deltas), *BLOCK[1:]) for deltas in sent],
        [
            (0, (everything, everything, len(LATE) * which + LATE.index(delta)), i, (pl.ds(8 * n + 4 * which, 4),))
            for i, deltas in enumerate(sent)
            for n, delta in enumerate(deltas)
            for which in range(2)
        ],
    )
    left_31, right_71 = both_ways(sent_31, sent_71, 1)
    left_4, right_6 = both_ways(sent_4, sent_6, 2)

    for which in range(2):
        here, there = places(which)
        part = slice(4 * which, 4 * which + 4)
        far = both_ways(
            jnp.concatenate([left_31[part], left_4[part]]),
            jnp.concatenate([right_71[part], right_6[part]]),
            2,
        )
        arrays = [packed, left_31, right_71, left_4, right_6, *far]
        planes[2 + which], planes[4 + which] = both_ways(
            correlate(before, z_lo, here, arrays), correlate(after, z_lo, there, arrays), 2
        )
        planes[0 + which] = correlate(position, z_lo, here, arrays)
        planes[6 + which] = correlate(position, z_lo, there, arrays)
    return gather_planes(position, planes)


def solution(mesh):
    in_specs = (P("feed", "tm"), P(), P())
    out_specs = P("tm", "feed", None)
    return jax.shard_map(
        per_device, mesh=mesh, in_specs=in_specs, out_specs=out_specs, check_vma=False
    )
```

time: 209 us -> 178 us (0.85)
  waiting for transfers between devices: 94.7 us -> 67.3 us
  starting transfers between devices: 72.7 us -> 60.2 us
  Pallas kernels: 31.9 us -> 42.9 us
  local copies, waits for them, and re-layouts: 7.21 us -> 4.03 us
    all_to_all x2, waiting for transfers between devices: 24.1 us -> 7.74 us  [turn(): lax.all_to_all(x, 'feed', split_axis=0, concat_axis=0, tiled=True, axis_i...]
    ppermute x17, starting transfers between devices: 58.1 us -> 42.4 us  [the longest x16 36.7 us: along_z(): return lax.ppermute(x, ('tm', 'feed'), pairs)]
    ppermute x17, waiting for transfers between devices: 70.6 us -> 59.6 us  [the longest x16 59.6 us: along_z(): return lax.ppermute(x, ('tm', 'feed'), pairs)]
    pallas_call x14, Pallas kernels: 28 us -> 38.9 us  [the longest x8 20.5 us: correlate(): pl.pallas_call(functools.partial(correlate_kernel, layout), in_specs=[pl....]
    unnamed x6 -> x24, local copies, waits for them, and re-layouts: 6.15 us -> 1.85 us
    all_to_all x2, starting transfers between devices: 14.6 us -> 17.8 us  [turn(): lax.all_to_all(x, 'feed', split_axis=0, concat_axis=0, tiled=True, axis_i...]
  transfers between devices with their start and end apart: 19 -> 19, of which waited for: 12 -> 12; matrix products, arithmetic and copies ran while one was open for 1% -> 2% of each run, Pallas kernels for 10% -> 16%
where the time goes in v2:
time: 178 us
  waiting for transfers between devices  67.3 us (38%)
  starting transfers between devices  60.2 us (34%)
  Pallas kernels  42.9 us (24%)
  local copies, waits for them, and re-layouts  4.03 us (2%)
  other arithmetic  2.1 us (1%)
    ppermute x16, waiting for transfers between devices, along_z(): return lax.ppermute(x, ('tm', 'feed'), pairs)  59.6 us
    ppermute x16, starting transfers between devices, along_z(): return lax.ppermute(x, ('tm', 'feed'), pairs)  36.7 us
    pallas_call x8, Pallas kernels, correlate(): pl.pallas_call(functools.partial(correlate_kernel, layout), in_specs=[pl....  20.5 us
    all_to_all x2, starting transfers between devices, turn(): lax.all_to_all(x, 'feed', split_axis=0, concat_axis=0, tiled=True, axis_i...  17.8 us
    all_to_all x2, waiting for transfers between devices, turn(): lax.all_to_all(x, 'feed', split_axis=0, concat_axis=0, tiled=True, axis_i...  7.74 us
    pallas_call x1, Pallas kernels, dft(): pl.pallas_call(functools.partial(dft_kernel, dests), in_specs=[vmem] * 4,...  7.73 us
    ppermute x1, starting transfers between devices, per_device(): arrived = lax.ppermute(carried, 'tm', [(i, i + 1) for i in range(N_TM - 1)])  5.74 us
    pallas_call x2, Pallas kernels, move(): pl.pallas_call(functools.partial(move_kernel, moves, len(arrays)), in_spe...  4.25 us
  transfers between devices with their start and end apart: 19, of which 12 were waited for; matrix products, arithmetic and copies ran while one was open for 2% of the time, Pallas kernels for 16%

profile of v2, /device:TPU:1, one launch (start us, length us, event | category | flops | bytes accessed | tf_op | source)
XLA Modules:
  0.0 177.6 jit_solution(93439422977046884)
XLA Ops:
  1.8 5.7 %collective-permute-start = (bf16[48,2048]{1,0:T(8,128)(2,1)S(1)}, bf16[48,2048]{1,0:T(8,128)(2,1)S(1)}, u32[]{:S(2)}, u32[]{:S(2)}) collective-permute-start(bf16[48,2048]{1,0:T(8,128)(2,1)S(1)} %carry.1), channel_id=1, source_target_pairs={{0,64},{64,128},{128,192},{1,65},{65,129},{129,193},{2,66},{66,130... | collective-permute-start | bytes 589832 | tf_op jit(solution)/shard_map/ppermute | solution.py:372
  10.8 4.1 %own_filter.1 = (bf16[1024,2048]{1,0:T(8,128)(2,1)S(1)}, f32[48,2048]{1,0:T(8,128)S(1)}) custom-call(s32[16,131072]{1,0:T(8,128)} %v_ref.3, f32[4,2048]{1,0:T(4,128)S(1)} %copy-done.3), custom_call_target="tpu_custom_call" | custom-call | tf_op jit(solution)/shard_map/own_filter/pallas_call | solution.py:142
  15.0 7.7 %dft.1 = (bf16[40,8,16,128]{3,2,1,0:T(8,128)(2,1)}, bf16[8,8,16,128]{3,2,1,0:T(8,128)(2,1)S(1)}, bf16[8,8,16,128]{3,2,1,0:T(8,128)(2,1)S(1)}, bf16[8,8,16,128]{3,2,1,0:T(8,128)(2,1)S(1)}) custom-call(bf16[1024,2048]{1,0:T(8,128)(2,1)S(1)} %get-tuple-element.37.f_ref, f32[48,2048]{1,0:T(8,128)S(1)} %get-tuple-element.38.head_ref, ...), custom_call_target="tpu_custom_call" | custom-call | tf_op jit(solution)/shard_map/dft/pallas_call | solution.py:227
  22.7 8.0 %all-to-all-start.1 = ((bf16[320,16,128]{2,1,0:T(8,128)(2,1)}), bf16[320,16,128]{2,1,0:T(8,128)(2,1)S(1)}, u32[]{:S(2)}, u32[]{:S(2)}) async-start(bf16[320,16,128]{2,1,0:T(8,128)(2,1)} %bitcast.6), calls=%async_computation.1 | async-start | bytes 2621440 | tf_op jit(solution)/shard_map/all_to_all | solution.py:62
  30.7 7.0 %collective-permute-start.3 = (bf16[8,8,16,128]{3,2,1,0:T(8,128)(2,1)S(1)}, bf16[8,8,16,128]{3,2,1,0:T(8,128)(2,1)S(1)}, u32[]{:S(2)}, u32[]{:S(2)}) collective-permute-start(bf16[8,8,16,128]{3,2,1,0:T(8,128)(2,1)S(1)} %get-tuple-element.44), channel_id=1, source_target_pairs={{0,136},{1,137},{2,138},{3,139},{4,140},{5,141},{6,142},{7,143},{1... | collective-permute-start | bytes 786440 | tf_op jit(solution)/shard_map/ppermute | solution.py:53
  37.7 4.8 %collective-permute-start.1 = (bf16[8,8,16,128]{3,2,1,0:T(8,128)(2,1)S(1)}, bf16[8,8,16,128]{3,2,1,0:T(8,128)(2,1)}, u32[]{:S(2)}, u32[]{:S(2)}) collective-permute-start(bf16[8,8,16,128]{3,2,1,0:T(8,128)(2,1)S(1)} %get-tuple-element.42.refs_4_), channel_id=1, source_target_pairs={{0,192},{1,193},{2,194},{3,195},{4,196},{5,197},{6,198},{7,199},{1... | collective-permute-start | bytes 786440 | tf_op jit(solution)/shard_map/ppermute | solution.py:53
  42.5 7.7 %all-to-all-done.1 = bf16[320,16,128]{2,1,0:T(8,128)(2,1)S(1)} async-done(((bf16[320,16,128]{2,1,0:T(8,128)(2,1)}), bf16[320,16,128]{2,1,0:T(8,128)(2,1)S(1)}, u32[]{:S(2)}, u32[]{:S(2)}) %all-to-all-start.1) | async-done | bytes 1310752 | tf_op jit(solution)/shard_map/all_to_all | solution.py:62
  52.9 7.3 %collective-permute-start.7 = (bf16[8,8,16,128]{3,2,1,0:T(8,128)(2,1)S(1)}, bf16[8,8,16,128]{3,2,1,0:T(8,128)(2,1)}, u32[]{:S(2)}, u32[]{:S(2)}) collective-permute-start(bf16[8,8,16,128]{3,2,1,0:T(8,128)(2,1)S(1)} %get-tuple-element.53), channel_id=1, source_target_pairs={{0,192},{1,193},{2,194},{3,195},{4,196},{5,197},{6,198},{7,199},{1... | collective-permute-start | bytes 786440 | tf_op jit(solution)/shard_map/ppermute | solution.py:53
  62.8 7.5 %collective-permute-done.1.refs_1_ = bf16[8,8,16,128]{3,2,1,0:T(8,128)(2,1)} collective-permute-done((bf16[8,8,16,128]{3,2,1,0:T(8,128)(2,1)S(1)}, bf16[8,8,16,128]{3,2,1,0:T(8,128)(2,1)}, u32[]{:S(2)}, u32[]{:S(2)}) %collective-permute-start.1) | collective-permute-done | bytes 262176 | tf_op jit(solution)/shard_map/ppermute | solution.py:53
  70.4 2.7 %move.2 = bf16[4,8,12,16,128]{4,3,2,1,0:T(8,128)(2,1)} custom-call(bf16[8,8,16,128]{3,2,1,0:T(8,128)(2,1)} %copy-done.1, bf16[8,8,16,128]{3,2,1,0:T(8,128)(2,1)} %collective-permute-done.1.refs_1_, bf16[8,8,16,128]{3,2,1,0:T(8,128)(2,1)} %collective-permute-done.4.refs_2_, bf16[8,8,16,128]{3,2,1,0:T(8,128)(2,1)} %collective-permute-done.2.refs_3_, ...), custom_call_target="tpu_custom_call" | custom-call | tf_op jit(solution)/shard_map/move/pallas_call | solution.py:255
  73.1 9.7 %all-to-all-start = ((bf16[384,16,128]{2,1,0:T(8,128)(2,1)}), bf16[384,16,128]{2,1,0:T(8,128)(2,1)}, u32[]{:S(2)}, u32[]{:S(2)}) async-start(bf16[384,16,128]{2,1,0:T(8,128)(2,1)} %bitcast.4), calls=%async_computation | async-start | bytes 3145728 | tf_op jit(solution)/shard_map/all_to_all | solution.py:62
  84.8 3.4 %collective-permute-done.5.refs_1_ = bf16[16,8,16,128]{3,2,1,0:T(8,128)(2,1)S(1)} collective-permute-done((bf16[16,8,16,128]{3,2,1,0:T(8,128)(2,1)S(1)}, bf16[16,8,16,128]{3,2,1,0:T(8,128)(2,1)S(1)}, u32[]{:S(2)}, u32[]{:S(2)}) %collective-permute-start.5) | collective-permute-done | bytes 524320 | tf_op jit(solution)/shard_map/ppermute | solution.py:53
  88.2 4.8 %collective-permute-done.6.refs_2_ = bf16[16,8,16,128]{3,2,1,0:T(8,128)(2,1)S(1)} collective-permute-done((bf16[16,8,16,128]{3,2,1,0:T(8,128)(2,1)S(1)}, bf16[16,8,16,128]{3,2,1,0:T(8,128)(2,1)S(1)}, u32[]{:S(2)}, u32[]{:S(2)}) %collective-permute-start.6) | collective-permute-done | bytes 524320 | tf_op jit(solution)/shard_map/ppermute | solution.py:53
  93.8 3.6 %collective-permute-start.11 = (bf16[8,8,16,128]{3,2,1,0:T(8,128)(2,1)}, bf16[8,8,16,128]{3,2,1,0:T(8,128)(2,1)S(1)}, u32[]{:S(2)}, u32[]{:S(2)}) collective-permute-start(bf16[8,8,16,128]{3,2,1,0:T(8,128)(2,1)} %pad_maximum_fusion.2), channel_id=1, source_target_pairs={{0,192},{1,193},{2,194},{3,195},{4,196},{5,197},{6,198},{7,199},{1... | collective-permute-start | bytes 786440 | tf_op jit(solution)/shard_map/ppermute | solution.py:53
  97.6 3.6 %collective-permute-start.9 = (bf16[8,8,16,128]{3,2,1,0:T(8,128)(2,1)S(1)}, bf16[8,8,16,128]{3,2,1,0:T(8,128)(2,1)S(1)}, u32[]{:S(2)}, u32[]{:S(2)}) collective-permute-start(bf16[8,8,16,128]{3,2,1,0:T(8,128)(2,1)S(1)} %pad_maximum_fusion), channel_id=1, source_target_pairs={{0,192},{1,193},{2,194},{3,195},{4,196},{5,197},{6,198},{7,199},{1... | collective-permute-start | bytes 786440 | tf_op jit(solution)/shard_map/ppermute | solution.py:53
  101.3 3.6 %collective-permute-done.12.refs_4_ = bf16[8,8,16,128]{3,2,1,0:T(8,128)(2,1)S(1)} collective-permute-done((bf16[8,8,16,128]{3,2,1,0:T(8,128)(2,1)S(1)}, bf16[8,8,16,128]{3,2,1,0:T(8,128)(2,1)S(1)}, u32[]{:S(2)}, u32[]{:S(2)}) %collective-permute-start.12) | collective-permute-done | bytes 262176 | tf_op jit(solution)/shard_map/ppermute | solution.py:53
  104.9 2.2 %collective-permute-done.11.refs_4_ = bf16[8,8,16,128]{3,2,1,0:T(8,128)(2,1)S(1)} collective-permute-done((bf16[8,8,16,128]{3,2,1,0:T(8,128)(2,1)}, bf16[8,8,16,128]{3,2,1,0:T(8,128)(2,1)S(1)}, u32[]{:S(2)}, u32[]{:S(2)}) %collective-permute-start.11) | collective-permute-done | bytes 262176 | tf_op jit(solution)/shard_map/ppermute | solution.py:53
  107.2 10.9 %collective-permute-done.10.refs_4_ = bf16[8,8,16,128]{3,2,1,0:T(8,128)(2,1)S(1)} collective-permute-done((bf16[8,8,16,128]{3,2,1,0:T(8,128)(2,1)S(1)}, bf16[8,8,16,128]{3,2,1,0:T(8,128)(2,1)S(1)}, u32[]{:S(2)}, u32[]{:S(2)}) %collective-permute-start.10) | collective-permute-done | bytes 262176 | tf_op jit(solution)/shard_map/ppermute | solution.py:53
  118.0 1.6 collective-permute-done.9.refs_4_
  119.7 2.6 %correlate.13 = bf16[256,1024]{1,0:T(8,128)(2,1)S(1)} custom-call(s32[2]{0:T(128)S(1)} %pad_add_fusion.3.where_ref, bf16[4,8,12,16,128]{4,3,2,1,0:T(8,128)(2,1)} %bitcast.5.refs_0_, bf16[16,8,16,128]{3,2,1,0:T(8,128)(2,1)} %copy-done.4, bf16[16,8,16,128]{3,2,1,0:T(8,128)(2,1)} %copy-done.5, bf16[8,8,16,128]{3,2,1,0:T(8,128)(2,1)} %collective-permute-done.7.refs_3_, ...), custom_call_target="tpu_custom_call" | custom-call | tf_op jit(solution)/shard_map/correlate/pallas_call | solution.py:314
  122.3 2.6 %correlate.12 = bf16[256,1024]{1,0:T(8,128)(2,1)S(1)} custom-call(s32[2]{0:T(128)S(1)} %pad_add_fusion.2.where_ref, bf16[4,8,12,16,128]{4,3,2,1,0:T(8,128)(2,1)} %bitcast.5.refs_0_, bf16[16,8,16,128]{3,2,1,0:T(8,128)(2,1)} %copy-done.4, bf16[16,8,16,128]{3,2,1,0:T(8,128)(2,1)} %copy-done.5, bf16[8,8,16,128]{3,2,1,0:T(8,128)(2,1)} %collective-permute-done.8.refs_3_, ...), custom_call_target="tpu_custom_call" | custom-call | tf_op jit(solution)/shard_map/correlate/pallas_call | solution.py:314
  124.9 3.6 %collective-permute-start.15 = (bf16[256,1024]{1,0:T(8,128)(2,1)S(1)}, bf16[256,1024]{1,0:T(8,128)(2,1)S(1)}, u32[]{:S(2)}, u32[]{:S(2)}) collective-permute-start(bf16[256,1024]{1,0:T(8,128)(2,1)S(1)} %correlate.12), channel_id=1, source_target_pairs={{0,192},{1,193},{2,194},{3,195},{4,196},{5,197},{6,198},{7,199},{1... | collective-permute-start | bytes 1572872 | tf_op jit(solution)/shard_map/ppermute | solution.py:53
  128.6 2.6 %correlate.11 = bf16[256,1024]{1,0:T(8,128)(2,1)S(1)} custom-call(s32[2]{0:T(128)S(1)} %pad_add_fusion.3.where_ref, bf16[4,8,12,16,128]{4,3,2,1,0:T(8,128)(2,1)} %bitcast.5.refs_0_, bf16[16,8,16,128]{3,2,1,0:T(8,128)(2,1)} %copy-done.4, bf16[16,8,16,128]{3,2,1,0:T(8,128)(2,1)} %copy-done.5, bf16[8,8,16,128]{3,2,1,0:T(8,128)(2,1)} %collective-permute-done.7.refs_3_, ...), custom_call_target="tpu_custom_call" | custom-call | tf_op jit(solution)/shard_map/correlate/pallas_call | solution.py:314
  131.4 2.6 %correlate.10 = bf16[256,1024]{1,0:T(8,128)(2,1)S(1)} custom-call(s32[2]{0:T(128)S(1)} %pad_add_fusion.2.where_ref, bf16[4,8,12,16,128]{4,3,2,1,0:T(8,128)(2,1)} %bitcast.5.refs_0_, bf16[16,8,16,128]{3,2,1,0:T(8,128)(2,1)} %copy-done.4, bf16[16,8,16,128]{3,2,1,0:T(8,128)(2,1)} %copy-done.5, bf16[8,8,16,128]{3,2,1,0:T(8,128)(2,1)} %collective-permute-done.8.refs_3_, ...), custom_call_target="tpu_custom_call" | custom-call | tf_op jit(solution)/shard_map/correlate/pallas_call | solution.py:314
  134.0 3.6 %collective-permute-start.13 = (bf16[256,1024]{1,0:T(8,128)(2,1)S(1)}, bf16[256,1024]{1,0:T(8,128)(2,1)S(1)}, u32[]{:S(2)}, u32[]{:S(2)}) collective-permute-start(bf16[256,1024]{1,0:T(8,128)(2,1)S(1)} %correlate.10), channel_id=1, source_target_pairs={{0,192},{1,193},{2,194},{3,195},{4,196},{5,197},{6,198},{7,199},{1... | collective-permute-start | bytes 1572872 | tf_op jit(solution)/shard_map/ppermute | solution.py:53
  137.7 2.6 %correlate.15.refs_7_ = bf16[256,1024]{1,0:T(8,128)(2,1)S(1)} custom-call(s32[2]{0:T(128)S(1)} %pad_add_fusion.1.where_ref, bf16[4,8,12,16,128]{4,3,2,1,0:T(8,128)(2,1)} %bitcast.5.refs_0_, bf16[16,8,16,128]{3,2,1,0:T(8,128)(2,1)} %copy-done.4, bf16[16,8,16,128]{3,2,1,0:T(8,128)(2,1)} %copy-done.5, bf16[8,8,16,128]{3,2,1,0:T(8,128)(2,1)} %collective-permute-done.7.refs_3_, ...), custom_call_target="tpu_custom_call" | custom-call | tf_op jit(solution)/shard_map/correlate/pallas_call | solution.py:314
  140.3 2.6 %correlate.14.refs_6_ = bf16[256,1024]{1,0:T(8,128)(2,1)S(1)} custom-call(s32[2]{0:T(128)S(1)} %pad_add_fusion.1.where_ref, bf16[4,8,12,16,128]{4,3,2,1,0:T(8,128)(2,1)} %bitcast.5.refs_0_, bf16[16,8,16,128]{3,2,1,0:T(8,128)(2,1)} %copy-done.4, bf16[16,8,16,128]{3,2,1,0:T(8,128)(2,1)} %copy-done.5, bf16[8,8,16,128]{3,2,1,0:T(8,128)(2,1)} %collective-permute-done.7.refs_3_, ...), custom_call_target="tpu_custom_call" | custom-call | tf_op jit(solution)/shard_map/correlate/pallas_call | solution.py:314
  142.9 2.6 %correlate.9.refs_1_ = bf16[256,1024]{1,0:T(8,128)(2,1)S(1)} custom-call(s32[2]{0:T(128)S(1)} %pad_add_fusion.1.where_ref, bf16[4,8,12,16,128]{4,3,2,1,0:T(8,128)(2,1)} %bitcast.5.refs_0_, bf16[16,8,16,128]{3,2,1,0:T(8,128)(2,1)} %copy-done.4, bf16[16,8,16,128]{3,2,1,0:T(8,128)(2,1)} %copy-done.5, bf16[8,8,16,128]{3,2,1,0:T(8,128)(2,1)} %collective-permute-done.8.refs_3_, ...), custom_call_target="tpu_custom_call" | custom-call | tf_op jit(solution)/shard_map/correlate/pallas_call | solution.py:314
  145.4 2.6 %correlate.8.refs_0_ = bf16[256,1024]{1,0:T(8,128)(2,1)S(1)} custom-call(s32[2]{0:T(128)S(1)} %pad_add_fusion.1.where_ref, bf16[4,8,12,16,128]{4,3,2,1,0:T(8,128)(2,1)} %bitcast.5.refs_0_, bf16[16,8,16,128]{3,2,1,0:T(8,128)(2,1)} %copy-done.4, bf16[16,8,16,128]{3,2,1,0:T(8,128)(2,1)} %copy-done.5, bf16[8,8,16,128]{3,2,1,0:T(8,128)(2,1)} %collective-permute-done.8.refs_3_, ...), custom_call_target="tpu_custom_call" | custom-call | tf_op jit(solution)/shard_map/correlate/pallas_call | solution.py:314
  148.0 12.8 %collective-permute-done.16.refs_5_ = bf16[256,1024]{1,0:T(8,128)(2,1)S(1)} collective-permute-done((bf16[256,1024]{1,0:T(8,128)(2,1)S(1)}, bf16[256,1024]{1,0:T(8,128)(2,1)S(1)}, u32[]{:S(2)}, u32[]{:S(2)}) %collective-permute-start.16) | collective-permute-done | bytes 524320 | tf_op jit(solution)/shard_map/ppermute | solution.py:53
  162.4 9.7 %collective-permute-done.14.refs_4_ = bf16[256,1024]{1,0:T(8,128)(2,1)S(1)} collective-permute-done((bf16[256,1024]{1,0:T(8,128)(2,1)S(1)}, bf16[256,1024]{1,0:T(8,128)(2,1)S(1)}, u32[]{:S(2)}, u32[]{:S(2)}) %collective-permute-start.14) | collective-permute-done | bytes 524320 | tf_op jit(solution)/shard_map/ppermute | solution.py:53
  173.6 3.9 %gather_planes.1 = bf16[256,8,1024]{2,1,0:T(8,128)(2,1)} custom-call(s32[1]{0:T(128)} %bitcast.position_ref, bf16[256,1024]{1,0:T(8,128)(2,1)S(1)} %correlate.8.refs_0_, bf16[256,1024]{1,0:T(8,128)(2,1)S(1)} %correlate.9.refs_1_, bf16[256,1024]{1,0:T(8,128)(2,1)S(1)} %collective-permute-done.13.refs_2_, ...), custom_call_target="tpu_custom_call" | custom-call | tf_op jit(solution)/shard_map/gather_planes/pallas_call | solution.py:346
  (68 shorter events, 16.3 us)
Async XLA Ops:
  0.0 0.8 copy-start.2
  1.8 8.9 %copy-start.3 = (f32[4,2048]{1,0:T(4,128)S(1)}, f32[4,2048]{1,0:T(4,128)}, u32[]{:S(2)}) copy-start(f32[4,2048]{1,0:T(4,128)} %w_ref.2) | copy-start | bytes 98308
  1.8 13.1 %collective-permute-start = (bf16[48,2048]{1,0:T(8,128)(2,1)S(1)}, bf16[48,2048]{1,0:T(8,128)(2,1)S(1)}, u32[]{:S(2)}, u32[]{:S(2)}) collective-permute-start(bf16[48,2048]{1,0:T(8,128)(2,1)S(1)} %carry.1), channel_id=1, source_target_pairs={{0,64},{64,128},{128,192},{1,65},{65,129},{129,193},{2,66},{66,130... | collective-permute-start | bytes 589832 | tf_op jit(solution)/shard_map/ppermute | solution.py:372
  22.7 47.6 %copy-start = (bf16[8,8,16,128]{3,2,1,0:T(8,128)(2,1)}, bf16[8,8,16,128]{3,2,1,0:T(8,128)(2,1)S(1)}, u32[]{:S(2)}) copy-start(bf16[8,8,16,128]{3,2,1,0:T(8,128)(2,1)S(1)} %get-tuple-element.42.refs_4_) | copy-start | bytes 786436
  22.7 47.7 %copy-start.1 = (bf16[8,8,16,128]{3,2,1,0:T(8,128)(2,1)}, bf16[8,8,16,128]{3,2,1,0:T(8,128)(2,1)S(1)}, u32[]{:S(2)}) copy-start(bf16[8,8,16,128]{3,2,1,0:T(8,128)(2,1)S(1)} %get-tuple-element.41.refs_0_) | copy-start | bytes 786436
  22.7 27.5 %all-to-all-start.1 = ((bf16[320,16,128]{2,1,0:T(8,128)(2,1)}), bf16[320,16,128]{2,1,0:T(8,128)(2,1)S(1)}, u32[]{:S(2)}, u32[]{:S(2)}) async-start(bf16[320,16,128]{2,1,0:T(8,128)(2,1)} %bitcast.6), calls=%async_computation.1 | async-start | bytes 2621440 | tf_op jit(solution)/shard_map/all_to_all | solution.py:62
  30.7 29.4 %collective-permute-start.3 = (bf16[8,8,16,128]{3,2,1,0:T(8,128)(2,1)S(1)}, bf16[8,8,16,128]{3,2,1,0:T(8,128)(2,1)S(1)}, u32[]{:S(2)}, u32[]{:S(2)}) collective-permute-start(bf16[8,8,16,128]{3,2,1,0:T(8,128)(2,1)S(1)} %get-tuple-element.44), channel_id=1, source_target_pairs={{0,136},{1,137},{2,138},{3,139},{4,140},{5,141},{6,142},{7,143},{1... | collective-permute-start | bytes 786440 | tf_op jit(solution)/shard_map/ppermute | solution.py:53
  37.7 23.6 %collective-permute-start.4 = (bf16[8,8,16,128]{3,2,1,0:T(8,128)(2,1)S(1)}, bf16[8,8,16,128]{3,2,1,0:T(8,128)(2,1)}, u32[]{:S(2)}, u32[]{:S(2)}) collective-permute-start(bf16[8,8,16,128]{3,2,1,0:T(8,128)(2,1)S(1)} %get-tuple-element.44), channel_id=1, source_target_pairs={{0,72},{1,73},{2,74},{3,75},{4,76},{5,77},{6,78},{7,79},{16,88},{1... | collective-permute-start | bytes 786440 | tf_op jit(solution)/shard_map/ppermute | solution.py:53
  37.7 32.6 %collective-permute-start.1 = (bf16[8,8,16,128]{3,2,1,0:T(8,128)(2,1)S(1)}, bf16[8,8,16,128]{3,2,1,0:T(8,128)(2,1)}, u32[]{:S(2)}, u32[]{:S(2)}) collective-permute-start(bf16[8,8,16,128]{3,2,1,0:T(8,128)(2,1)S(1)} %get-tuple-element.42.refs_4_), channel_id=1, source_target_pairs={{0,192},{1,193},{2,194},{3,195},{4,196},{5,197},{6,198},{7,199},{1... | collective-permute-start | bytes 786440 | tf_op jit(solution)/shard_map/ppermute | solution.py:53
  42.5 27.8 %collective-permute-start.2 = (bf16[8,8,16,128]{3,2,1,0:T(8,128)(2,1)S(1)}, bf16[8,8,16,128]{3,2,1,0:T(8,128)(2,1)}, u32[]{:S(2)}, u32[]{:S(2)}) collective-permute-start(bf16[8,8,16,128]{3,2,1,0:T(8,128)(2,1)S(1)} %get-tuple-element.41.refs_0_), channel_id=1, source_target_pairs={{0,64},{1,65},{2,66},{3,67},{4,68},{5,69},{6,70},{7,71},{16,80},{1... | collective-permute-start | bytes 786440 | tf_op jit(solution)/shard_map/ppermute | solution.py:53
  50.2 1.1 copy-start.6
  52.9 29.9 %collective-permute-start.7 = (bf16[8,8,16,128]{3,2,1,0:T(8,128)(2,1)S(1)}, bf16[8,8,16,128]{3,2,1,0:T(8,128)(2,1)}, u32[]{:S(2)}, u32[]{:S(2)}) collective-permute-start(bf16[8,8,16,128]{3,2,1,0:T(8,128)(2,1)S(1)} %get-tuple-element.53), channel_id=1, source_target_pairs={{0,192},{1,193},{2,194},{3,195},{4,196},{5,197},{6,198},{7,199},{1... | collective-permute-start | bytes 786440 | tf_op jit(solution)/shard_map/ppermute | solution.py:53
  60.1 10.2 %copy-start.11 = (bf16[8,8,16,128]{3,2,1,0:T(8,128)(2,1)}, bf16[8,8,16,128]{3,2,1,0:T(8,128)(2,1)S(1)}, u32[]{:S(2)}) copy-start(bf16[8,8,16,128]{3,2,1,0:T(8,128)(2,1)S(1)} %collective-permute-done.3.refs_5_) | copy-start | bytes 786436
  60.1 22.7 %collective-permute-start.8 = (bf16[8,8,16,128]{3,2,1,0:T(8,128)(2,1)S(1)}, bf16[8,8,16,128]{3,2,1,0:T(8,128)(2,1)}, u32[]{:S(2)}, u32[]{:S(2)}) collective-permute-start(bf16[8,8,16,128]{3,2,1,0:T(8,128)(2,1)S(1)} %get-tuple-element.54), channel_id=1, source_target_pairs={{0,64},{1,65},{2,66},{3,67},{4,68},{5,69},{6,70},{7,71},{16,80},{1... | collective-permute-start | bytes 786440 | tf_op jit(solution)/shard_map/ppermute | solution.py:53
  61.3 26.9 %collective-permute-start.5 = (bf16[16,8,16,128]{3,2,1,0:T(8,128)(2,1)S(1)}, bf16[16,8,16,128]{3,2,1,0:T(8,128)(2,1)S(1)}, u32[]{:S(2)}, u32[]{:S(2)}) collective-permute-start(bf16[16,8,16,128]{3,2,1,0:T(8,128)(2,1)S(1)} %get-tuple-element.49), channel_id=1, source_target_pairs={{0,200},{1,201},{2,202},{3,203},{4,204},{5,205},{6,206},{7,207},{1... | collective-permute-start | bytes 1572872 | tf_op jit(solution)/shard_map/ppermute | solution.py:53
  70.3 22.6 %collective-permute-start.6 = (bf16[16,8,16,128]{3,2,1,0:T(8,128)(2,1)S(1)}, bf16[16,8,16,128]{3,2,1,0:T(8,128)(2,1)S(1)}, u32[]{:S(2)}, u32[]{:S(2)}) collective-permute-start(bf16[16,8,16,128]{3,2,1,0:T(8,128)(2,1)S(1)} %get-tuple-element.50), channel_id=1, source_target_pairs={{0,8},{1,9},{2,10},{3,11},{4,12},{5,13},{6,14},{7,15},{16,24},{17,... | collective-permute-start | bytes 1572872 | tf_op jit(solution)/shard_map/ppermute | solution.py:53
  73.1 46.6 %all-to-all-start = ((bf16[384,16,128]{2,1,0:T(8,128)(2,1)}), bf16[384,16,128]{2,1,0:T(8,128)(2,1)}, u32[]{:S(2)}, u32[]{:S(2)}) async-start(bf16[384,16,128]{2,1,0:T(8,128)(2,1)} %bitcast.4), calls=%async_computation | async-start | bytes 3145728 | tf_op jit(solution)/shard_map/all_to_all | solution.py:62
  88.2 31.5 %copy-start.4 = (bf16[16,8,16,128]{3,2,1,0:T(8,128)(2,1)}, bf16[16,8,16,128]{3,2,1,0:T(8,128)(2,1)S(1)}, u32[]{:S(2)}) copy-start(bf16[16,8,16,128]{3,2,1,0:T(8,128)(2,1)S(1)} %collective-permute-done.5.refs_1_) | copy-start | bytes 1572868
  92.9 26.7 %copy-start.5 = (bf16[16,8,16,128]{3,2,1,0:T(8,128)(2,1)}, bf16[16,8,16,128]{3,2,1,0:T(8,128)(2,1)S(1)}, u32[]{:S(2)}) copy-start(bf16[16,8,16,128]{3,2,1,0:T(8,128)(2,1)S(1)} %collective-permute-done.6.refs_2_) | copy-start | bytes 1572868
  93.0 11.9 %collective-permute-start.12 = (bf16[8,8,16,128]{3,2,1,0:T(8,128)(2,1)S(1)}, bf16[8,8,16,128]{3,2,1,0:T(8,128)(2,1)S(1)}, u32[]{:S(2)}, u32[]{:S(2)}) collective-permute-start(bf16[8,8,16,128]{3,2,1,0:T(8,128)(2,1)S(1)} %pad_maximum_fusion.3), channel_id=1, source_target_pairs={{0,64},{1,65},{2,66},{3,67},{4,68},{5,69},{6,70},{7,71},{16,80},{1... | collective-permute-start | bytes 786440 | tf_op jit(solution)/shard_map/ppermute | solution.py:53
  93.8 13.3 %collective-permute-start.11 = (bf16[8,8,16,128]{3,2,1,0:T(8,128)(2,1)}, bf16[8,8,16,128]{3,2,1,0:T(8,128)(2,1)S(1)}, u32[]{:S(2)}, u32[]{:S(2)}) collective-permute-start(bf16[8,8,16,128]{3,2,1,0:T(8,128)(2,1)} %pad_maximum_fusion.2), channel_id=1, source_target_pairs={{0,192},{1,193},{2,194},{3,195},{4,196},{5,197},{6,198},{7,199},{1... | collective-permute-start | bytes 786440 | tf_op jit(solution)/shard_map/ppermute | solution.py:53
  97.4 20.6 %collective-permute-start.10 = (bf16[8,8,16,128]{3,2,1,0:T(8,128)(2,1)S(1)}, bf16[8,8,16,128]{3,2,1,0:T(8,128)(2,1)S(1)}, u32[]{:S(2)}, u32[]{:S(2)}) collective-permute-start(bf16[8,8,16,128]{3,2,1,0:T(8,128)(2,1)S(1)} %pad_maximum_fusion.1), channel_id=1, source_target_pairs={{0,64},{1,65},{2,66},{3,67},{4,68},{5,69},{6,70},{7,71},{16,80},{1... | collective-permute-start | bytes 786440 | tf_op jit(solution)/shard_map/ppermute | solution.py:53
  97.6 22.1 %collective-permute-start.9 = (bf16[8,8,16,128]{3,2,1,0:T(8,128)(2,1)S(1)}, bf16[8,8,16,128]{3,2,1,0:T(8,128)(2,1)S(1)}, u32[]{:S(2)}, u32[]{:S(2)}) collective-permute-start(bf16[8,8,16,128]{3,2,1,0:T(8,128)(2,1)S(1)} %pad_maximum_fusion), channel_id=1, source_target_pairs={{0,192},{1,193},{2,194},{3,195},{4,196},{5,197},{6,198},{7,199},{1... | collective-permute-start | bytes 786440 | tf_op jit(solution)/shard_map/ppermute | solution.py:53
  104.9 14.7 %copy-start.7 = (bf16[8,8,16,128]{3,2,1,0:T(8,128)(2,1)}, bf16[8,8,16,128]{3,2,1,0:T(8,128)(2,1)S(1)}, u32[]{:S(2)}) copy-start(bf16[8,8,16,128]{3,2,1,0:T(8,128)(2,1)S(1)} %collective-permute-done.12.refs_4_) | copy-start | bytes 786436
  107.2 15.2 %copy-start.8 = (bf16[8,8,16,128]{3,2,1,0:T(8,128)(2,1)}, bf16[8,8,16,128]{3,2,1,0:T(8,128)(2,1)S(1)}, u32[]{:S(2)}) copy-start(bf16[8,8,16,128]{3,2,1,0:T(8,128)(2,1)S(1)} %collective-permute-done.11.refs_4_) | copy-start | bytes 786436
  118.0 10.5 %copy-start.9 = (bf16[8,8,16,128]{3,2,1,0:T(8,128)(2,1)}, bf16[8,8,16,128]{3,2,1,0:T(8,128)(2,1)S(1)}, u32[]{:S(2)}) copy-start(bf16[8,8,16,128]{3,2,1,0:T(8,128)(2,1)S(1)} %collective-permute-done.10.refs_4_) | copy-start | bytes 786436
  119.6 11.5 %copy-start.10 = (bf16[8,8,16,128]{3,2,1,0:T(8,128)(2,1)}, bf16[8,8,16,128]{3,2,1,0:T(8,128)(2,1)S(1)}, u32[]{:S(2)}) copy-start(bf16[8,8,16,128]{3,2,1,0:T(8,128)(2,1)S(1)} %collective-permute-done.9.refs_4_) | copy-start | bytes 786436
  122.2 38.6 %collective-permute-start.16 = (bf16[256,1024]{1,0:T(8,128)(2,1)S(1)}, bf16[256,1024]{1,0:T(8,128)(2,1)S(1)}, u32[]{:S(2)}, u32[]{:S(2)}) collective-permute-start(bf16[256,1024]{1,0:T(8,128)(2,1)S(1)} %correlate.13), channel_id=1, source_target_pairs={{0,64},{1,65},{2,66},{3,67},{4,68},{5,69},{6,70},{7,71},{16,80},{1... | collective-permute-start | bytes 1572872 | tf_op jit(solution)/shard_map/ppermute | solution.py:53
  124.9 37.5 %collective-permute-start.15 = (bf16[256,1024]{1,0:T(8,128)(2,1)S(1)}, bf16[256,1024]{1,0:T(8,128)(2,1)S(1)}, u32[]{:S(2)}, u32[]{:S(2)}) collective-permute-start(bf16[256,1024]{1,0:T(8,128)(2,1)S(1)} %correlate.12), channel_id=1, source_target_pairs={{0,192},{1,193},{2,194},{3,195},{4,196},{5,197},{6,198},{7,199},{1... | collective-permute-start | bytes 1572872 | tf_op jit(solution)/shard_map/ppermute | solution.py:53
  131.1 40.9 %collective-permute-start.14 = (bf16[256,1024]{1,0:T(8,128)(2,1)S(1)}, bf16[256,1024]{1,0:T(8,128)(2,1)S(1)}, u32[]{:S(2)}, u32[]{:S(2)}) collective-permute-start(bf16[256,1024]{1,0:T(8,128)(2,1)S(1)} %correlate.11), channel_id=1, source_target_pairs={{0,64},{1,65},{2,66},{3,67},{4,68},{5,69},{6,70},{7,71},{16,80},{1... | collective-permute-start | bytes 1572872 | tf_op jit(solution)/shard_map/ppermute | solution.py:53
  134.0 39.6 %collective-permute-start.13 = (bf16[256,1024]{1,0:T(8,128)(2,1)S(1)}, bf16[256,1024]{1,0:T(8,128)(2,1)S(1)}, u32[]{:S(2)}, u32[]{:S(2)}) collective-permute-start(bf16[256,1024]{1,0:T(8,128)(2,1)S(1)} %correlate.10), channel_id=1, source_target_pairs={{0,192},{1,193},{2,194},{3,195},{4,196},{5,197},{6,198},{7,199},{1... | collective-permute-start | bytes 1572872 | tf_op jit(solution)/shard_map/ppermute | solution.py:53

commit v3 on v2

--- a/solution.py
+++ b/solution.py
@@ -196,47 +196,65 @@
     )(coarse[0], coarse[1], fine[0] * scale, fine[1] * scale)
 
 
-def dft_kernel(dests, f_ref, head_ref, arrived_ref, t_ref, *refs):
-    outs, (fixed, wide, turned) = refs[:-3], refs[-3:]
+def product_kernel(f_ref, t_ref, out_ref):
+    for part in range(t_ref.shape[0]):
+        both = jnp.dot(f_ref[...], t_ref[part], preferred_element_type=jnp.float32)
+        for r in range(2):
+            out_ref[part, r] = both[:, r * 128 : (r + 1) * 128]
+
+
+def product(filtered, dft_table):
+    vmem = pl.BlockSpec(memory_space=pltpu.VMEM)
+    return pl.pallas_call(
+        product_kernel,
+        in_specs=[vmem] * 2,
+        out_specs=vmem,
+        out_shape=jax.ShapeDtypeStruct((dft_table.shape[0], 2, SPEC * INP, 128), jnp.float32),
+        compiler_params=params(12),
+        name="product",
+    )(filtered, dft_table)
+
+
+def dft_kernel(dests, position_ref, wide, head_ref, arrived_ref, t_ref, *refs):
+    outs, (heads, turned) = refs[:-2], refs[-2:]
     head_rows = head_ref.shape[0]
-    fixed[...] = (head_ref[...] + arrived_ref[...].astype(jnp.float32)).astype(jnp.bfloat16)
+    arrived = jnp.where(position_ref[0] > 0, arrived_ref[...].astype(jnp.float32), 0.0)
+    fixed = (head_ref[...] + arrived).astype(jnp.bfloat16)
     for part in range(t_ref.shape[0]):
-        first = jnp.dot(fixed[...], t_ref[part], preferred_element_type=jnp.float32)
-        rest = jnp.dot(f_ref[head_rows:, :], t_ref[part], preferred_element_type=jnp.float32)
+        first = jnp.dot(fixed, t_ref[part], preferred_element_type=jnp.float32)
         for r in range(2):
-            wide[part, r, :head_rows, :] = first[:, r * 128 : (r + 1) * 128]
-            wide[part, r, head_rows:, :] = rest[:, r * 128 : (r + 1) * 128]
+            heads[part, r, :head_rows, :] = first[:, r * 128 : (r + 1) * 128]
+    is_head = lax.broadcasted_iota(jnp.int32, (8, 128), 0) < TAPS - 1
     for part in range(t_ref.shape[0]):
         for i in range(INP):
-            rows = pl.ds(i, SPEC, stride=INP)
-            both = jnp.concatenate([wide[part, 0, rows, :], wide[part, 1, rows, :]], 0)
-            turned[part, pl.ds(i, 128, stride=INP), :] = both.T
+            frames = []
+            for r in range(2):
+                top, rest = pl.ds(i, 8, stride=INP), pl.ds(i + 8 * INP, SPEC - 8, stride=INP)
+                frames.append(jnp.where(is_head, heads[part, r, top, :], wide[part, r, top, :]))
+                frames.append(wide[part, r, rest, :])
+            turned[part, pl.ds(i, 128, stride=INP), :] = jnp.concatenate(frames, 0).T
         for run in range(4):
             rows = slice(run * N_D * INP, (run + 1) * N_D * INP)
             block = turned[part, rows, :].astype(jnp.bfloat16).reshape(BLOCK)
-            for n, (which, at) in enumerate(dests[part * 4 + run]):
-                if outs[which].shape[0] == at + 2:
-                    outs[which][at:] = block[2 * n : 2 * n + 2]
-                else:
-                    outs[which][at : at + 4] = block
-
-
-def dft(filtered, head, arrived, dft_table, counts, dests):
+            for which, at in dests[part * 4 + run]:
+                outs[which][at : at + 4] = block
+
+
+def dft(position, wide, head, arrived, dft_table, counts, dests):
     parts = dft_table.shape[0]
     vmem = pl.BlockSpec(memory_space=pltpu.VMEM)
     return pl.pallas_call(
         functools.partial(dft_kernel, dests),
-        in_specs=[vmem] * 4,
+        in_specs=[pl.BlockSpec(memory_space=pltpu.SMEM)] + [vmem] * 4,
         out_specs=[vmem] * len(counts),
         out_shape=[jax.ShapeDtypeStruct((count, *BLOCK[1:]), jnp.bfloat16) for count in counts],
         scratch_shapes=[
-            pltpu.VMEM(head.shape, jnp.bfloat16),
-            pltpu.VMEM((parts, 2, SPEC * INP, 128), jnp.float32),
+            pltpu.VMEM((parts, 2, 8 * INP, 128), jnp.float32),
             pltpu.VMEM((parts, 128 * INP, PIECE), jnp.float32),
         ],
-        compiler_params=params(24),
+        compiler_params=params(16),
         name="dft",
-    )(filtered, head, arrived, dft_table)
+    )(position, wide, head, arrived, dft_table)
 
 
 def move_kernel(moves, n_in, *refs):
@@ -369,14 +387,17 @@
     z = 2 * position + z_lo
     after, before = (position + 1) % N_TM, (position + N_TM - 1) % N_TM
     carried, first_channel = lax.optimization_barrier((carry(voltages, window), first_channel))
-    arrived = lax.ppermute(carried, "tm", [(i, i + 1) for i in range(N_TM - 1)])
-    dft_table, window = lax.optimization_barrier((table(first_channel, z), window))
+    arrived = along_z(carried, 2)
+    where = position.astype(jnp.int32).reshape(1)
+    dft_table, window, where = lax.optimization_barrier((table(first_channel, z), window, where))
     filtered, head = filter_own(voltages, window)
     planes = [None] * CH_DEV
 
     dests = [[(0, 4 * i)] for i in range(FAR)]
     dests += [[(1 + i // 2, i % 2 * 4)] for i in range(2 * N_Z - FAR)]
-    spectra, twos, zeros, fives = dft(filtered, head, arrived, dft_table, (4 * FAR, 8, 8, 8), dests)
+    spectra, twos, zeros, fives = dft(
+        where, product(filtered, dft_table), head, arrived, dft_table, (4 * FAR, 8, 8, 8), dests
+    )
     turned = turn(spectra.reshape(-1, INP, PIECE)).reshape(*BLOCK[:2], FAR, *BLOCK[2:])
     left_5, right_5 = both_ways(fives, fives, 3)
     left_2, right_0 = both_ways(twos, zeros, 2)
@@ -406,14 +427,18 @@
     left_31, right_71 = both_ways(sent_31, sent_71, 1)
     left_4, right_6 = both_ways(sent_4, sent_6, 2)
 
-    for which in range(2):
-        here, there = places(which)
+    def onward(which):
         part = slice(4 * which, 4 * which + 4)
-        far = both_ways(
+        return [
             jnp.concatenate([left_31[part], left_4[part]]),
             jnp.concatenate([right_71[part], right_6[part]]),
-            2,
-        )
+        ]
+
+    far_0 = both_ways(*onward(0), 2)
+    far_0, onward_1 = lax.optimization_barrier((far_0, onward(1)))
+    far_1 = both_ways(*onward_1, 2)
+    for which, far in enumerate((far_0, far_1)):
+        here, there = places(which)
         arrays = [packed, left_31, right_71, left_4, right_6, *far]
         planes[2 + which], planes[4 + which] = both_ways(
             correlate(before, z_lo, here, arrays), correlate(after, z_lo, there, arrays), 2

time: 178 us -> 171 us (0.961)
  starting transfers between devices: 60.2 us -> 50.4 us
    ppermute x1 -> x0, starting transfers between devices: 5.74 us -> none  [per_device(): arrived = lax.ppermute(carried, 'tm', [(i, i + 1) for i in range(N_TM - 1)])]
    ppermute x16 -> x17, starting transfers between devices: 36.7 us -> 31.3 us  [along_z(): return lax.ppermute(x, ('tm', 'feed'), pairs)]
    all_to_all x2, waiting for transfers between devices: 7.74 us -> 10.8 us  [turn(): lax.all_to_all(x, 'feed', split_axis=0, concat_axis=0, tiled=True, axis_i...]
    ppermute x16 -> x17, waiting for transfers between devices: 59.6 us -> 58.2 us  [along_z(): return lax.ppermute(x, ('tm', 'feed'), pairs)]
    pallas_call x1 -> x2, Pallas kernels: 7.73 us -> 8.5 us  [the longest x1 4.5 us: product(): pl.pallas_call(product_kernel, in_specs=[vmem] * 2, out_specs=vmem, out_s...]
  transfers between devices with their start and end apart: 19 -> 19, of which waited for: 12 -> 9; matrix products, arithmetic and copies ran while one was open for 2% -> 2% of each run, Pallas kernels for 16% -> 20%
where the time goes in v3:
time: 171 us; the launch traced here: 170 us
  waiting for transfers between devices  68.9 us (40%)
  starting transfers between devices  50.4 us (29%)
  Pallas kernels  43.6 us (25%)
  local copies, waits for them, and re-layouts  4.72 us (3%)
    ppermute x17, waiting for transfers between devices, along_z(): return lax.ppermute(x, ('tm', 'feed'), pairs)  58.2 us
    ppermute x17, starting transfers between devices, along_z(): return lax.ppermute(x, ('tm', 'feed'), pairs)  31.3 us
    pallas_call x8, Pallas kernels, correlate(): pl.pallas_call(functools.partial(correlate_kernel, layout), in_specs=[pl....  20.5 us
    all_to_all x2, starting transfers between devices, turn(): lax.all_to_all(x, 'feed', split_axis=0, concat_axis=0, tiled=True, axis_i...  19.2 us
    all_to_all x2, waiting for transfers between devices, turn(): lax.all_to_all(x, 'feed', split_axis=0, concat_axis=0, tiled=True, axis_i...  10.8 us
    pallas_call x1, Pallas kernels, product(): pl.pallas_call(product_kernel, in_specs=[vmem] * 2, out_specs=vmem, out_s...  4.5 us
    pallas_call x2, Pallas kernels, move(): pl.pallas_call(functools.partial(move_kernel, moves, len(arrays)), in_spe...  4.25 us
    pallas_call x1, Pallas kernels, filter_own(): pl.pallas_call(filter_kernel, in_specs=[pl.BlockSpec(memory_space=pltpu.H...  4.15 us
  transfers between devices with their start and end apart: 19, of which 9 were waited for; matrix products, arithmetic and copies ran while one was open for 2% of the time, Pallas kernels for 20%

profile of v3, /device:TPU:1, one launch (start us, length us, event | category | flops | bytes accessed | tf_op | source)
XLA Modules:
  0.0 170.1 jit_solution(11346895983785010934)
XLA Ops:
  1.8 3.9 %collective-permute-start = (bf16[48,2048]{1,0:T(8,128)(2,1)S(1)}, bf16[48,2048]{1,0:T(8,128)(2,1)S(1)}, u32[]{:S(2)}, u32[]{:S(2)}) collective-permute-start(bf16[48,2048]{1,0:T(8,128)(2,1)S(1)} %carry.1), channel_id=1, source_target_pairs={{0,64},{1,65},{2,66},{3,67},{4,68},{5,69},{6,70},{7,71},{16,80},{1... | collective-permute-start | bytes 589832 | tf_op jit(solution)/shard_map/ppermute | solution.py:53
  8.9 4.1 %own_filter.1 = (bf16[1024,2048]{1,0:T(8,128)(2,1)S(1)}, f32[48,2048]{1,0:T(8,128)S(1)}) custom-call(s32[16,131072]{1,0:T(8,128)} %v_ref.3, f32[4,2048]{1,0:T(4,128)S(1)} %copy-done.3), custom_call_target="tpu_custom_call" | custom-call | tf_op jit(solution)/shard_map/own_filter/pallas_call | solution.py:142
  13.1 4.5 %product.1.wide = f32[4,2,1024,128]{3,2,1,0:T(8,128)S(1)} custom-call(bf16[1024,2048]{1,0:T(8,128)(2,1)S(1)} %get-tuple-element.43.f_ref, bf16[4,2048,256]{2,1,0:T(8,128)(2,1)S(1)} %dft_table.1.t_ref), custom_call_target="tpu_custom_call" | custom-call | tf_op jit(solution)/shard_map/product/pallas_call | solution.py:208
  17.6 4.0 %dft.1 = (bf16[40,8,16,128]{3,2,1,0:T(8,128)(2,1)}, bf16[8,8,16,128]{3,2,1,0:T(8,128)(2,1)S(1)}, bf16[8,8,16,128]{3,2,1,0:T(8,128)(2,1)S(1)}, bf16[8,8,16,128]{3,2,1,0:T(8,128)(2,1)S(1)}) custom-call(s32[1]{0:T(128)} %bitcast.position_ref, f32[4,2,1024,128]{3,2,1,0:T(8,128)S(1)} %product.1.wide, f32[48,2048]{1,0:T(8,128)S(1)} %get-tuple-element.45.head_ref, ...), custom_call_target="tpu_custom_call" | custom-call | tf_op jit(solution)/shard_map/dft/pallas_call | solution.py:246
  21.6 8.0 %all-to-all-start.1 = ((bf16[320,16,128]{2,1,0:T(8,128)(2,1)}), bf16[320,16,128]{2,1,0:T(8,128)(2,1)S(1)}, u32[]{:S(2)}, u32[]{:S(2)}) async-start(bf16[320,16,128]{2,1,0:T(8,128)(2,1)} %bitcast.6), calls=%async_computation.1 | async-start | bytes 2621440 | tf_op jit(solution)/shard_map/all_to_all | solution.py:62
  29.6 2.9 %collective-permute-start.1 = (bf16[8,8,16,128]{3,2,1,0:T(8,128)(2,1)S(1)}, bf16[8,8,16,128]{3,2,1,0:T(8,128)(2,1)S(1)}, u32[]{:S(2)}, u32[]{:S(2)}) collective-permute-start(bf16[8,8,16,128]{3,2,1,0:T(8,128)(2,1)S(1)} %get-tuple-element.48.refs_4_), channel_id=1, source_target_pairs={{0,192},{1,193},{2,194},{3,195},{4,196},{5,197},{6,198},{7,199},{1... | collective-permute-start | bytes 786440 | tf_op jit(solution)/shard_map/ppermute | solution.py:53
  34.0 2.8 %collective-permute-start.3 = (bf16[8,8,16,128]{3,2,1,0:T(8,128)(2,1)S(1)}, bf16[8,8,16,128]{3,2,1,0:T(8,128)(2,1)}, u32[]{:S(2)}, u32[]{:S(2)}) collective-permute-start(bf16[8,8,16,128]{3,2,1,0:T(8,128)(2,1)S(1)} %get-tuple-element.50), channel_id=1, source_target_pairs={{0,136},{1,137},{2,138},{3,139},{4,140},{5,141},{6,142},{7,143},{1... | collective-permute-start | bytes 786440 | tf_op jit(solution)/shard_map/ppermute | solution.py:53
  38.0 10.8 %all-to-all-done.1 = bf16[320,16,128]{2,1,0:T(8,128)(2,1)S(1)} async-done(((bf16[320,16,128]{2,1,0:T(8,128)(2,1)}), bf16[320,16,128]{2,1,0:T(8,128)(2,1)S(1)}, u32[]{:S(2)}, u32[]{:S(2)}) %all-to-all-start.1) | async-done | bytes 1310752 | tf_op jit(solution)/shard_map/all_to_all | solution.py:62
  49.8 1.6 move.3
  51.4 3.3 %collective-permute-start.7 = (bf16[8,8,16,128]{3,2,1,0:T(8,128)(2,1)S(1)}, bf16[8,8,16,128]{3,2,1,0:T(8,128)(2,1)}, u32[]{:S(2)}, u32[]{:S(2)}) collective-permute-start(bf16[8,8,16,128]{3,2,1,0:T(8,128)(2,1)S(1)} %get-tuple-element.59), channel_id=1, source_target_pairs={{0,192},{1,193},{2,194},{3,195},{4,196},{5,197},{6,198},{7,199},{1... | collective-permute-start | bytes 786440 | tf_op jit(solution)/shard_map/ppermute | solution.py:53
  54.6 1.5 collective-permute-start.8
  57.4 4.5 %collective-permute-done.3.refs_5_ = bf16[8,8,16,128]{3,2,1,0:T(8,128)(2,1)} collective-permute-done((bf16[8,8,16,128]{3,2,1,0:T(8,128)(2,1)S(1)}, bf16[8,8,16,128]{3,2,1,0:T(8,128)(2,1)}, u32[]{:S(2)}, u32[]{:S(2)}) %collective-permute-start.3) | collective-permute-done | bytes 262176 | tf_op jit(solution)/shard_map/ppermute | solution.py:53
  61.9 2.9 %collective-permute-start.6 = (bf16[16,8,16,128]{3,2,1,0:T(8,128)(2,1)S(1)}, bf16[16,8,16,128]{3,2,1,0:T(8,128)(2,1)S(1)}, u32[]{:S(2)}, u32[]{:S(2)}) collective-permute-start(bf16[16,8,16,128]{3,2,1,0:T(8,128)(2,1)S(1)} %get-tuple-element.56), channel_id=1, source_target_pairs={{0,8},{1,9},{2,10},{3,11},{4,12},{5,13},{6,14},{7,15},{16,24},{17,... | collective-permute-start | bytes 1572872 | tf_op jit(solution)/shard_map/ppermute | solution.py:53
  65.8 2.7 %move.2 = bf16[4,8,12,16,128]{4,3,2,1,0:T(8,128)(2,1)} custom-call(bf16[8,8,16,128]{3,2,1,0:T(8,128)(2,1)} %copy-done.1, bf16[8,8,16,128]{3,2,1,0:T(8,128)(2,1)} %copy-done.11, bf16[8,8,16,128]{3,2,1,0:T(8,128)(2,1)} %collective-permute-done.4.refs_2_, bf16[8,8,16,128]{3,2,1,0:T(8,128)(2,1)} %collective-permute-done.2.refs_3_, ...), custom_call_target="tpu_custom_call" | custom-call | tf_op jit(solution)/shard_map/move/pallas_call | solution.py:273
  68.5 11.1 %all-to-all-start = ((bf16[384,16,128]{2,1,0:T(8,128)(2,1)}), bf16[384,16,128]{2,1,0:T(8,128)(2,1)}, u32[]{:S(2)}, u32[]{:S(2)}) async-start(bf16[384,16,128]{2,1,0:T(8,128)(2,1)} %bitcast.4), calls=%async_computation | async-start | bytes 3145728 | tf_op jit(solution)/shard_map/all_to_all | solution.py:62
  81.6 2.9 %collective-permute-done.5.refs_1_ = bf16[16,8,16,128]{3,2,1,0:T(8,128)(2,1)S(1)} collective-permute-done((bf16[16,8,16,128]{3,2,1,0:T(8,128)(2,1)S(1)}, bf16[16,8,16,128]{3,2,1,0:T(8,128)(2,1)S(1)}, u32[]{:S(2)}, u32[]{:S(2)}) %collective-permute-start.5) | collective-permute-done | bytes 524320 | tf_op jit(solution)/shard_map/ppermute | solution.py:53
  84.5 2.9 %collective-permute-done.6.refs_2_ = bf16[16,8,16,128]{3,2,1,0:T(8,128)(2,1)S(1)} collective-permute-done((bf16[16,8,16,128]{3,2,1,0:T(8,128)(2,1)S(1)}, bf16[16,8,16,128]{3,2,1,0:T(8,128)(2,1)S(1)}, u32[]{:S(2)}, u32[]{:S(2)}) %collective-permute-start.6) | collective-permute-done | bytes 524320 | tf_op jit(solution)/shard_map/ppermute | solution.py:53
  90.1 12.3 %collective-permute-done.9.refs_4_ = bf16[8,8,16,128]{3,2,1,0:T(8,128)(2,1)S(1)} collective-permute-done((bf16[8,8,16,128]{3,2,1,0:T(8,128)(2,1)S(1)}, bf16[8,8,16,128]{3,2,1,0:T(8,128)(2,1)S(1)}, u32[]{:S(2)}, u32[]{:S(2)}) %collective-permute-start.9) | collective-permute-done | bytes 262176 | tf_op jit(solution)/shard_map/ppermute | solution.py:53
  102.4 2.2 %collective-permute-done.10.refs_4_ = bf16[8,8,16,128]{3,2,1,0:T(8,128)(2,1)S(1)} collective-permute-done((bf16[8,8,16,128]{3,2,1,0:T(8,128)(2,1)S(1)}, bf16[8,8,16,128]{3,2,1,0:T(8,128)(2,1)S(1)}, u32[]{:S(2)}, u32[]{:S(2)}) %collective-permute-start.10) | collective-permute-done | bytes 262176 | tf_op jit(solution)/shard_map/ppermute | solution.py:53
  104.6 2.4 %collective-permute-start.12 = (bf16[8,8,16,128]{3,2,1,0:T(8,128)(2,1)S(1)}, bf16[8,8,16,128]{3,2,1,0:T(8,128)(2,1)S(1)}, u32[]{:S(2)}, u32[]{:S(2)}) collective-permute-start(bf16[8,8,16,128]{3,2,1,0:T(8,128)(2,1)S(1)} %pad_maximum_fusion.3), channel_id=1, source_target_pairs={{0,64},{1,65},{2,66},{3,67},{4,68},{5,69},{6,70},{7,71},{16,80},{1... | collective-permute-start | bytes 786440 | tf_op jit(solution)/shard_map/ppermute | solution.py:53
  107.1 2.6 %correlate.10 = bf16[256,1024]{1,0:T(8,128)(2,1)S(1)} custom-call(s32[2]{0:T(128)S(1)} %pad_add_fusion.2.where_ref, bf16[4,8,12,16,128]{4,3,2,1,0:T(8,128)(2,1)} %bitcast.5.refs_0_, bf16[16,8,16,128]{3,2,1,0:T(8,128)(2,1)} %copy-done.4, bf16[16,8,16,128]{3,2,1,0:T(8,128)(2,1)} %copy-done.5, bf16[8,8,16,128]{3,2,1,0:T(8,128)(2,1)} %collective-permute-done.8.refs_3_, ...), custom_call_target="tpu_custom_call" | custom-call | tf_op jit(solution)/shard_map/correlate/pallas_call | solution.py:332
  111.0 2.6 %correlate.11 = bf16[256,1024]{1,0:T(8,128)(2,1)S(1)} custom-call(s32[2]{0:T(128)S(1)} %pad_add_fusion.3.where_ref, bf16[4,8,12,16,128]{4,3,2,1,0:T(8,128)(2,1)} %bitcast.5.refs_0_, bf16[16,8,16,128]{3,2,1,0:T(8,128)(2,1)} %copy-done.4, bf16[16,8,16,128]{3,2,1,0:T(8,128)(2,1)} %copy-done.5, bf16[8,8,16,128]{3,2,1,0:T(8,128)(2,1)} %collective-permute-done.7.refs_3_, ...), custom_call_target="tpu_custom_call" | custom-call | tf_op jit(solution)/shard_map/correlate/pallas_call | solution.py:332
  115.7 2.6 %correlate.12 = bf16[256,1024]{1,0:T(8,128)(2,1)S(1)} custom-call(s32[2]{0:T(128)S(1)} %pad_add_fusion.2.where_ref, bf16[4,8,12,16,128]{4,3,2,1,0:T(8,128)(2,1)} %bitcast.5.refs_0_, bf16[16,8,16,128]{3,2,1,0:T(8,128)(2,1)} %copy-done.4, bf16[16,8,16,128]{3,2,1,0:T(8,128)(2,1)} %copy-done.5, bf16[8,8,16,128]{3,2,1,0:T(8,128)(2,1)} %collective-permute-done.8.refs_3_, ...), custom_call_target="tpu_custom_call" | custom-call | tf_op jit(solution)/shard_map/correlate/pallas_call | solution.py:332
  118.3 2.5 %collective-permute-start.15 = (bf16[256,1024]{1,0:T(8,128)(2,1)S(1)}, bf16[256,1024]{1,0:T(8,128)(2,1)S(1)}, u32[]{:S(2)}, u32[]{:S(2)}) collective-permute-start(bf16[256,1024]{1,0:T(8,128)(2,1)S(1)} %correlate.12), channel_id=1, source_target_pairs={{0,192},{1,193},{2,194},{3,195},{4,196},{5,197},{6,198},{7,199},{1... | collective-permute-start | bytes 1572872 | tf_op jit(solution)/shard_map/ppermute | solution.py:53
  120.8 2.6 %correlate.13 = bf16[256,1024]{1,0:T(8,128)(2,1)S(1)} custom-call(s32[2]{0:T(128)S(1)} %pad_add_fusion.3.where_ref, bf16[4,8,12,16,128]{4,3,2,1,0:T(8,128)(2,1)} %bitcast.5.refs_0_, bf16[16,8,16,128]{3,2,1,0:T(8,128)(2,1)} %copy-done.4, bf16[16,8,16,128]{3,2,1,0:T(8,128)(2,1)} %copy-done.5, bf16[8,8,16,128]{3,2,1,0:T(8,128)(2,1)} %collective-permute-done.7.refs_3_, ...), custom_call_target="tpu_custom_call" | custom-call | tf_op jit(solution)/shard_map/correlate/pallas_call | solution.py:332
  123.5 2.6 %correlate.8.refs_0_ = bf16[256,1024]{1,0:T(8,128)(2,1)S(1)} custom-call(s32[2]{0:T(128)S(1)} %pad_add_fusion.1.where_ref, bf16[4,8,12,16,128]{4,3,2,1,0:T(8,128)(2,1)} %bitcast.5.refs_0_, bf16[16,8,16,128]{3,2,1,0:T(8,128)(2,1)} %copy-done.4, bf16[16,8,16,128]{3,2,1,0:T(8,128)(2,1)} %copy-done.5, bf16[8,8,16,128]{3,2,1,0:T(8,128)(2,1)} %collective-permute-done.8.refs_3_, ...), custom_call_target="tpu_custom_call" | custom-call | tf_op jit(solution)/shard_map/correlate/pallas_call | solution.py:332
  126.1 2.6 %correlate.14.refs_6_ = bf16[256,1024]{1,0:T(8,128)(2,1)S(1)} custom-call(s32[2]{0:T(128)S(1)} %pad_add_fusion.1.where_ref, bf16[4,8,12,16,128]{4,3,2,1,0:T(8,128)(2,1)} %bitcast.5.refs_0_, bf16[16,8,16,128]{3,2,1,0:T(8,128)(2,1)} %copy-done.4, bf16[16,8,16,128]{3,2,1,0:T(8,128)(2,1)} %copy-done.5, bf16[8,8,16,128]{3,2,1,0:T(8,128)(2,1)} %collective-permute-done.7.refs_3_, ...), custom_call_target="tpu_custom_call" | custom-call | tf_op jit(solution)/shard_map/correlate/pallas_call | solution.py:332
  128.7 2.6 %correlate.9.refs_1_ = bf16[256,1024]{1,0:T(8,128)(2,1)S(1)} custom-call(s32[2]{0:T(128)S(1)} %pad_add_fusion.1.where_ref, bf16[4,8,12,16,128]{4,3,2,1,0:T(8,128)(2,1)} %bitcast.5.refs_0_, bf16[16,8,16,128]{3,2,1,0:T(8,128)(2,1)} %copy-done.4, bf16[16,8,16,128]{3,2,1,0:T(8,128)(2,1)} %copy-done.5, bf16[8,8,16,128]{3,2,1,0:T(8,128)(2,1)} %collective-permute-done.8.refs_3_, ...), custom_call_target="tpu_custom_call" | custom-call | tf_op jit(solution)/shard_map/correlate/pallas_call | solution.py:332
  131.2 2.6 %correlate.15.refs_7_ = bf16[256,1024]{1,0:T(8,128)(2,1)S(1)} custom-call(s32[2]{0:T(128)S(1)} %pad_add_fusion.1.where_ref, bf16[4,8,12,16,128]{4,3,2,1,0:T(8,128)(2,1)} %bitcast.5.refs_0_, bf16[16,8,16,128]{3,2,1,0:T(8,128)(2,1)} %copy-done.4, bf16[16,8,16,128]{3,2,1,0:T(8,128)(2,1)} %copy-done.5, bf16[8,8,16,128]{3,2,1,0:T(8,128)(2,1)} %collective-permute-done.7.refs_3_, ...), custom_call_target="tpu_custom_call" | custom-call | tf_op jit(solution)/shard_map/correlate/pallas_call | solution.py:332
  133.8 9.8 %collective-permute-done.14.refs_4_ = bf16[256,1024]{1,0:T(8,128)(2,1)S(1)} collective-permute-done((bf16[256,1024]{1,0:T(8,128)(2,1)S(1)}, bf16[256,1024]{1,0:T(8,128)(2,1)S(1)}, u32[]{:S(2)}, u32[]{:S(2)}) %collective-permute-start.14) | collective-permute-done | bytes 524320 | tf_op jit(solution)/shard_map/ppermute | solution.py:53
  143.6 22.5 %collective-permute-done.16.refs_5_ = bf16[256,1024]{1,0:T(8,128)(2,1)S(1)} collective-permute-done((bf16[256,1024]{1,0:T(8,128)(2,1)S(1)}, bf16[256,1024]{1,0:T(8,128)(2,1)S(1)}, u32[]{:S(2)}, u32[]{:S(2)}) %collective-permute-start.16) | collective-permute-done | bytes 524320 | tf_op jit(solution)/shard_map/ppermute | solution.py:53
  166.2 3.9 %gather_planes.1 = bf16[256,8,1024]{2,1,0:T(8,128)(2,1)} custom-call(s32[1]{0:T(128)} %bitcast.position_ref, bf16[256,1024]{1,0:T(8,128)(2,1)S(1)} %correlate.8.refs_0_, bf16[256,1024]{1,0:T(8,128)(2,1)S(1)} %correlate.9.refs_1_, bf16[256,1024]{1,0:T(8,128)(2,1)S(1)} %collective-permute-done.13.refs_2_, ...), custom_call_target="tpu_custom_call" | custom-call | tf_op jit(solution)/shard_map/gather_planes/pallas_call | solution.py:364
  (69 shorter events, 18.7 us)
Async XLA Ops:
  0.0 0.8 copy-start.2
  1.8 7.1 %copy-start.3 = (f32[4,2048]{1,0:T(4,128)S(1)}, f32[4,2048]{1,0:T(4,128)}, u32[]{:S(2)}) copy-start(f32[4,2048]{1,0:T(4,128)} %w_ref.2) | copy-start | bytes 98308
  1.8 15.7 %collective-permute-start = (bf16[48,2048]{1,0:T(8,128)(2,1)S(1)}, bf16[48,2048]{1,0:T(8,128)(2,1)S(1)}, u32[]{:S(2)}, u32[]{:S(2)}) collective-permute-start(bf16[48,2048]{1,0:T(8,128)(2,1)S(1)} %carry.1), channel_id=1, source_target_pairs={{0,64},{1,65},{2,66},{3,67},{4,68},{5,69},{6,70},{7,71},{16,80},{1... | collective-permute-start | bytes 589832 | tf_op jit(solution)/shard_map/ppermute | solution.py:53
  21.6 44.2 %copy-start = (bf16[8,8,16,128]{3,2,1,0:T(8,128)(2,1)}, bf16[8,8,16,128]{3,2,1,0:T(8,128)(2,1)S(1)}, u32[]{:S(2)}) copy-start(bf16[8,8,16,128]{3,2,1,0:T(8,128)(2,1)S(1)} %get-tuple-element.48.refs_4_) | copy-start | bytes 786436
  21.6 44.2 %copy-start.1 = (bf16[8,8,16,128]{3,2,1,0:T(8,128)(2,1)}, bf16[8,8,16,128]{3,2,1,0:T(8,128)(2,1)S(1)}, u32[]{:S(2)}) copy-start(bf16[8,8,16,128]{3,2,1,0:T(8,128)(2,1)S(1)} %get-tuple-element.47.refs_0_) | copy-start | bytes 786436
  21.6 27.1 %all-to-all-start.1 = ((bf16[320,16,128]{2,1,0:T(8,128)(2,1)}), bf16[320,16,128]{2,1,0:T(8,128)(2,1)S(1)}, u32[]{:S(2)}, u32[]{:S(2)}) async-start(bf16[320,16,128]{2,1,0:T(8,128)(2,1)} %bitcast.6), calls=%async_computation.1 | async-start | bytes 2621440 | tf_op jit(solution)/shard_map/all_to_all | solution.py:62
  29.6 25.0 %collective-permute-start.1 = (bf16[8,8,16,128]{3,2,1,0:T(8,128)(2,1)S(1)}, bf16[8,8,16,128]{3,2,1,0:T(8,128)(2,1)S(1)}, u32[]{:S(2)}, u32[]{:S(2)}) collective-permute-start(bf16[8,8,16,128]{3,2,1,0:T(8,128)(2,1)S(1)} %get-tuple-element.48.refs_4_), channel_id=1, source_target_pairs={{0,192},{1,193},{2,194},{3,195},{4,196},{5,197},{6,198},{7,199},{1... | collective-permute-start | bytes 786440 | tf_op jit(solution)/shard_map/ppermute | solution.py:53
  32.5 23.6 %collective-permute-start.2 = (bf16[8,8,16,128]{3,2,1,0:T(8,128)(2,1)S(1)}, bf16[8,8,16,128]{3,2,1,0:T(8,128)(2,1)}, u32[]{:S(2)}, u32[]{:S(2)}) collective-permute-start(bf16[8,8,16,128]{3,2,1,0:T(8,128)(2,1)S(1)} %get-tuple-element.47.refs_0_), channel_id=1, source_target_pairs={{0,64},{1,65},{2,66},{3,67},{4,68},{5,69},{6,70},{7,71},{16,80},{1... | collective-permute-start | bytes 786440 | tf_op jit(solution)/shard_map/ppermute | solution.py:53
  34.0 27.8 %collective-permute-start.3 = (bf16[8,8,16,128]{3,2,1,0:T(8,128)(2,1)S(1)}, bf16[8,8,16,128]{3,2,1,0:T(8,128)(2,1)}, u32[]{:S(2)}, u32[]{:S(2)}) collective-permute-start(bf16[8,8,16,128]{3,2,1,0:T(8,128)(2,1)S(1)} %get-tuple-element.50), channel_id=1, source_target_pairs={{0,136},{1,137},{2,138},{3,139},{4,140},{5,141},{6,142},{7,143},{1... | collective-permute-start | bytes 786440 | tf_op jit(solution)/shard_map/ppermute | solution.py:53
  36.8 29.0 %collective-permute-start.4 = (bf16[8,8,16,128]{3,2,1,0:T(8,128)(2,1)S(1)}, bf16[8,8,16,128]{3,2,1,0:T(8,128)(2,1)}, u32[]{:S(2)}, u32[]{:S(2)}) collective-permute-start(bf16[8,8,16,128]{3,2,1,0:T(8,128)(2,1)S(1)} %get-tuple-element.50), channel_id=1, source_target_pairs={{0,72},{1,73},{2,74},{3,75},{4,76},{5,77},{6,78},{7,79},{16,88},{1... | collective-permute-start | bytes 786440 | tf_op jit(solution)/shard_map/ppermute | solution.py:53
  48.7 1.1 copy-start.6
  51.4 28.2 %collective-permute-start.7 = (bf16[8,8,16,128]{3,2,1,0:T(8,128)(2,1)S(1)}, bf16[8,8,16,128]{3,2,1,0:T(8,128)(2,1)}, u32[]{:S(2)}, u32[]{:S(2)}) collective-permute-start(bf16[8,8,16,128]{3,2,1,0:T(8,128)(2,1)S(1)} %get-tuple-element.59), channel_id=1, source_target_pairs={{0,192},{1,193},{2,194},{3,195},{4,196},{5,197},{6,198},{7,199},{1... | collective-permute-start | bytes 786440 | tf_op jit(solution)/shard_map/ppermute | solution.py:53
  54.6 7.2 %copy-start.11 = (bf16[8,8,16,128]{3,2,1,0:T(8,128)(2,1)}, bf16[8,8,16,128]{3,2,1,0:T(8,128)(2,1)S(1)}, u32[]{:S(2)}) copy-start(bf16[8,8,16,128]{3,2,1,0:T(8,128)(2,1)S(1)} %collective-permute-done.1.refs_1_) | copy-start | bytes 786436
  54.6 25.0 %collective-permute-start.8 = (bf16[8,8,16,128]{3,2,1,0:T(8,128)(2,1)S(1)}, bf16[8,8,16,128]{3,2,1,0:T(8,128)(2,1)}, u32[]{:S(2)}, u32[]{:S(2)}) collective-permute-start(bf16[8,8,16,128]{3,2,1,0:T(8,128)(2,1)S(1)} %get-tuple-element.60), channel_id=1, source_target_pairs={{0,64},{1,65},{2,66},{3,67},{4,68},{5,69},{6,70},{7,71},{16,80},{1... | collective-permute-start | bytes 786440 | tf_op jit(solution)/shard_map/ppermute | solution.py:53
  56.2 28.4 %collective-permute-start.5 = (bf16[16,8,16,128]{3,2,1,0:T(8,128)(2,1)S(1)}, bf16[16,8,16,128]{3,2,1,0:T(8,128)(2,1)S(1)}, u32[]{:S(2)}, u32[]{:S(2)}) collective-permute-start(bf16[16,8,16,128]{3,2,1,0:T(8,128)(2,1)S(1)} %get-tuple-element.55), channel_id=1, source_target_pairs={{0,200},{1,201},{2,202},{3,203},{4,204},{5,205},{6,206},{7,207},{1... | collective-permute-start | bytes 1572872 | tf_op jit(solution)/shard_map/ppermute | solution.py:53
  61.9 25.5 %collective-permute-start.6 = (bf16[16,8,16,128]{3,2,1,0:T(8,128)(2,1)S(1)}, bf16[16,8,16,128]{3,2,1,0:T(8,128)(2,1)S(1)}, u32[]{:S(2)}, u32[]{:S(2)}) collective-permute-start(bf16[16,8,16,128]{3,2,1,0:T(8,128)(2,1)S(1)} %get-tuple-element.56), channel_id=1, source_target_pairs={{0,8},{1,9},{2,10},{3,11},{4,12},{5,13},{6,14},{7,15},{16,24},{17,... | collective-permute-start | bytes 1572872 | tf_op jit(solution)/shard_map/ppermute | solution.py:53
  68.5 38.6 %all-to-all-start = ((bf16[384,16,128]{2,1,0:T(8,128)(2,1)}), bf16[384,16,128]{2,1,0:T(8,128)(2,1)}, u32[]{:S(2)}, u32[]{:S(2)}) async-start(bf16[384,16,128]{2,1,0:T(8,128)(2,1)} %bitcast.4), calls=%async_computation | async-start | bytes 3145728 | tf_op jit(solution)/shard_map/all_to_all | solution.py:62
  84.5 22.6 %copy-start.4 = (bf16[16,8,16,128]{3,2,1,0:T(8,128)(2,1)}, bf16[16,8,16,128]{3,2,1,0:T(8,128)(2,1)S(1)}, u32[]{:S(2)}) copy-start(bf16[16,8,16,128]{3,2,1,0:T(8,128)(2,1)S(1)} %collective-permute-done.5.refs_1_) | copy-start | bytes 1572868
  87.4 19.7 %copy-start.5 = (bf16[16,8,16,128]{3,2,1,0:T(8,128)(2,1)}, bf16[16,8,16,128]{3,2,1,0:T(8,128)(2,1)S(1)}, u32[]{:S(2)}) copy-start(bf16[16,8,16,128]{3,2,1,0:T(8,128)(2,1)S(1)} %collective-permute-done.6.refs_2_) | copy-start | bytes 1572868
  87.4 14.9 %collective-permute-start.9 = (bf16[8,8,16,128]{3,2,1,0:T(8,128)(2,1)S(1)}, bf16[8,8,16,128]{3,2,1,0:T(8,128)(2,1)S(1)}, u32[]{:S(2)}, u32[]{:S(2)}) collective-permute-start(bf16[8,8,16,128]{3,2,1,0:T(8,128)(2,1)S(1)} %pad_maximum_fusion), channel_id=1, source_target_pairs={{0,192},{1,193},{2,194},{3,195},{4,196},{5,197},{6,198},{7,199},{1... | collective-permute-start | bytes 786440 | tf_op jit(solution)/shard_map/ppermute | solution.py:53
  88.6 16.0 %collective-permute-start.10 = (bf16[8,8,16,128]{3,2,1,0:T(8,128)(2,1)S(1)}, bf16[8,8,16,128]{3,2,1,0:T(8,128)(2,1)S(1)}, u32[]{:S(2)}, u32[]{:S(2)}) collective-permute-start(bf16[8,8,16,128]{3,2,1,0:T(8,128)(2,1)S(1)} %pad_maximum_fusion.1), channel_id=1, source_target_pairs={{0,64},{1,65},{2,66},{3,67},{4,68},{5,69},{6,70},{7,71},{16,80},{1... | collective-permute-start | bytes 786440 | tf_op jit(solution)/shard_map/ppermute | solution.py:53
  102.4 4.7 %copy-start.7 = (bf16[8,8,16,128]{3,2,1,0:T(8,128)(2,1)}, bf16[8,8,16,128]{3,2,1,0:T(8,128)(2,1)S(1)}, u32[]{:S(2)}) copy-start(bf16[8,8,16,128]{3,2,1,0:T(8,128)(2,1)S(1)} %collective-permute-done.9.refs_4_) | copy-start | bytes 786436
  104.6 6.4 %copy-start.8 = (bf16[8,8,16,128]{3,2,1,0:T(8,128)(2,1)}, bf16[8,8,16,128]{3,2,1,0:T(8,128)(2,1)S(1)}, u32[]{:S(2)}) copy-start(bf16[8,8,16,128]{3,2,1,0:T(8,128)(2,1)S(1)} %collective-permute-done.10.refs_4_) | copy-start | bytes 786436
  104.6 10.4 %collective-permute-start.11 = (bf16[8,8,16,128]{3,2,1,0:T(8,128)(2,1)S(1)}, bf16[8,8,16,128]{3,2,1,0:T(8,128)(2,1)S(1)}, u32[]{:S(2)}, u32[]{:S(2)}) collective-permute-start(bf16[8,8,16,128]{3,2,1,0:T(8,128)(2,1)S(1)} %pad_maximum_fusion.2), channel_id=1, source_target_pairs={{0,192},{1,193},{2,194},{3,195},{4,196},{5,197},{6,198},{7,199},{1... | collective-permute-start | bytes 786440 | tf_op jit(solution)/shard_map/ppermute | solution.py:53
  104.6 10.4 %collective-permute-start.12 = (bf16[8,8,16,128]{3,2,1,0:T(8,128)(2,1)S(1)}, bf16[8,8,16,128]{3,2,1,0:T(8,128)(2,1)S(1)}, u32[]{:S(2)}, u32[]{:S(2)}) collective-permute-start(bf16[8,8,16,128]{3,2,1,0:T(8,128)(2,1)S(1)} %pad_maximum_fusion.3), channel_id=1, source_target_pairs={{0,64},{1,65},{2,66},{3,67},{4,68},{5,69},{6,70},{7,71},{16,80},{1... | collective-permute-start | bytes 786440 | tf_op jit(solution)/shard_map/ppermute | solution.py:53
  109.7 24.1 %collective-permute-start.13 = (bf16[256,1024]{1,0:T(8,128)(2,1)S(1)}, bf16[256,1024]{1,0:T(8,128)(2,1)S(1)}, u32[]{:S(2)}, u32[]{:S(2)}) collective-permute-start(bf16[256,1024]{1,0:T(8,128)(2,1)S(1)} %correlate.10), channel_id=1, source_target_pairs={{0,192},{1,193},{2,194},{3,195},{4,196},{5,197},{6,198},{7,199},{1... | collective-permute-start | bytes 1572872 | tf_op jit(solution)/shard_map/ppermute | solution.py:53
  113.5 30.1 %collective-permute-start.14 = (bf16[256,1024]{1,0:T(8,128)(2,1)S(1)}, bf16[256,1024]{1,0:T(8,128)(2,1)S(1)}, u32[]{:S(2)}, u32[]{:S(2)}) collective-permute-start(bf16[256,1024]{1,0:T(8,128)(2,1)S(1)} %correlate.11), channel_id=1, source_target_pairs={{0,64},{1,65},{2,66},{3,67},{4,68},{5,69},{6,70},{7,71},{16,80},{1... | collective-permute-start | bytes 1572872 | tf_op jit(solution)/shard_map/ppermute | solution.py:53
  115.0 0.7 copy-start.10
  115.7 5.1 %copy-start.9 = (bf16[8,8,16,128]{3,2,1,0:T(8,128)(2,1)}, bf16[8,8,16,128]{3,2,1,0:T(8,128)(2,1)S(1)}, u32[]{:S(2)}) copy-start(bf16[8,8,16,128]{3,2,1,0:T(8,128)(2,1)S(1)} %collective-permute-done.12.refs_4_) | copy-start | bytes 786436
  118.3 25.3 %collective-permute-start.15 = (bf16[256,1024]{1,0:T(8,128)(2,1)S(1)}, bf16[256,1024]{1,0:T(8,128)(2,1)S(1)}, u32[]{:S(2)}, u32[]{:S(2)}) collective-permute-start(bf16[256,1024]{1,0:T(8,128)(2,1)S(1)} %correlate.12), channel_id=1, source_target_pairs={{0,192},{1,193},{2,194},{3,195},{4,196},{5,197},{6,198},{7,199},{1... | collective-permute-start | bytes 1572872 | tf_op jit(solution)/shard_map/ppermute | solution.py:53
  123.4 42.8 %collective-permute-start.16 = (bf16[256,1024]{1,0:T(8,128)(2,1)S(1)}, bf16[256,1024]{1,0:T(8,128)(2,1)S(1)}, u32[]{:S(2)}, u32[]{:S(2)}) collective-permute-start(bf16[256,1024]{1,0:T(8,128)(2,1)S(1)} %correlate.13), channel_id=1, source_target_pairs={{0,64},{1,65},{2,66},{3,67},{4,68},{5,69},{6,70},{7,71},{16,80},{1... | collective-permute-start | bytes 1572872 | tf_op jit(solution)/shard_map/ppermute | solution.py:53

commit v4 on v3

--- a/solution.py
+++ b/solution.py
@@ -376,8 +376,8 @@
 
 def places(which):
     at, early = 4 * which, 6 * which
-    here = [(0, early), (1, 8 + at), (0, early + 1), (5, 0), (5, 4), (0, early + 2), (4, at), (2, at)]
-    there = [(0, early + 3), (2, 8 + at), (0, early + 4), (1, at), (3, at), (0, early + 5), (6, 4), (6, 0)]
+    here = [(0, early), (7, at), (0, early + 1), (5, 0), (5, 4), (0, early + 2), (4, at), (2, at)]
+    there = [(0, early + 3), (8, at), (0, early + 4), (1, at), (3, at), (0, early + 5), (6, 4), (6, 0)]
     return [[[(*place, 0, 4)] for place in side] for side in (here, there)]
 
 
@@ -413,8 +413,8 @@
         ],
     )
     packed = turn(packed.reshape(-1, INP, PIECE)).reshape(packed.shape)
-    sent = ((3, 1), (7, 1), (4,), (6,))
-    sent_31, sent_71, sent_4, sent_6 = move(
+    sent = ((3,), (7,), (4,), (6,), (1,))
+    sent_3, sent_7, sent_4, sent_6, sent_1 = move(
         [turned],
         [(8 * len(deltas), *BLOCK[1:]) for deltas in sent],
         [
@@ -424,8 +424,10 @@
             for which in range(2)
         ],
     )
-    left_31, right_71 = both_ways(sent_31, sent_71, 1)
+    left_31, right_71 = both_ways(sent_3, sent_7, 1)
     left_4, right_6 = both_ways(sent_4, sent_6, 2)
+    sent_1, left_4, right_6 = lax.optimization_barrier((sent_1, left_4, right_6))
+    ones = both_ways(sent_1, sent_1, 1)
 
     def onward(which):
         part = slice(4 * which, 4 * which + 4)
@@ -439,7 +441,7 @@
     far_1 = both_ways(*onward_1, 2)
     for which, far in enumerate((far_0, far_1)):
         here, there = places(which)
-        arrays = [packed, left_31, right_71, left_4, right_6, *far]
+        arrays = [packed, left_31, right_71, left_4, right_6, *far, *ones]
         planes[2 + which], planes[4 + which] = both_ways(
             correlate(before, z_lo, here, arrays), correlate(after, z_lo, there, arrays), 2
         )

time: 171 us -> 165 us (0.965); the launches traced: 170 us -> 162 us
  waiting for transfers between devices: 68.9 us -> 60.7 us
  local copies, waits for them, and re-layouts: 4.72 us -> 2.8 us
    ppermute x17 -> x19, waiting for transfers between devices: 58.2 us -> 49.9 us  [along_z(): return lax.ppermute(x, ('tm', 'feed'), pairs)]
    ppermute x17 -> x19, starting transfers between devices: 31.3 us -> 32.5 us  [along_z(): return lax.ppermute(x, ('tm', 'feed'), pairs)]
  transfers between devices with their start and end apart: 19 -> 21, of which waited for: 9 -> 10; matrix products, arithmetic and copies ran while one was open for 2% -> 1% of each run, Pallas kernels for 20% -> 21%
where the time goes in v4:
time: 165 us; the launch traced here: 162 us
  waiting for transfers between devices  60.7 us (37%)
  starting transfers between devices  51.7 us (31%)
  Pallas kernels  43.5 us (26%)
  local copies, waits for them, and re-layouts  2.8 us (2%)
  other arithmetic  2.09 us (1%)
    ppermute x19, waiting for transfers between devices, along_z(): return lax.ppermute(x, ('tm', 'feed'), pairs)  49.9 us
    ppermute x19, starting transfers between devices, along_z(): return lax.ppermute(x, ('tm', 'feed'), pairs)  32.5 us
    pallas_call x8, Pallas kernels, correlate(): pl.pallas_call(functools.partial(correlate_kernel, layout), in_specs=[pl....  20.5 us
    all_to_all x2, starting transfers between devices, turn(): lax.all_to_all(x, 'feed', split_axis=0, concat_axis=0, tiled=True, axis_i...  19.2 us
    all_to_all x2, waiting for transfers between devices, turn(): lax.all_to_all(x, 'feed', split_axis=0, concat_axis=0, tiled=True, axis_i...  10.8 us
    pallas_call x1, Pallas kernels, product(): pl.pallas_call(product_kernel, in_specs=[vmem] * 2, out_specs=vmem, out_s...  4.5 us
    pallas_call x1, Pallas kernels, filter_own(): pl.pallas_call(filter_kernel, in_specs=[pl.BlockSpec(memory_space=pltpu.H...  4.15 us
    pallas_call x2, Pallas kernels, move(): pl.pallas_call(functools.partial(move_kernel, moves, len(arrays)), in_spe...  4.15 us
  transfers between devices with their start and end apart: 21, of which 10 were waited for; matrix products, arithmetic and copies ran while one was open for 1% of the time, Pallas kernels for 21%

profile of v4, /device:TPU:1, one launch (start us, length us, event | category | flops | bytes accessed | tf_op | source)
XLA Modules:
  0.0 161.7 jit_solution(10075483487006155611)
XLA Ops:
  1.8 3.9 %collective-permute-start = (bf16[48,2048]{1,0:T(8,128)(2,1)S(1)}, bf16[48,2048]{1,0:T(8,128)(2,1)S(1)}, u32[]{:S(2)}, u32[]{:S(2)}) collective-permute-start(bf16[48,2048]{1,0:T(8,128)(2,1)S(1)} %carry.1), channel_id=1, source_target_pairs={{0,64},{1,65},{2,66},{3,67},{4,68},{5,69},{6,70},{7,71},{16,80},{1... | collective-permute-start | bytes 589832 | tf_op jit(solution)/shard_map/ppermute | solution.py:53
  8.9 4.1 %own_filter.1 = (bf16[1024,2048]{1,0:T(8,128)(2,1)S(1)}, f32[48,2048]{1,0:T(8,128)S(1)}) custom-call(s32[16,131072]{1,0:T(8,128)} %v_ref.3, f32[4,2048]{1,0:T(4,128)S(1)} %copy-done.3), custom_call_target="tpu_custom_call" | custom-call | tf_op jit(solution)/shard_map/own_filter/pallas_call | solution.py:142
  13.1 4.5 %product.1.wide = f32[4,2,1024,128]{3,2,1,0:T(8,128)S(1)} custom-call(bf16[1024,2048]{1,0:T(8,128)(2,1)S(1)} %get-tuple-element.49.f_ref, bf16[4,2048,256]{2,1,0:T(8,128)(2,1)S(1)} %dft_table.1.t_ref), custom_call_target="tpu_custom_call" | custom-call | tf_op jit(solution)/shard_map/product/pallas_call | solution.py:208
  17.6 4.0 %dft.1 = (bf16[40,8,16,128]{3,2,1,0:T(8,128)(2,1)}, bf16[8,8,16,128]{3,2,1,0:T(8,128)(2,1)S(1)}, bf16[8,8,16,128]{3,2,1,0:T(8,128)(2,1)S(1)}, bf16[8,8,16,128]{3,2,1,0:T(8,128)(2,1)S(1)}) custom-call(s32[1]{0:T(128)} %bitcast.position_ref, f32[4,2,1024,128]{3,2,1,0:T(8,128)S(1)} %product.1.wide, f32[48,2048]{1,0:T(8,128)S(1)} %get-tuple-element.51.head_ref, ...), custom_call_target="tpu_custom_call" | custom-call | tf_op jit(solution)/shard_map/dft/pallas_call | solution.py:246
  21.6 8.0 %all-to-all-start.1 = ((bf16[320,16,128]{2,1,0:T(8,128)(2,1)}), bf16[320,16,128]{2,1,0:T(8,128)(2,1)S(1)}, u32[]{:S(2)}, u32[]{:S(2)}) async-start(bf16[320,16,128]{2,1,0:T(8,128)(2,1)} %bitcast.6), calls=%async_computation.1 | async-start | bytes 2621440 | tf_op jit(solution)/shard_map/all_to_all | solution.py:62
  29.6 2.9 %collective-permute-start.1 = (bf16[8,8,16,128]{3,2,1,0:T(8,128)(2,1)S(1)}, bf16[8,8,16,128]{3,2,1,0:T(8,128)(2,1)}, u32[]{:S(2)}, u32[]{:S(2)}) collective-permute-start(bf16[8,8,16,128]{3,2,1,0:T(8,128)(2,1)S(1)} %get-tuple-element.54.refs_4_), channel_id=1, source_target_pairs={{0,192},{1,193},{2,194},{3,195},{4,196},{5,197},{6,198},{7,199},{1... | collective-permute-start | bytes 786440 | tf_op jit(solution)/shard_map/ppermute | solution.py:53
  34.0 2.8 %collective-permute-start.3 = (bf16[8,8,16,128]{3,2,1,0:T(8,128)(2,1)S(1)}, bf16[8,8,16,128]{3,2,1,0:T(8,128)(2,1)}, u32[]{:S(2)}, u32[]{:S(2)}) collective-permute-start(bf16[8,8,16,128]{3,2,1,0:T(8,128)(2,1)S(1)} %get-tuple-element.56), channel_id=1, source_target_pairs={{0,136},{1,137},{2,138},{3,139},{4,140},{5,141},{6,142},{7,143},{1... | collective-permute-start | bytes 786440 | tf_op jit(solution)/shard_map/ppermute | solution.py:53
  38.0 10.8 %all-to-all-done.1 = bf16[320,16,128]{2,1,0:T(8,128)(2,1)S(1)} async-done(((bf16[320,16,128]{2,1,0:T(8,128)(2,1)}), bf16[320,16,128]{2,1,0:T(8,128)(2,1)S(1)}, u32[]{:S(2)}, u32[]{:S(2)}) %all-to-all-start.1) | async-done | bytes 1310752 | tf_op jit(solution)/shard_map/all_to_all | solution.py:62
  51.3 3.3 %collective-permute-start.7 = (bf16[8,8,16,128]{3,2,1,0:T(8,128)(2,1)S(1)}, bf16[8,8,16,128]{3,2,1,0:T(8,128)(2,1)S(1)}, u32[]{:S(2)}, u32[]{:S(2)}) collective-permute-start(bf16[8,8,16,128]{3,2,1,0:T(8,128)(2,1)S(1)} %get-tuple-element.65), channel_id=1, source_target_pairs={{0,192},{1,193},{2,194},{3,195},{4,196},{5,197},{6,198},{7,199},{1... | collective-permute-start | bytes 786440 | tf_op jit(solution)/shard_map/ppermute | solution.py:53
  54.5 1.5 collective-permute-start.8
  57.3 4.6 %collective-permute-done.3.refs_5_ = bf16[8,8,16,128]{3,2,1,0:T(8,128)(2,1)} collective-permute-done((bf16[8,8,16,128]{3,2,1,0:T(8,128)(2,1)S(1)}, bf16[8,8,16,128]{3,2,1,0:T(8,128)(2,1)}, u32[]{:S(2)}, u32[]{:S(2)}) %collective-permute-start.3) | collective-permute-done | bytes 262176 | tf_op jit(solution)/shard_map/ppermute | solution.py:53
  61.9 2.9 %collective-permute-start.6 = (bf16[8,8,16,128]{3,2,1,0:T(8,128)(2,1)S(1)}, bf16[8,8,16,128]{3,2,1,0:T(8,128)(2,1)S(1)}, u32[]{:S(2)}, u32[]{:S(2)}) collective-permute-start(bf16[8,8,16,128]{3,2,1,0:T(8,128)(2,1)S(1)} %get-tuple-element.62), channel_id=1, source_target_pairs={{0,8},{1,9},{2,10},{3,11},{4,12},{5,13},{6,14},{7,15},{16,24},{17,... | collective-permute-start | bytes 786440 | tf_op jit(solution)/shard_map/ppermute | solution.py:53
  65.7 2.7 %move.2 = bf16[4,8,12,16,128]{4,3,2,1,0:T(8,128)(2,1)} custom-call(bf16[8,8,16,128]{3,2,1,0:T(8,128)(2,1)} %copy-done.1, bf16[8,8,16,128]{3,2,1,0:T(8,128)(2,1)} %collective-permute-done.1.refs_1_, bf16[8,8,16,128]{3,2,1,0:T(8,128)(2,1)} %collective-permute-done.4.refs_2_, bf16[8,8,16,128]{3,2,1,0:T(8,128)(2,1)} %collective-permute-done.2.refs_3_, ...), custom_call_target="tpu_custom_call" | custom-call | tf_op jit(solution)/shard_map/move/pallas_call | solution.py:273
  68.4 11.1 %all-to-all-start = ((bf16[384,16,128]{2,1,0:T(8,128)(2,1)}), bf16[384,16,128]{2,1,0:T(8,128)(2,1)}, u32[]{:S(2)}, u32[]{:S(2)}) async-start(bf16[384,16,128]{2,1,0:T(8,128)(2,1)} %bitcast.4), calls=%async_computation | async-start | bytes 3145728 | tf_op jit(solution)/shard_map/all_to_all | solution.py:62
  79.7 2.0 %collective-permute-done.6.refs_1_ = bf16[8,8,16,128]{3,2,1,0:T(8,128)(2,1)S(1)} collective-permute-done((bf16[8,8,16,128]{3,2,1,0:T(8,128)(2,1)S(1)}, bf16[8,8,16,128]{3,2,1,0:T(8,128)(2,1)S(1)}, u32[]{:S(2)}, u32[]{:S(2)}) %collective-permute-start.6) | collective-permute-done | bytes 262176 | tf_op jit(solution)/shard_map/ppermute | solution.py:53
  86.5 10.1 %collective-permute-done.9.refs_3_ = bf16[8,8,16,128]{3,2,1,0:T(8,128)(2,1)S(1)} collective-permute-done((bf16[8,8,16,128]{3,2,1,0:T(8,128)(2,1)S(1)}, bf16[8,8,16,128]{3,2,1,0:T(8,128)(2,1)S(1)}, u32[]{:S(2)}, u32[]{:S(2)}) %collective-permute-start.9) | collective-permute-done | bytes 262176 | tf_op jit(solution)/shard_map/ppermute | solution.py:53
  96.6 2.0 %collective-permute-done.10.refs_3_ = bf16[8,8,16,128]{3,2,1,0:T(8,128)(2,1)S(1)} collective-permute-done((bf16[8,8,16,128]{3,2,1,0:T(8,128)(2,1)S(1)}, bf16[8,8,16,128]{3,2,1,0:T(8,128)(2,1)S(1)}, u32[]{:S(2)}, u32[]{:S(2)}) %collective-permute-start.10) | collective-permute-done | bytes 262176 | tf_op jit(solution)/shard_map/ppermute | solution.py:53
  98.6 2.4 %collective-permute-start.14 = (bf16[8,8,16,128]{3,2,1,0:T(8,128)(2,1)}, bf16[8,8,16,128]{3,2,1,0:T(8,128)(2,1)S(1)}, u32[]{:S(2)}, u32[]{:S(2)}) collective-permute-start(bf16[8,8,16,128]{3,2,1,0:T(8,128)(2,1)} %pad_maximum_fusion.3), channel_id=1, source_target_pairs={{0,64},{1,65},{2,66},{3,67},{4,68},{5,69},{6,70},{7,71},{16,80},{1... | collective-permute-start | bytes 786440 | tf_op jit(solution)/shard_map/ppermute | solution.py:53
  102.4 2.6 %correlate.10 = bf16[256,1024]{1,0:T(8,128)(2,1)S(1)} custom-call(s32[2]{0:T(128)S(1)} %pad_add_fusion.2.where_ref, bf16[4,8,12,16,128]{4,3,2,1,0:T(8,128)(2,1)} %bitcast.5.refs_0_, bf16[8,8,16,128]{3,2,1,0:T(8,128)(2,1)} %copy-done.7, bf16[8,8,16,128]{3,2,1,0:T(8,128)(2,1)} %copy-done.5, bf16[8,8,16,128]{3,2,1,0:T(8,128)(2,1)} %copy-done.11, ...), custom_call_target="tpu_custom_call" | custom-call | tf_op jit(solution)/shard_map/correlate/pallas_call | solution.py:332
  105.0 1.9 %collective-permute-start.15 = (bf16[256,1024]{1,0:T(8,128)(2,1)S(1)}, bf16[256,1024]{1,0:T(8,128)(2,1)S(1)}, u32[]{:S(2)}, u32[]{:S(2)}) collective-permute-start(bf16[256,1024]{1,0:T(8,128)(2,1)S(1)} %correlate.10), channel_id=1, source_target_pairs={{0,192},{1,193},{2,194},{3,195},{4,196},{5,197},{6,198},{7,199},{1... | collective-permute-start | bytes 1572872 | tf_op jit(solution)/shard_map/ppermute | solution.py:53
  106.9 2.6 %correlate.11 = bf16[256,1024]{1,0:T(8,128)(2,1)S(1)} custom-call(s32[2]{0:T(128)S(1)} %pad_add_fusion.3.where_ref, bf16[4,8,12,16,128]{4,3,2,1,0:T(8,128)(2,1)} %bitcast.5.refs_0_, bf16[8,8,16,128]{3,2,1,0:T(8,128)(2,1)} %copy-done.6, bf16[8,8,16,128]{3,2,1,0:T(8,128)(2,1)} %copy-done.4, bf16[8,8,16,128]{3,2,1,0:T(8,128)(2,1)} %copy-done.12, ...), custom_call_target="tpu_custom_call" | custom-call | tf_op jit(solution)/shard_map/correlate/pallas_call | solution.py:332
  110.1 4.7 %collective-permute-done.13.refs_3_ = bf16[8,8,16,128]{3,2,1,0:T(8,128)(2,1)S(1)} collective-permute-done((bf16[8,8,16,128]{3,2,1,0:T(8,128)(2,1)S(1)}, bf16[8,8,16,128]{3,2,1,0:T(8,128)(2,1)S(1)}, u32[]{:S(2)}, u32[]{:S(2)}) %collective-permute-start.13) | collective-permute-done | bytes 262176 | tf_op jit(solution)/shard_map/ppermute | solution.py:53
  115.5 2.6 %correlate.12 = bf16[256,1024]{1,0:T(8,128)(2,1)S(1)} custom-call(s32[2]{0:T(128)S(1)} %pad_add_fusion.2.where_ref, bf16[4,8,12,16,128]{4,3,2,1,0:T(8,128)(2,1)} %bitcast.5.refs_0_, bf16[8,8,16,128]{3,2,1,0:T(8,128)(2,1)} %copy-done.7, bf16[8,8,16,128]{3,2,1,0:T(8,128)(2,1)} %copy-done.5, bf16[8,8,16,128]{3,2,1,0:T(8,128)(2,1)} %copy-done.14, ...), custom_call_target="tpu_custom_call" | custom-call | tf_op jit(solution)/shard_map/correlate/pallas_call | solution.py:332
  118.0 1.7 %collective-permute-start.17 = (bf16[256,1024]{1,0:T(8,128)(2,1)S(1)}, bf16[256,1024]{1,0:T(8,128)(2,1)S(1)}, u32[]{:S(2)}, u32[]{:S(2)}) collective-permute-start(bf16[256,1024]{1,0:T(8,128)(2,1)S(1)} %correlate.12), channel_id=1, source_target_pairs={{0,192},{1,193},{2,194},{3,195},{4,196},{5,197},{6,198},{7,199},{1... | collective-permute-start | bytes 1572872 | tf_op jit(solution)/shard_map/ppermute | solution.py:53
  119.8 2.6 %correlate.13 = bf16[256,1024]{1,0:T(8,128)(2,1)S(1)} custom-call(s32[2]{0:T(128)S(1)} %pad_add_fusion.3.where_ref, bf16[4,8,12,16,128]{4,3,2,1,0:T(8,128)(2,1)} %bitcast.5.refs_0_, bf16[8,8,16,128]{3,2,1,0:T(8,128)(2,1)} %copy-done.6, bf16[8,8,16,128]{3,2,1,0:T(8,128)(2,1)} %copy-done.4, bf16[8,8,16,128]{3,2,1,0:T(8,128)(2,1)} %copy-done.13, ...), custom_call_target="tpu_custom_call" | custom-call | tf_op jit(solution)/shard_map/correlate/pallas_call | solution.py:332
  123.2 2.6 %correlate.8.refs_0_ = bf16[256,1024]{1,0:T(8,128)(2,1)S(1)} custom-call(s32[2]{0:T(128)S(1)} %pad_add_fusion.1.where_ref, bf16[4,8,12,16,128]{4,3,2,1,0:T(8,128)(2,1)} %bitcast.5.refs_0_, bf16[8,8,16,128]{3,2,1,0:T(8,128)(2,1)} %copy-done.7, bf16[8,8,16,128]{3,2,1,0:T(8,128)(2,1)} %copy-done.5, bf16[8,8,16,128]{3,2,1,0:T(8,128)(2,1)} %copy-done.11, ...), custom_call_target="tpu_custom_call" | custom-call | tf_op jit(solution)/shard_map/correlate/pallas_call | solution.py:332
  125.8 2.6 %correlate.14.refs_6_ = bf16[256,1024]{1,0:T(8,128)(2,1)S(1)} custom-call(s32[2]{0:T(128)S(1)} %pad_add_fusion.1.where_ref, bf16[4,8,12,16,128]{4,3,2,1,0:T(8,128)(2,1)} %bitcast.5.refs_0_, bf16[8,8,16,128]{3,2,1,0:T(8,128)(2,1)} %copy-done.6, bf16[8,8,16,128]{3,2,1,0:T(8,128)(2,1)} %copy-done.4, bf16[8,8,16,128]{3,2,1,0:T(8,128)(2,1)} %copy-done.12, ...), custom_call_target="tpu_custom_call" | custom-call | tf_op jit(solution)/shard_map/correlate/pallas_call | solution.py:332
  128.4 2.6 %correlate.9.refs_1_ = bf16[256,1024]{1,0:T(8,128)(2,1)S(1)} custom-call(s32[2]{0:T(128)S(1)} %pad_add_fusion.1.where_ref, bf16[4,8,12,16,128]{4,3,2,1,0:T(8,128)(2,1)} %bitcast.5.refs_0_, bf16[8,8,16,128]{3,2,1,0:T(8,128)(2,1)} %copy-done.7, bf16[8,8,16,128]{3,2,1,0:T(8,128)(2,1)} %copy-done.5, bf16[8,8,16,128]{3,2,1,0:T(8,128)(2,1)} %copy-done.14, ...), custom_call_target="tpu_custom_call" | custom-call | tf_op jit(solution)/shard_map/correlate/pallas_call | solution.py:332
  130.9 2.6 %correlate.15.refs_7_ = bf16[256,1024]{1,0:T(8,128)(2,1)S(1)} custom-call(s32[2]{0:T(128)S(1)} %pad_add_fusion.1.where_ref, bf16[4,8,12,16,128]{4,3,2,1,0:T(8,128)(2,1)} %bitcast.5.refs_0_, bf16[8,8,16,128]{3,2,1,0:T(8,128)(2,1)} %copy-done.6, bf16[8,8,16,128]{3,2,1,0:T(8,128)(2,1)} %copy-done.4, bf16[8,8,16,128]{3,2,1,0:T(8,128)(2,1)} %copy-done.13, ...), custom_call_target="tpu_custom_call" | custom-call | tf_op jit(solution)/shard_map/correlate/pallas_call | solution.py:332
  133.5 8.6 %collective-permute-done.15.refs_2_ = bf16[256,1024]{1,0:T(8,128)(2,1)S(1)} collective-permute-done((bf16[256,1024]{1,0:T(8,128)(2,1)S(1)}, bf16[256,1024]{1,0:T(8,128)(2,1)S(1)}, u32[]{:S(2)}, u32[]{:S(2)}) %collective-permute-start.15) | collective-permute-done | bytes 524320 | tf_op jit(solution)/shard_map/ppermute | solution.py:53
  142.1 15.7 %collective-permute-done.17.refs_3_ = bf16[256,1024]{1,0:T(8,128)(2,1)S(1)} collective-permute-done((bf16[256,1024]{1,0:T(8,128)(2,1)S(1)}, bf16[256,1024]{1,0:T(8,128)(2,1)S(1)}, u32[]{:S(2)}, u32[]{:S(2)}) %collective-permute-start.17) | collective-permute-done | bytes 524320 | tf_op jit(solution)/shard_map/ppermute | solution.py:53
  157.8 3.9 %gather_planes.1 = bf16[256,8,1024]{2,1,0:T(8,128)(2,1)} custom-call(s32[1]{0:T(128)} %bitcast.position_ref, bf16[256,1024]{1,0:T(8,128)(2,1)S(1)} %correlate.8.refs_0_, bf16[256,1024]{1,0:T(8,128)(2,1)S(1)} %correlate.9.refs_1_, bf16[256,1024]{1,0:T(8,128)(2,1)S(1)} %collective-permute-done.15.refs_2_, ...), custom_call_target="tpu_custom_call" | custom-call | tf_op jit(solution)/shard_map/gather_planes/pallas_call | solution.py:364
  (79 shorter events, 20.3 us)
Async XLA Ops:
  1.8 7.1 %copy-start.3 = (f32[4,2048]{1,0:T(4,128)S(1)}, f32[4,2048]{1,0:T(4,128)}, u32[]{:S(2)}) copy-start(f32[4,2048]{1,0:T(4,128)} %w_ref.2) | copy-start | bytes 98308
  1.8 15.7 %collective-permute-start = (bf16[48,2048]{1,0:T(8,128)(2,1)S(1)}, bf16[48,2048]{1,0:T(8,128)(2,1)S(1)}, u32[]{:S(2)}, u32[]{:S(2)}) collective-permute-start(bf16[48,2048]{1,0:T(8,128)(2,1)S(1)} %carry.1), channel_id=1, source_target_pairs={{0,64},{1,65},{2,66},{3,67},{4,68},{5,69},{6,70},{7,71},{16,80},{1... | collective-permute-start | bytes 589832 | tf_op jit(solution)/shard_map/ppermute | solution.py:53
  21.6 44.2 %copy-start = (bf16[8,8,16,128]{3,2,1,0:T(8,128)(2,1)}, bf16[8,8,16,128]{3,2,1,0:T(8,128)(2,1)S(1)}, u32[]{:S(2)}) copy-start(bf16[8,8,16,128]{3,2,1,0:T(8,128)(2,1)S(1)} %get-tuple-element.54.refs_4_) | copy-start | bytes 786436
  21.6 44.2 %copy-start.1 = (bf16[8,8,16,128]{3,2,1,0:T(8,128)(2,1)}, bf16[8,8,16,128]{3,2,1,0:T(8,128)(2,1)S(1)}, u32[]{:S(2)}) copy-start(bf16[8,8,16,128]{3,2,1,0:T(8,128)(2,1)S(1)} %get-tuple-element.53.refs_0_) | copy-start | bytes 786436
  21.6 27.1 %all-to-all-start.1 = ((bf16[320,16,128]{2,1,0:T(8,128)(2,1)}), bf16[320,16,128]{2,1,0:T(8,128)(2,1)S(1)}, u32[]{:S(2)}, u32[]{:S(2)}) async-start(bf16[320,16,128]{2,1,0:T(8,128)(2,1)} %bitcast.6), calls=%async_computation.1 | async-start | bytes 2621440 | tf_op jit(solution)/shard_map/all_to_all | solution.py:62
  29.6 24.9 %collective-permute-start.1 = (bf16[8,8,16,128]{3,2,1,0:T(8,128)(2,1)S(1)}, bf16[8,8,16,128]{3,2,1,0:T(8,128)(2,1)}, u32[]{:S(2)}, u32[]{:S(2)}) collective-permute-start(bf16[8,8,16,128]{3,2,1,0:T(8,128)(2,1)S(1)} %get-tuple-element.54.refs_4_), channel_id=1, source_target_pairs={{0,192},{1,193},{2,194},{3,195},{4,196},{5,197},{6,198},{7,199},{1... | collective-permute-start | bytes 786440 | tf_op jit(solution)/shard_map/ppermute | solution.py:53
  32.5 23.5 %collective-permute-start.2 = (bf16[8,8,16,128]{3,2,1,0:T(8,128)(2,1)S(1)}, bf16[8,8,16,128]{3,2,1,0:T(8,128)(2,1)}, u32[]{:S(2)}, u32[]{:S(2)}) collective-permute-start(bf16[8,8,16,128]{3,2,1,0:T(8,128)(2,1)S(1)} %get-tuple-element.53.refs_0_), channel_id=1, source_target_pairs={{0,64},{1,65},{2,66},{3,67},{4,68},{5,69},{6,70},{7,71},{16,80},{1... | collective-permute-start | bytes 786440 | tf_op jit(solution)/shard_map/ppermute | solution.py:53
  34.0 27.8 %collective-permute-start.3 = (bf16[8,8,16,128]{3,2,1,0:T(8,128)(2,1)S(1)}, bf16[8,8,16,128]{3,2,1,0:T(8,128)(2,1)}, u32[]{:S(2)}, u32[]{:S(2)}) collective-permute-start(bf16[8,8,16,128]{3,2,1,0:T(8,128)(2,1)S(1)} %get-tuple-element.56), channel_id=1, source_target_pairs={{0,136},{1,137},{2,138},{3,139},{4,140},{5,141},{6,142},{7,143},{1... | collective-permute-start | bytes 786440 | tf_op jit(solution)/shard_map/ppermute | solution.py:53
  36.8 29.0 %collective-permute-start.4 = (bf16[8,8,16,128]{3,2,1,0:T(8,128)(2,1)S(1)}, bf16[8,8,16,128]{3,2,1,0:T(8,128)(2,1)}, u32[]{:S(2)}, u32[]{:S(2)}) collective-permute-start(bf16[8,8,16,128]{3,2,1,0:T(8,128)(2,1)S(1)} %get-tuple-element.56), channel_id=1, source_target_pairs={{0,72},{1,73},{2,74},{3,75},{4,76},{5,77},{6,78},{7,79},{16,88},{1... | collective-permute-start | bytes 786440 | tf_op jit(solution)/shard_map/ppermute | solution.py:53
  51.3 28.3 %collective-permute-start.7 = (bf16[8,8,16,128]{3,2,1,0:T(8,128)(2,1)S(1)}, bf16[8,8,16,128]{3,2,1,0:T(8,128)(2,1)S(1)}, u32[]{:S(2)}, u32[]{:S(2)}) collective-permute-start(bf16[8,8,16,128]{3,2,1,0:T(8,128)(2,1)S(1)} %get-tuple-element.65), channel_id=1, source_target_pairs={{0,192},{1,193},{2,194},{3,195},{4,196},{5,197},{6,198},{7,199},{1... | collective-permute-start | bytes 786440 | tf_op jit(solution)/shard_map/ppermute | solution.py:53
  54.5 25.1 %collective-permute-start.8 = (bf16[8,8,16,128]{3,2,1,0:T(8,128)(2,1)S(1)}, bf16[8,8,16,128]{3,2,1,0:T(8,128)(2,1)S(1)}, u32[]{:S(2)}, u32[]{:S(2)}) collective-permute-start(bf16[8,8,16,128]{3,2,1,0:T(8,128)(2,1)S(1)} %get-tuple-element.66), channel_id=1, source_target_pairs={{0,64},{1,65},{2,66},{3,67},{4,68},{5,69},{6,70},{7,71},{16,80},{1... | collective-permute-start | bytes 786440 | tf_op jit(solution)/shard_map/ppermute | solution.py:53
  56.0 23.6 %collective-permute-start.5 = (bf16[8,8,16,128]{3,2,1,0:T(8,128)(2,1)S(1)}, bf16[8,8,16,128]{3,2,1,0:T(8,128)(2,1)S(1)}, u32[]{:S(2)}, u32[]{:S(2)}) collective-permute-start(bf16[8,8,16,128]{3,2,1,0:T(8,128)(2,1)S(1)} %get-tuple-element.61), channel_id=1, source_target_pairs={{0,200},{1,201},{2,202},{3,203},{4,204},{5,205},{6,206},{7,207},{1... | collective-permute-start | bytes 786440 | tf_op jit(solution)/shard_map/ppermute | solution.py:53
  61.9 19.8 %collective-permute-start.6 = (bf16[8,8,16,128]{3,2,1,0:T(8,128)(2,1)S(1)}, bf16[8,8,16,128]{3,2,1,0:T(8,128)(2,1)S(1)}, u32[]{:S(2)}, u32[]{:S(2)}) collective-permute-start(bf16[8,8,16,128]{3,2,1,0:T(8,128)(2,1)S(1)} %get-tuple-element.62), channel_id=1, source_target_pairs={{0,8},{1,9},{2,10},{3,11},{4,12},{5,13},{6,14},{7,15},{16,24},{17,... | collective-permute-start | bytes 786440 | tf_op jit(solution)/shard_map/ppermute | solution.py:53
  68.4 34.0 %all-to-all-start = ((bf16[384,16,128]{2,1,0:T(8,128)(2,1)}), bf16[384,16,128]{2,1,0:T(8,128)(2,1)}, u32[]{:S(2)}, u32[]{:S(2)}) async-start(bf16[384,16,128]{2,1,0:T(8,128)(2,1)} %bitcast.4), calls=%async_computation | async-start | bytes 3145728 | tf_op jit(solution)/shard_map/all_to_all | solution.py:62
  79.6 27.3 %copy-start.4 = (bf16[8,8,16,128]{3,2,1,0:T(8,128)(2,1)}, bf16[8,8,16,128]{3,2,1,0:T(8,128)(2,1)S(1)}, u32[]{:S(2)}) copy-start(bf16[8,8,16,128]{3,2,1,0:T(8,128)(2,1)S(1)} %collective-permute-done.7.refs_2_) | copy-start | bytes 786436
  79.6 22.8 %copy-start.5 = (bf16[8,8,16,128]{3,2,1,0:T(8,128)(2,1)}, bf16[8,8,16,128]{3,2,1,0:T(8,128)(2,1)S(1)}, u32[]{:S(2)}) copy-start(bf16[8,8,16,128]{3,2,1,0:T(8,128)(2,1)S(1)} %collective-permute-done.8.refs_2_) | copy-start | bytes 786436
  79.7 27.2 %copy-start.6 = (bf16[8,8,16,128]{3,2,1,0:T(8,128)(2,1)}, bf16[8,8,16,128]{3,2,1,0:T(8,128)(2,1)S(1)}, u32[]{:S(2)}) copy-start(bf16[8,8,16,128]{3,2,1,0:T(8,128)(2,1)S(1)} %collective-permute-done.5.refs_1_) | copy-start | bytes 786436
  81.6 20.8 %copy-start.7 = (bf16[8,8,16,128]{3,2,1,0:T(8,128)(2,1)}, bf16[8,8,16,128]{3,2,1,0:T(8,128)(2,1)S(1)}, u32[]{:S(2)}) copy-start(bf16[8,8,16,128]{3,2,1,0:T(8,128)(2,1)S(1)} %collective-permute-done.6.refs_1_) | copy-start | bytes 786436
  81.7 14.9 %collective-permute-start.9 = (bf16[8,8,16,128]{3,2,1,0:T(8,128)(2,1)S(1)}, bf16[8,8,16,128]{3,2,1,0:T(8,128)(2,1)S(1)}, u32[]{:S(2)}, u32[]{:S(2)}) collective-permute-start(bf16[8,8,16,128]{3,2,1,0:T(8,128)(2,1)S(1)} %pad_maximum_fusion), channel_id=1, source_target_pairs={{0,192},{1,193},{2,194},{3,195},{4,196},{5,197},{6,198},{7,199},{1... | collective-permute-start | bytes 786440 | tf_op jit(solution)/shard_map/ppermute | solution.py:53
  82.9 15.6 %collective-permute-start.10 = (bf16[8,8,16,128]{3,2,1,0:T(8,128)(2,1)S(1)}, bf16[8,8,16,128]{3,2,1,0:T(8,128)(2,1)S(1)}, u32[]{:S(2)}, u32[]{:S(2)}) collective-permute-start(bf16[8,8,16,128]{3,2,1,0:T(8,128)(2,1)S(1)} %pad_maximum_fusion.1), channel_id=1, source_target_pairs={{0,64},{1,65},{2,66},{3,67},{4,68},{5,69},{6,70},{7,71},{16,80},{1... | collective-permute-start | bytes 786440 | tf_op jit(solution)/shard_map/ppermute | solution.py:53
  84.3 16.8 %collective-permute-start.11 = (bf16[8,8,16,128]{3,2,1,0:T(8,128)(2,1)S(1)}, bf16[8,8,16,128]{3,2,1,0:T(8,128)(2,1)S(1)}, u32[]{:S(2)}, u32[]{:S(2)}) collective-permute-start(bf16[8,8,16,128]{3,2,1,0:T(8,128)(2,1)S(1)} %get-tuple-element.75), channel_id=1, source_target_pairs={{0,200},{1,201},{2,202},{3,203},{4,204},{5,205},{6,206},{7,207},{1... | collective-permute-start | bytes 786440 | tf_op jit(solution)/shard_map/ppermute | solution.py:53
  85.8 16.6 %collective-permute-start.12 = (bf16[8,8,16,128]{3,2,1,0:T(8,128)(2,1)S(1)}, bf16[8,8,16,128]{3,2,1,0:T(8,128)(2,1)S(1)}, u32[]{:S(2)}, u32[]{:S(2)}) collective-permute-start(bf16[8,8,16,128]{3,2,1,0:T(8,128)(2,1)S(1)} %get-tuple-element.75), channel_id=1, source_target_pairs={{0,8},{1,9},{2,10},{3,11},{4,12},{5,13},{6,14},{7,15},{16,24},{17,... | collective-permute-start | bytes 786440 | tf_op jit(solution)/shard_map/ppermute | solution.py:53
  96.6 5.8 %copy-start.11 = (bf16[8,8,16,128]{3,2,1,0:T(8,128)(2,1)}, bf16[8,8,16,128]{3,2,1,0:T(8,128)(2,1)S(1)}, u32[]{:S(2)}) copy-start(bf16[8,8,16,128]{3,2,1,0:T(8,128)(2,1)S(1)} %collective-permute-done.9.refs_3_) | copy-start | bytes 786436
  98.6 8.4 %copy-start.12 = (bf16[8,8,16,128]{3,2,1,0:T(8,128)(2,1)}, bf16[8,8,16,128]{3,2,1,0:T(8,128)(2,1)S(1)}, u32[]{:S(2)}) copy-start(bf16[8,8,16,128]{3,2,1,0:T(8,128)(2,1)S(1)} %collective-permute-done.10.refs_3_) | copy-start | bytes 786436
  98.6 16.2 %collective-permute-start.13 = (bf16[8,8,16,128]{3,2,1,0:T(8,128)(2,1)S(1)}, bf16[8,8,16,128]{3,2,1,0:T(8,128)(2,1)S(1)}, u32[]{:S(2)}, u32[]{:S(2)}) collective-permute-start(bf16[8,8,16,128]{3,2,1,0:T(8,128)(2,1)S(1)} %pad_maximum_fusion.2), channel_id=1, source_target_pairs={{0,192},{1,193},{2,194},{3,195},{4,196},{5,197},{6,198},{7,199},{1... | collective-permute-start | bytes 786440 | tf_op jit(solution)/shard_map/ppermute | solution.py:53
  98.6 16.2 %collective-permute-start.14 = (bf16[8,8,16,128]{3,2,1,0:T(8,128)(2,1)}, bf16[8,8,16,128]{3,2,1,0:T(8,128)(2,1)S(1)}, u32[]{:S(2)}, u32[]{:S(2)}) collective-permute-start(bf16[8,8,16,128]{3,2,1,0:T(8,128)(2,1)} %pad_maximum_fusion.3), channel_id=1, source_target_pairs={{0,64},{1,65},{2,66},{3,67},{4,68},{5,69},{6,70},{7,71},{16,80},{1... | collective-permute-start | bytes 786440 | tf_op jit(solution)/shard_map/ppermute | solution.py:53
  102.4 4.5 %copy-start.9 = (bf16[8,8,16,128]{3,2,1,0:T(8,128)(2,1)}, bf16[8,8,16,128]{3,2,1,0:T(8,128)(2,1)S(1)}, u32[]{:S(2)}) copy-start(bf16[8,8,16,128]{3,2,1,0:T(8,128)(2,1)S(1)} %collective-permute-done.12.refs_4_) | copy-start | bytes 786436
  105.0 37.1 %collective-permute-start.15 = (bf16[256,1024]{1,0:T(8,128)(2,1)S(1)}, bf16[256,1024]{1,0:T(8,128)(2,1)S(1)}, u32[]{:S(2)}, u32[]{:S(2)}) collective-permute-start(bf16[256,1024]{1,0:T(8,128)(2,1)S(1)} %correlate.10), channel_id=1, source_target_pairs={{0,192},{1,193},{2,194},{3,195},{4,196},{5,197},{6,198},{7,199},{1... | collective-permute-start | bytes 1572872 | tf_op jit(solution)/shard_map/ppermute | solution.py:53
  109.5 32.6 %collective-permute-start.16 = (bf16[256,1024]{1,0:T(8,128)(2,1)S(1)}, bf16[256,1024]{1,0:T(8,128)(2,1)S(1)}, u32[]{:S(2)}, u32[]{:S(2)}) collective-permute-start(bf16[256,1024]{1,0:T(8,128)(2,1)S(1)} %correlate.11), channel_id=1, source_target_pairs={{0,64},{1,65},{2,66},{3,67},{4,68},{5,69},{6,70},{7,71},{16,80},{1... | collective-permute-start | bytes 1572872 | tf_op jit(solution)/shard_map/ppermute | solution.py:53
  115.5 4.3 %copy-start.13 = (bf16[8,8,16,128]{3,2,1,0:T(8,128)(2,1)}, bf16[8,8,16,128]{3,2,1,0:T(8,128)(2,1)S(1)}, u32[]{:S(2)}) copy-start(bf16[8,8,16,128]{3,2,1,0:T(8,128)(2,1)S(1)} %collective-permute-done.14.refs_3_) | copy-start | bytes 786436
  118.0 39.7 %collective-permute-start.17 = (bf16[256,1024]{1,0:T(8,128)(2,1)S(1)}, bf16[256,1024]{1,0:T(8,128)(2,1)S(1)}, u32[]{:S(2)}, u32[]{:S(2)}) collective-permute-start(bf16[256,1024]{1,0:T(8,128)(2,1)S(1)} %correlate.12), channel_id=1, source_target_pairs={{0,192},{1,193},{2,194},{3,195},{4,196},{5,197},{6,198},{7,199},{1... | collective-permute-start | bytes 1572872 | tf_op jit(solution)/shard_map/ppermute | solution.py:53
  122.4 35.4 %collective-permute-start.18 = (bf16[256,1024]{1,0:T(8,128)(2,1)S(1)}, bf16[256,1024]{1,0:T(8,128)(2,1)S(1)}, u32[]{:S(2)}, u32[]{:S(2)}) collective-permute-start(bf16[256,1024]{1,0:T(8,128)(2,1)S(1)} %correlate.13), channel_id=1, source_target_pairs={{0,64},{1,65},{2,66},{3,67},{4,68},{5,69},{6,70},{7,71},{16,80},{1... | collective-permute-start | bytes 1572872 | tf_op jit(solution)/shard_map/ppermute | solution.py:53
  (4 other events, 3.9 us)

commit v5 on v4

--- a/solution.py
+++ b/solution.py
@@ -376,8 +376,8 @@
 
 def places(which):
     at, early = 4 * which, 6 * which
-    here = [(0, early), (7, at), (0, early + 1), (5, 0), (5, 4), (0, early + 2), (4, at), (2, at)]
-    there = [(0, early + 3), (8, at), (0, early + 4), (1, at), (3, at), (0, early + 5), (6, 4), (6, 0)]
+    here = [(0, early), (7, 0), (0, early + 1), (5, 0), (5, 4), (0, early + 2), (4, at), (2, at)]
+    there = [(0, early + 3), (8, 0), (0, early + 4), (1, at), (3, at), (0, early + 5), (6, 4), (6, 0)]
     return [[[(*place, 0, 4)] for place in side] for side in (here, there)]
 
 
@@ -427,7 +427,7 @@
     left_31, right_71 = both_ways(sent_3, sent_7, 1)
     left_4, right_6 = both_ways(sent_4, sent_6, 2)
     sent_1, left_4, right_6 = lax.optimization_barrier((sent_1, left_4, right_6))
-    ones = both_ways(sent_1, sent_1, 1)
+    ones = [both_ways(sent_1[:4], sent_1[:4], 1)]
 
     def onward(which):
         part = slice(4 * which, 4 * which + 4)
@@ -437,11 +437,12 @@
         ]
 
     far_0 = both_ways(*onward(0), 2)
-    far_0, onward_1 = lax.optimization_barrier((far_0, onward(1)))
+    far_0, onward_1, sent_1 = lax.optimization_barrier((far_0, onward(1), sent_1))
     far_1 = both_ways(*onward_1, 2)
+    ones.append(both_ways(sent_1[4:], sent_1[4:], 1))
     for which, far in enumerate((far_0, far_1)):
         here, there = places(which)
-        arrays = [packed, left_31, right_71, left_4, right_6, *far, *ones]
+        arrays = [packed, left_31, right_71, left_4, right_6, *far, *ones[which]]
         planes[2 + which], planes[4 + which] = both_ways(
             correlate(before, z_lo, here, arrays), correlate(after, z_lo, there, arrays), 2
         )

time: 165 us -> 175 us (1.061)
  waiting for transfers between devices: 60.7 us -> 67.9 us
  starting transfers between devices: 51.7 us -> 55.4 us
    ppermute x19 -> x21, waiting for transfers between devices: 49.9 us -> 57.1 us  [along_z(): return lax.ppermute(x, ('tm', 'feed'), pairs)]
    ppermute x19 -> x21, starting transfers between devices: 32.5 us -> 36.2 us  [along_z(): return lax.ppermute(x, ('tm', 'feed'), pairs)]
  transfers between devices with their start and end apart: 21 -> 23, of which waited for: 10 -> 11; matrix products, arithmetic and copies ran while one was open for 1% -> 1% of each run, Pallas kernels for 21% -> 20%
where the time goes in v5:
time: 175 us; the launch traced here: 173 us
  waiting for transfers between devices  67.9 us (39%)
  starting transfers between devices  55.4 us (32%)
  Pallas kernels  43.5 us (25%)
  local copies, waits for them, and re-layouts  2.85 us (2%)
  other arithmetic  2.11 us (1%)
    ppermute x21, waiting for transfers between devices, along_z(): return lax.ppermute(x, ('tm', 'feed'), pairs)  57.1 us
    ppermute x21, starting transfers between devices, along_z(): return lax.ppermute(x, ('tm', 'feed'), pairs)  36.2 us
    pallas_call x8, Pallas kernels, correlate(): pl.pallas_call(functools.partial(correlate_kernel, layout), in_specs=[pl....  20.5 us
    all_to_all x2, starting transfers between devices, turn(): lax.all_to_all(x, 'feed', split_axis=0, concat_axis=0, tiled=True, axis_i...  19.2 us
    all_to_all x2, waiting for transfers between devices, turn(): lax.all_to_all(x, 'feed', split_axis=0, concat_axis=0, tiled=True, axis_i...  10.8 us
    pallas_call x1, Pallas kernels, product(): pl.pallas_call(product_kernel, in_specs=[vmem] * 2, out_specs=vmem, out_s...  4.5 us
    pallas_call x1, Pallas kernels, filter_own(): pl.pallas_call(filter_kernel, in_specs=[pl.BlockSpec(memory_space=pltpu.H...  4.15 us
    pallas_call x2, Pallas kernels, move(): pl.pallas_call(functools.partial(move_kernel, moves, len(arrays)), in_spe...  4.15 us
  transfers between devices with their start and end apart: 23, of which 11 were waited for; matrix products, arithmetic and copies ran while one was open for 1% of the time, Pallas kernels for 20%

profile of v5, /device:TPU:1, one launch (start us, length us, event | category | flops | bytes accessed | tf_op | source)
XLA Modules:
  0.0 172.9 jit_solution(1327778650207571712)
XLA Ops:
  1.8 3.9 %collective-permute-start = (bf16[48,2048]{1,0:T(8,128)(2,1)S(1)}, bf16[48,2048]{1,0:T(8,128)(2,1)S(1)}, u32[]{:S(2)}, u32[]{:S(2)}) collective-permute-start(bf16[48,2048]{1,0:T(8,128)(2,1)S(1)} %carry.1), channel_id=1, source_target_pairs={{0,64},{1,65},{2,66},{3,67},{4,68},{5,69},{6,70},{7,71},{16,80},{1... | collective-permute-start | bytes 589832 | tf_op jit(solution)/shard_map/ppermute | solution.py:53
  8.9 4.1 %own_filter.1 = (bf16[1024,2048]{1,0:T(8,128)(2,1)S(1)}, f32[48,2048]{1,0:T(8,128)S(1)}) custom-call(s32[16,131072]{1,0:T(8,128)} %v_ref.3, f32[4,2048]{1,0:T(4,128)S(1)} %copy-done.3), custom_call_target="tpu_custom_call" | custom-call | tf_op jit(solution)/shard_map/own_filter/pallas_call | solution.py:142
  13.1 4.5 %product.1.wide = f32[4,2,1024,128]{3,2,1,0:T(8,128)S(1)} custom-call(bf16[1024,2048]{1,0:T(8,128)(2,1)S(1)} %get-tuple-element.52.f_ref, bf16[4,2048,256]{2,1,0:T(8,128)(2,1)S(1)} %dft_table.1.t_ref), custom_call_target="tpu_custom_call" | custom-call | tf_op jit(solution)/shard_map/product/pallas_call | solution.py:208
  17.6 4.0 %dft.1 = (bf16[40,8,16,128]{3,2,1,0:T(8,128)(2,1)}, bf16[8,8,16,128]{3,2,1,0:T(8,128)(2,1)S(1)}, bf16[8,8,16,128]{3,2,1,0:T(8,128)(2,1)S(1)}, bf16[8,8,16,128]{3,2,1,0:T(8,128)(2,1)S(1)}) custom-call(s32[1]{0:T(128)} %bitcast.position_ref, f32[4,2,1024,128]{3,2,1,0:T(8,128)S(1)} %product.1.wide, f32[48,2048]{1,0:T(8,128)S(1)} %get-tuple-element.54.head_ref, ...), custom_call_target="tpu_custom_call" | custom-call | tf_op jit(solution)/shard_map/dft/pallas_call | solution.py:246
  21.6 8.0 %all-to-all-start.1 = ((bf16[320,16,128]{2,1,0:T(8,128)(2,1)}), bf16[320,16,128]{2,1,0:T(8,128)(2,1)S(1)}, u32[]{:S(2)}, u32[]{:S(2)}) async-start(bf16[320,16,128]{2,1,0:T(8,128)(2,1)} %bitcast.6), calls=%async_computation.1 | async-start | bytes 2621440 | tf_op jit(solution)/shard_map/all_to_all | solution.py:62
  29.6 2.9 %collective-permute-start.1 = (bf16[8,8,16,128]{3,2,1,0:T(8,128)(2,1)S(1)}, bf16[8,8,16,128]{3,2,1,0:T(8,128)(2,1)}, u32[]{:S(2)}, u32[]{:S(2)}) collective-permute-start(bf16[8,8,16,128]{3,2,1,0:T(8,128)(2,1)S(1)} %get-tuple-element.57.refs_4_), channel_id=1, source_target_pairs={{0,192},{1,193},{2,194},{3,195},{4,196},{5,197},{6,198},{7,199},{1... | collective-permute-start | bytes 786440 | tf_op jit(solution)/shard_map/ppermute | solution.py:53
  34.0 2.8 %collective-permute-start.3 = (bf16[8,8,16,128]{3,2,1,0:T(8,128)(2,1)S(1)}, bf16[8,8,16,128]{3,2,1,0:T(8,128)(2,1)}, u32[]{:S(2)}, u32[]{:S(2)}) collective-permute-start(bf16[8,8,16,128]{3,2,1,0:T(8,128)(2,1)S(1)} %get-tuple-element.59), channel_id=1, source_target_pairs={{0,136},{1,137},{2,138},{3,139},{4,140},{5,141},{6,142},{7,143},{1... | collective-permute-start | bytes 786440 | tf_op jit(solution)/shard_map/ppermute | solution.py:53
  38.0 10.8 %all-to-all-done.1 = bf16[320,16,128]{2,1,0:T(8,128)(2,1)S(1)} async-done(((bf16[320,16,128]{2,1,0:T(8,128)(2,1)}), bf16[320,16,128]{2,1,0:T(8,128)(2,1)S(1)}, u32[]{:S(2)}, u32[]{:S(2)}) %all-to-all-start.1) | async-done | bytes 1310752 | tf_op jit(solution)/shard_map/all_to_all | solution.py:62
  51.3 3.3 %collective-permute-start.7 = (bf16[8,8,16,128]{3,2,1,0:T(8,128)(2,1)S(1)}, bf16[8,8,16,128]{3,2,1,0:T(8,128)(2,1)S(1)}, u32[]{:S(2)}, u32[]{:S(2)}) collective-permute-start(bf16[8,8,16,128]{3,2,1,0:T(8,128)(2,1)S(1)} %get-tuple-element.68), channel_id=1, source_target_pairs={{0,192},{1,193},{2,194},{3,195},{4,196},{5,197},{6,198},{7,199},{1... | collective-permute-start | bytes 786440 | tf_op jit(solution)/shard_map/ppermute | solution.py:53
  57.3 4.6 %collective-permute-done.3.refs_5_ = bf16[8,8,16,128]{3,2,1,0:T(8,128)(2,1)} collective-permute-done((bf16[8,8,16,128]{3,2,1,0:T(8,128)(2,1)S(1)}, bf16[8,8,16,128]{3,2,1,0:T(8,128)(2,1)}, u32[]{:S(2)}, u32[]{:S(2)}) %collective-permute-start.3) | collective-permute-done | bytes 262176 | tf_op jit(solution)/shard_map/ppermute | solution.py:53
  61.9 2.9 %collective-permute-start.6 = (bf16[8,8,16,128]{3,2,1,0:T(8,128)(2,1)S(1)}, bf16[8,8,16,128]{3,2,1,0:T(8,128)(2,1)S(1)}, u32[]{:S(2)}, u32[]{:S(2)}) collective-permute-start(bf16[8,8,16,128]{3,2,1,0:T(8,128)(2,1)S(1)} %get-tuple-element.65), channel_id=1, source_target_pairs={{0,8},{1,9},{2,10},{3,11},{4,12},{5,13},{6,14},{7,15},{16,24},{17,... | collective-permute-start | bytes 786440 | tf_op jit(solution)/shard_map/ppermute | solution.py:53
  65.7 2.7 %move.2 = bf16[4,8,12,16,128]{4,3,2,1,0:T(8,128)(2,1)} custom-call(bf16[8,8,16,128]{3,2,1,0:T(8,128)(2,1)} %copy-done.1, bf16[8,8,16,128]{3,2,1,0:T(8,128)(2,1)} %collective-permute-done.1.refs_1_, bf16[8,8,16,128]{3,2,1,0:T(8,128)(2,1)} %collective-permute-done.4.refs_2_, bf16[8,8,16,128]{3,2,1,0:T(8,128)(2,1)} %collective-permute-done.2.refs_3_, ...), custom_call_target="tpu_custom_call" | custom-call | tf_op jit(solution)/shard_map/move/pallas_call | solution.py:273
  68.4 11.1 %all-to-all-start = ((bf16[384,16,128]{2,1,0:T(8,128)(2,1)}), bf16[384,16,128]{2,1,0:T(8,128)(2,1)}, u32[]{:S(2)}, u32[]{:S(2)}) async-start(bf16[384,16,128]{2,1,0:T(8,128)(2,1)} %bitcast.4), calls=%async_computation | async-start | bytes 3145728 | tf_op jit(solution)/shard_map/all_to_all | solution.py:62
  79.7 2.0 %collective-permute-done.6.refs_1_ = bf16[8,8,16,128]{3,2,1,0:T(8,128)(2,1)S(1)} collective-permute-done((bf16[8,8,16,128]{3,2,1,0:T(8,128)(2,1)S(1)}, bf16[8,8,16,128]{3,2,1,0:T(8,128)(2,1)S(1)}, u32[]{:S(2)}, u32[]{:S(2)}) %collective-permute-start.6) | collective-permute-done | bytes 262176 | tf_op jit(solution)/shard_map/ppermute | solution.py:53
  86.6 10.0 %collective-permute-done.9.refs_3_ = bf16[8,8,16,128]{3,2,1,0:T(8,128)(2,1)S(1)} collective-permute-done((bf16[8,8,16,128]{3,2,1,0:T(8,128)(2,1)S(1)}, bf16[8,8,16,128]{3,2,1,0:T(8,128)(2,1)S(1)}, u32[]{:S(2)}, u32[]{:S(2)}) %collective-permute-start.9) | collective-permute-done | bytes 262176 | tf_op jit(solution)/shard_map/ppermute | solution.py:53
  96.6 2.3 %collective-permute-done.10.refs_3_ = bf16[8,8,16,128]{3,2,1,0:T(8,128)(2,1)S(1)} collective-permute-done((bf16[8,8,16,128]{3,2,1,0:T(8,128)(2,1)S(1)}, bf16[8,8,16,128]{3,2,1,0:T(8,128)(2,1)S(1)}, u32[]{:S(2)}, u32[]{:S(2)}) %collective-permute-start.10) | collective-permute-done | bytes 262176 | tf_op jit(solution)/shard_map/ppermute | solution.py:53
  98.9 2.4 %collective-permute-start.14 = (bf16[8,8,16,128]{3,2,1,0:T(8,128)(2,1)}, bf16[8,8,16,128]{3,2,1,0:T(8,128)(2,1)S(1)}, u32[]{:S(2)}, u32[]{:S(2)}) collective-permute-start(bf16[8,8,16,128]{3,2,1,0:T(8,128)(2,1)} %pad_maximum_fusion.3), channel_id=1, source_target_pairs={{0,64},{1,65},{2,66},{3,67},{4,68},{5,69},{6,70},{7,71},{16,80},{1... | collective-permute-start | bytes 786440 | tf_op jit(solution)/shard_map/ppermute | solution.py:53
  101.3 3.0 %collective-permute-start.15 = (bf16[4,8,16,128]{3,2,1,0:T(8,128)(2,1)S(1)}, bf16[4,8,16,128]{3,2,1,0:T(8,128)(2,1)S(1)}, u32[]{:S(2)}, u32[]{:S(2)}) collective-permute-start(bf16[4,8,16,128]{3,2,1,0:T(8,128)(2,1)S(1)} %slice.41), channel_id=1, source_target_pairs={{0,200},{1,201},{2,202},{3,203},{4,204},{5,205},{6,206},{7,207},{1... | collective-permute-start | bytes 393224 | tf_op jit(solution)/shard_map/ppermute | solution.py:53
  104.4 11.1 %collective-permute-done.12.refs_4_ = bf16[4,8,16,128]{3,2,1,0:T(8,128)(2,1)S(1)} collective-permute-done((bf16[4,8,16,128]{3,2,1,0:T(8,128)(2,1)S(1)}, bf16[4,8,16,128]{3,2,1,0:T(8,128)(2,1)S(1)}, u32[]{:S(2)}, u32[]{:S(2)}) %collective-permute-start.12) | collective-permute-done | bytes 131104 | tf_op jit(solution)/shard_map/ppermute | solution.py:53
  115.5 2.6 %correlate.10 = bf16[256,1024]{1,0:T(8,128)(2,1)S(1)} custom-call(s32[2]{0:T(128)S(1)} %pad_add_fusion.2.where_ref, bf16[4,8,12,16,128]{4,3,2,1,0:T(8,128)(2,1)} %bitcast.5.refs_0_, bf16[8,8,16,128]{3,2,1,0:T(8,128)(2,1)} %copy-done.7, bf16[8,8,16,128]{3,2,1,0:T(8,128)(2,1)} %copy-done.5, bf16[8,8,16,128]{3,2,1,0:T(8,128)(2,1)} %copy-done.9, ...), custom_call_target="tpu_custom_call" | custom-call | tf_op jit(solution)/shard_map/correlate/pallas_call | solution.py:332
  120.1 2.6 %correlate.11 = bf16[256,1024]{1,0:T(8,128)(2,1)S(1)} custom-call(s32[2]{0:T(128)S(1)} %pad_add_fusion.3.where_ref, bf16[4,8,12,16,128]{4,3,2,1,0:T(8,128)(2,1)} %bitcast.5.refs_0_, bf16[8,8,16,128]{3,2,1,0:T(8,128)(2,1)} %copy-done.6, bf16[8,8,16,128]{3,2,1,0:T(8,128)(2,1)} %copy-done.4, bf16[8,8,16,128]{3,2,1,0:T(8,128)(2,1)} %copy-done.10, ...), custom_call_target="tpu_custom_call" | custom-call | tf_op jit(solution)/shard_map/correlate/pallas_call | solution.py:332
  124.0 2.6 %correlate.12 = bf16[256,1024]{1,0:T(8,128)(2,1)S(1)} custom-call(s32[2]{0:T(128)S(1)} %pad_add_fusion.2.where_ref, bf16[4,8,12,16,128]{4,3,2,1,0:T(8,128)(2,1)} %bitcast.5.refs_0_, bf16[8,8,16,128]{3,2,1,0:T(8,128)(2,1)} %copy-done.7, bf16[8,8,16,128]{3,2,1,0:T(8,128)(2,1)} %copy-done.5, bf16[8,8,16,128]{3,2,1,0:T(8,128)(2,1)} %copy-done.12, ...), custom_call_target="tpu_custom_call" | custom-call | tf_op jit(solution)/shard_map/correlate/pallas_call | solution.py:332
  126.5 3.2 %collective-permute-start.19 = (bf16[256,1024]{1,0:T(8,128)(2,1)S(1)}, bf16[256,1024]{1,0:T(8,128)(2,1)S(1)}, u32[]{:S(2)}, u32[]{:S(2)}) collective-permute-start(bf16[256,1024]{1,0:T(8,128)(2,1)S(1)} %correlate.12), channel_id=1, source_target_pairs={{0,192},{1,193},{2,194},{3,195},{4,196},{5,197},{6,198},{7,199},{1... | collective-permute-start | bytes 1572872 | tf_op jit(solution)/shard_map/ppermute | solution.py:53
  129.7 2.6 %correlate.13 = bf16[256,1024]{1,0:T(8,128)(2,1)S(1)} custom-call(s32[2]{0:T(128)S(1)} %pad_add_fusion.3.where_ref, bf16[4,8,12,16,128]{4,3,2,1,0:T(8,128)(2,1)} %bitcast.5.refs_0_, bf16[8,8,16,128]{3,2,1,0:T(8,128)(2,1)} %copy-done.6, bf16[8,8,16,128]{3,2,1,0:T(8,128)(2,1)} %copy-done.4, bf16[8,8,16,128]{3,2,1,0:T(8,128)(2,1)} %copy-done.11, ...), custom_call_target="tpu_custom_call" | custom-call | tf_op jit(solution)/shard_map/correlate/pallas_call | solution.py:332
  132.5 2.6 %correlate.8.refs_0_ = bf16[256,1024]{1,0:T(8,128)(2,1)S(1)} custom-call(s32[2]{0:T(128)S(1)} %pad_add_fusion.1.where_ref, bf16[4,8,12,16,128]{4,3,2,1,0:T(8,128)(2,1)} %bitcast.5.refs_0_, bf16[8,8,16,128]{3,2,1,0:T(8,128)(2,1)} %copy-done.7, bf16[8,8,16,128]{3,2,1,0:T(8,128)(2,1)} %copy-done.5, bf16[8,8,16,128]{3,2,1,0:T(8,128)(2,1)} %copy-done.9, ...), custom_call_target="tpu_custom_call" | custom-call | tf_op jit(solution)/shard_map/correlate/pallas_call | solution.py:332
  135.0 2.6 %correlate.14.refs_6_ = bf16[256,1024]{1,0:T(8,128)(2,1)S(1)} custom-call(s32[2]{0:T(128)S(1)} %pad_add_fusion.1.where_ref, bf16[4,8,12,16,128]{4,3,2,1,0:T(8,128)(2,1)} %bitcast.5.refs_0_, bf16[8,8,16,128]{3,2,1,0:T(8,128)(2,1)} %copy-done.6, bf16[8,8,16,128]{3,2,1,0:T(8,128)(2,1)} %copy-done.4, bf16[8,8,16,128]{3,2,1,0:T(8,128)(2,1)} %copy-done.10, ...), custom_call_target="tpu_custom_call" | custom-call | tf_op jit(solution)/shard_map/correlate/pallas_call | solution.py:332
  137.6 2.6 %correlate.9.refs_1_ = bf16[256,1024]{1,0:T(8,128)(2,1)S(1)} custom-call(s32[2]{0:T(128)S(1)} %pad_add_fusion.1.where_ref, bf16[4,8,12,16,128]{4,3,2,1,0:T(8,128)(2,1)} %bitcast.5.refs_0_, bf16[8,8,16,128]{3,2,1,0:T(8,128)(2,1)} %copy-done.7, bf16[8,8,16,128]{3,2,1,0:T(8,128)(2,1)} %copy-done.5, bf16[8,8,16,128]{3,2,1,0:T(8,128)(2,1)} %copy-done.12, ...), custom_call_target="tpu_custom_call" | custom-call | tf_op jit(solution)/shard_map/correlate/pallas_call | solution.py:332
  140.2 2.6 %correlate.15.refs_7_ = bf16[256,1024]{1,0:T(8,128)(2,1)S(1)} custom-call(s32[2]{0:T(128)S(1)} %pad_add_fusion.1.where_ref, bf16[4,8,12,16,128]{4,3,2,1,0:T(8,128)(2,1)} %bitcast.5.refs_0_, bf16[8,8,16,128]{3,2,1,0:T(8,128)(2,1)} %copy-done.6, bf16[8,8,16,128]{3,2,1,0:T(8,128)(2,1)} %copy-done.4, bf16[8,8,16,128]{3,2,1,0:T(8,128)(2,1)} %copy-done.11, ...), custom_call_target="tpu_custom_call" | custom-call | tf_op jit(solution)/shard_map/correlate/pallas_call | solution.py:332
  144.2 4.9 %collective-permute-done.18.refs_4_ = bf16[256,1024]{1,0:T(8,128)(2,1)S(1)} collective-permute-done((bf16[256,1024]{1,0:T(8,128)(2,1)S(1)}, bf16[256,1024]{1,0:T(8,128)(2,1)S(1)}, u32[]{:S(2)}, u32[]{:S(2)}) %collective-permute-start.18) | collective-permute-done | bytes 524320 | tf_op jit(solution)/shard_map/ppermute | solution.py:53
  149.1 15.6 %collective-permute-done.19.refs_3_ = bf16[256,1024]{1,0:T(8,128)(2,1)S(1)} collective-permute-done((bf16[256,1024]{1,0:T(8,128)(2,1)S(1)}, bf16[256,1024]{1,0:T(8,128)(2,1)S(1)}, u32[]{:S(2)}, u32[]{:S(2)}) %collective-permute-start.19) | collective-permute-done | bytes 524320 | tf_op jit(solution)/shard_map/ppermute | solution.py:53
  164.7 4.3 %collective-permute-done.20.refs_5_ = bf16[256,1024]{1,0:T(8,128)(2,1)S(1)} collective-permute-done((bf16[256,1024]{1,0:T(8,128)(2,1)S(1)}, bf16[256,1024]{1,0:T(8,128)(2,1)S(1)}, u32[]{:S(2)}, u32[]{:S(2)}) %collective-permute-start.20) | collective-permute-done | bytes 524320 | tf_op jit(solution)/shard_map/ppermute | solution.py:53
  168.9 3.9 %gather_planes.1 = bf16[256,8,1024]{2,1,0:T(8,128)(2,1)} custom-call(s32[1]{0:T(128)} %bitcast.position_ref, bf16[256,1024]{1,0:T(8,128)(2,1)S(1)} %correlate.8.refs_0_, bf16[256,1024]{1,0:T(8,128)(2,1)S(1)} %correlate.9.refs_1_, bf16[256,1024]{1,0:T(8,128)(2,1)S(1)} %collective-permute-done.17.refs_2_, ...), custom_call_target="tpu_custom_call" | custom-call | tf_op jit(solution)/shard_map/gather_planes/pallas_call | solution.py:364
  (89 shorter events, 23.2 us)
Async XLA Ops:
  1.8 15.7 %collective-permute-start = (bf16[48,2048]{1,0:T(8,128)(2,1)S(1)}, bf16[48,2048]{1,0:T(8,128)(2,1)S(1)}, u32[]{:S(2)}, u32[]{:S(2)}) collective-permute-start(bf16[48,2048]{1,0:T(8,128)(2,1)S(1)} %carry.1), channel_id=1, source_target_pairs={{0,64},{1,65},{2,66},{3,67},{4,68},{5,69},{6,70},{7,71},{16,80},{1... | collective-permute-start | bytes 589832 | tf_op jit(solution)/shard_map/ppermute | solution.py:53
  21.6 44.2 %copy-start = (bf16[8,8,16,128]{3,2,1,0:T(8,128)(2,1)}, bf16[8,8,16,128]{3,2,1,0:T(8,128)(2,1)S(1)}, u32[]{:S(2)}) copy-start(bf16[8,8,16,128]{3,2,1,0:T(8,128)(2,1)S(1)} %get-tuple-element.57.refs_4_) | copy-start | bytes 786436
  21.6 44.2 %copy-start.1 = (bf16[8,8,16,128]{3,2,1,0:T(8,128)(2,1)}, bf16[8,8,16,128]{3,2,1,0:T(8,128)(2,1)S(1)}, u32[]{:S(2)}) copy-start(bf16[8,8,16,128]{3,2,1,0:T(8,128)(2,1)S(1)} %get-tuple-element.56.refs_0_) | copy-start | bytes 786436
  21.6 27.1 %all-to-all-start.1 = ((bf16[320,16,128]{2,1,0:T(8,128)(2,1)}), bf16[320,16,128]{2,1,0:T(8,128)(2,1)S(1)}, u32[]{:S(2)}, u32[]{:S(2)}) async-start(bf16[320,16,128]{2,1,0:T(8,128)(2,1)} %bitcast.6), calls=%async_computation.1 | async-start | bytes 2621440 | tf_op jit(solution)/shard_map/all_to_all | solution.py:62
  29.6 24.9 %collective-permute-start.1 = (bf16[8,8,16,128]{3,2,1,0:T(8,128)(2,1)S(1)}, bf16[8,8,16,128]{3,2,1,0:T(8,128)(2,1)}, u32[]{:S(2)}, u32[]{:S(2)}) collective-permute-start(bf16[8,8,16,128]{3,2,1,0:T(8,128)(2,1)S(1)} %get-tuple-element.57.refs_4_), channel_id=1, source_target_pairs={{0,192},{1,193},{2,194},{3,195},{4,196},{5,197},{6,198},{7,199},{1... | collective-permute-start | bytes 786440 | tf_op jit(solution)/shard_map/ppermute | solution.py:53
  32.5 23.5 %collective-permute-start.2 = (bf16[8,8,16,128]{3,2,1,0:T(8,128)(2,1)S(1)}, bf16[8,8,16,128]{3,2,1,0:T(8,128)(2,1)}, u32[]{:S(2)}, u32[]{:S(2)}) collective-permute-start(bf16[8,8,16,128]{3,2,1,0:T(8,128)(2,1)S(1)} %get-tuple-element.56.refs_0_), channel_id=1, source_target_pairs={{0,64},{1,65},{2,66},{3,67},{4,68},{5,69},{6,70},{7,71},{16,80},{1... | collective-permute-start | bytes 786440 | tf_op jit(solution)/shard_map/ppermute | solution.py:53
  34.0 27.8 %collective-permute-start.3 = (bf16[8,8,16,128]{3,2,1,0:T(8,128)(2,1)S(1)}, bf16[8,8,16,128]{3,2,1,0:T(8,128)(2,1)}, u32[]{:S(2)}, u32[]{:S(2)}) collective-permute-start(bf16[8,8,16,128]{3,2,1,0:T(8,128)(2,1)S(1)} %get-tuple-element.59), channel_id=1, source_target_pairs={{0,136},{1,137},{2,138},{3,139},{4,140},{5,141},{6,142},{7,143},{1... | collective-permute-start | bytes 786440 | tf_op jit(solution)/shard_map/ppermute | solution.py:53
  36.8 29.0 %collective-permute-start.4 = (bf16[8,8,16,128]{3,2,1,0:T(8,128)(2,1)S(1)}, bf16[8,8,16,128]{3,2,1,0:T(8,128)(2,1)}, u32[]{:S(2)}, u32[]{:S(2)}) collective-permute-start(bf16[8,8,16,128]{3,2,1,0:T(8,128)(2,1)S(1)} %get-tuple-element.59), channel_id=1, source_target_pairs={{0,72},{1,73},{2,74},{3,75},{4,76},{5,77},{6,78},{7,79},{16,88},{1... | collective-permute-start | bytes 786440 | tf_op jit(solution)/shard_map/ppermute | solution.py:53
  51.3 28.3 %collective-permute-start.7 = (bf16[8,8,16,128]{3,2,1,0:T(8,128)(2,1)S(1)}, bf16[8,8,16,128]{3,2,1,0:T(8,128)(2,1)S(1)}, u32[]{:S(2)}, u32[]{:S(2)}) collective-permute-start(bf16[8,8,16,128]{3,2,1,0:T(8,128)(2,1)S(1)} %get-tuple-element.68), channel_id=1, source_target_pairs={{0,192},{1,193},{2,194},{3,195},{4,196},{5,197},{6,198},{7,199},{1... | collective-permute-start | bytes 786440 | tf_op jit(solution)/shard_map/ppermute | solution.py:53
  54.5 25.1 %collective-permute-start.8 = (bf16[8,8,16,128]{3,2,1,0:T(8,128)(2,1)S(1)}, bf16[8,8,16,128]{3,2,1,0:T(8,128)(2,1)S(1)}, u32[]{:S(2)}, u32[]{:S(2)}) collective-permute-start(bf16[8,8,16,128]{3,2,1,0:T(8,128)(2,1)S(1)} %get-tuple-element.69), channel_id=1, source_target_pairs={{0,64},{1,65},{2,66},{3,67},{4,68},{5,69},{6,70},{7,71},{16,80},{1... | collective-permute-start | bytes 786440 | tf_op jit(solution)/shard_map/ppermute | solution.py:53
  56.0 23.6 %collective-permute-start.5 = (bf16[8,8,16,128]{3,2,1,0:T(8,128)(2,1)S(1)}, bf16[8,8,16,128]{3,2,1,0:T(8,128)(2,1)S(1)}, u32[]{:S(2)}, u32[]{:S(2)}) collective-permute-start(bf16[8,8,16,128]{3,2,1,0:T(8,128)(2,1)S(1)} %get-tuple-element.64), channel_id=1, source_target_pairs={{0,200},{1,201},{2,202},{3,203},{4,204},{5,205},{6,206},{7,207},{1... | collective-permute-start | bytes 786440 | tf_op jit(solution)/shard_map/ppermute | solution.py:53
  61.9 19.8 %collective-permute-start.6 = (bf16[8,8,16,128]{3,2,1,0:T(8,128)(2,1)S(1)}, bf16[8,8,16,128]{3,2,1,0:T(8,128)(2,1)S(1)}, u32[]{:S(2)}, u32[]{:S(2)}) collective-permute-start(bf16[8,8,16,128]{3,2,1,0:T(8,128)(2,1)S(1)} %get-tuple-element.65), channel_id=1, source_target_pairs={{0,8},{1,9},{2,10},{3,11},{4,12},{5,13},{6,14},{7,15},{16,24},{17,... | collective-permute-start | bytes 786440 | tf_op jit(solution)/shard_map/ppermute | solution.py:53
  68.4 47.0 %all-to-all-start = ((bf16[384,16,128]{2,1,0:T(8,128)(2,1)}), bf16[384,16,128]{2,1,0:T(8,128)(2,1)}, u32[]{:S(2)}, u32[]{:S(2)}) async-start(bf16[384,16,128]{2,1,0:T(8,128)(2,1)} %bitcast.4), calls=%async_computation | async-start | bytes 3145728 | tf_op jit(solution)/shard_map/all_to_all | solution.py:62
  79.6 40.5 %copy-start.4 = (bf16[8,8,16,128]{3,2,1,0:T(8,128)(2,1)}, bf16[8,8,16,128]{3,2,1,0:T(8,128)(2,1)S(1)}, u32[]{:S(2)}) copy-start(bf16[8,8,16,128]{3,2,1,0:T(8,128)(2,1)S(1)} %collective-permute-done.7.refs_2_) | copy-start | bytes 786436
  79.6 35.9 %copy-start.5 = (bf16[8,8,16,128]{3,2,1,0:T(8,128)(2,1)}, bf16[8,8,16,128]{3,2,1,0:T(8,128)(2,1)S(1)}, u32[]{:S(2)}) copy-start(bf16[8,8,16,128]{3,2,1,0:T(8,128)(2,1)S(1)} %collective-permute-done.8.refs_2_) | copy-start | bytes 786436
  79.7 40.4 %copy-start.6 = (bf16[8,8,16,128]{3,2,1,0:T(8,128)(2,1)}, bf16[8,8,16,128]{3,2,1,0:T(8,128)(2,1)S(1)}, u32[]{:S(2)}) copy-start(bf16[8,8,16,128]{3,2,1,0:T(8,128)(2,1)S(1)} %collective-permute-done.5.refs_1_) | copy-start | bytes 786436
  81.6 33.8 %copy-start.7 = (bf16[8,8,16,128]{3,2,1,0:T(8,128)(2,1)}, bf16[8,8,16,128]{3,2,1,0:T(8,128)(2,1)S(1)}, u32[]{:S(2)}) copy-start(bf16[8,8,16,128]{3,2,1,0:T(8,128)(2,1)S(1)} %collective-permute-done.6.refs_1_) | copy-start | bytes 786436
  81.7 14.9 %collective-permute-start.9 = (bf16[8,8,16,128]{3,2,1,0:T(8,128)(2,1)S(1)}, bf16[8,8,16,128]{3,2,1,0:T(8,128)(2,1)S(1)}, u32[]{:S(2)}, u32[]{:S(2)}) collective-permute-start(bf16[8,8,16,128]{3,2,1,0:T(8,128)(2,1)S(1)} %pad_maximum_fusion), channel_id=1, source_target_pairs={{0,192},{1,193},{2,194},{3,195},{4,196},{5,197},{6,198},{7,199},{1... | collective-permute-start | bytes 786440 | tf_op jit(solution)/shard_map/ppermute | solution.py:53
  82.9 16.0 %collective-permute-start.10 = (bf16[8,8,16,128]{3,2,1,0:T(8,128)(2,1)S(1)}, bf16[8,8,16,128]{3,2,1,0:T(8,128)(2,1)S(1)}, u32[]{:S(2)}, u32[]{:S(2)}) collective-permute-start(bf16[8,8,16,128]{3,2,1,0:T(8,128)(2,1)S(1)} %pad_maximum_fusion.1), channel_id=1, source_target_pairs={{0,64},{1,65},{2,66},{3,67},{4,68},{5,69},{6,70},{7,71},{16,80},{1... | collective-permute-start | bytes 786440 | tf_op jit(solution)/shard_map/ppermute | solution.py:53
  84.3 19.9 %collective-permute-start.11 = (bf16[4,8,16,128]{3,2,1,0:T(8,128)(2,1)S(1)}, bf16[4,8,16,128]{3,2,1,0:T(8,128)(2,1)S(1)}, u32[]{:S(2)}, u32[]{:S(2)}) collective-permute-start(bf16[4,8,16,128]{3,2,1,0:T(8,128)(2,1)S(1)} %slice.40), channel_id=1, source_target_pairs={{0,200},{1,201},{2,202},{3,203},{4,204},{5,205},{6,206},{7,207},{1... | collective-permute-start | bytes 393224 | tf_op jit(solution)/shard_map/ppermute | solution.py:53
  96.6 18.9 %copy-start.9 = (bf16[8,8,16,128]{3,2,1,0:T(8,128)(2,1)}, bf16[8,8,16,128]{3,2,1,0:T(8,128)(2,1)S(1)}, u32[]{:S(2)}) copy-start(bf16[8,8,16,128]{3,2,1,0:T(8,128)(2,1)S(1)} %collective-permute-done.9.refs_3_) | copy-start | bytes 786436
  98.9 21.2 %copy-start.10 = (bf16[8,8,16,128]{3,2,1,0:T(8,128)(2,1)}, bf16[8,8,16,128]{3,2,1,0:T(8,128)(2,1)S(1)}, u32[]{:S(2)}) copy-start(bf16[8,8,16,128]{3,2,1,0:T(8,128)(2,1)S(1)} %collective-permute-done.10.refs_3_) | copy-start | bytes 786436
  98.9 24.3 %collective-permute-start.13 = (bf16[8,8,16,128]{3,2,1,0:T(8,128)(2,1)S(1)}, bf16[8,8,16,128]{3,2,1,0:T(8,128)(2,1)S(1)}, u32[]{:S(2)}, u32[]{:S(2)}) collective-permute-start(bf16[8,8,16,128]{3,2,1,0:T(8,128)(2,1)S(1)} %pad_maximum_fusion.2), channel_id=1, source_target_pairs={{0,192},{1,193},{2,194},{3,195},{4,196},{5,197},{6,198},{7,199},{1... | collective-permute-start | bytes 786440 | tf_op jit(solution)/shard_map/ppermute | solution.py:53
  98.9 24.4 %collective-permute-start.14 = (bf16[8,8,16,128]{3,2,1,0:T(8,128)(2,1)}, bf16[8,8,16,128]{3,2,1,0:T(8,128)(2,1)S(1)}, u32[]{:S(2)}, u32[]{:S(2)}) collective-permute-start(bf16[8,8,16,128]{3,2,1,0:T(8,128)(2,1)} %pad_maximum_fusion.3), channel_id=1, source_target_pairs={{0,64},{1,65},{2,66},{3,67},{4,68},{5,69},{6,70},{7,71},{16,80},{1... | collective-permute-start | bytes 786440 | tf_op jit(solution)/shard_map/ppermute | solution.py:53
  101.2 14.2 %collective-permute-start.12 = (bf16[4,8,16,128]{3,2,1,0:T(8,128)(2,1)S(1)}, bf16[4,8,16,128]{3,2,1,0:T(8,128)(2,1)S(1)}, u32[]{:S(2)}, u32[]{:S(2)}) collective-permute-start(bf16[4,8,16,128]{3,2,1,0:T(8,128)(2,1)S(1)} %slice.40), channel_id=1, source_target_pairs={{0,8},{1,9},{2,10},{3,11},{4,12},{5,13},{6,14},{7,15},{16,24},{17,... | collective-permute-start | bytes 393224 | tf_op jit(solution)/shard_map/ppermute | solution.py:53
  101.3 21.4 %collective-permute-start.15 = (bf16[4,8,16,128]{3,2,1,0:T(8,128)(2,1)S(1)}, bf16[4,8,16,128]{3,2,1,0:T(8,128)(2,1)S(1)}, u32[]{:S(2)}, u32[]{:S(2)}) collective-permute-start(bf16[4,8,16,128]{3,2,1,0:T(8,128)(2,1)S(1)} %slice.41), channel_id=1, source_target_pairs={{0,200},{1,201},{2,202},{3,203},{4,204},{5,205},{6,206},{7,207},{1... | collective-permute-start | bytes 393224 | tf_op jit(solution)/shard_map/ppermute | solution.py:53
  104.2 11.3 %copy-start.13 = (bf16[4,8,16,128]{3,2,1,0:T(8,128)(2,1)}, bf16[4,8,16,128]{3,2,1,0:T(8,128)(2,1)S(1)}, u32[]{:S(2)}) copy-start(bf16[4,8,16,128]{3,2,1,0:T(8,128)(2,1)S(1)} %collective-permute-done.11.refs_4_) | copy-start | bytes 393220
  104.2 19.0 %collective-permute-start.16 = (bf16[4,8,16,128]{3,2,1,0:T(8,128)(2,1)S(1)}, bf16[4,8,16,128]{3,2,1,0:T(8,128)(2,1)S(1)}, u32[]{:S(2)}, u32[]{:S(2)}) collective-permute-start(bf16[4,8,16,128]{3,2,1,0:T(8,128)(2,1)S(1)} %slice.41), channel_id=1, source_target_pairs={{0,8},{1,9},{2,10},{3,11},{4,12},{5,13},{6,14},{7,15},{16,24},{17,... | collective-permute-start | bytes 393224 | tf_op jit(solution)/shard_map/ppermute | solution.py:53
  118.1 26.1 %collective-permute-start.17 = (bf16[256,1024]{1,0:T(8,128)(2,1)S(1)}, bf16[256,1024]{1,0:T(8,128)(2,1)S(1)}, u32[]{:S(2)}, u32[]{:S(2)}) collective-permute-start(bf16[256,1024]{1,0:T(8,128)(2,1)S(1)} %correlate.10), channel_id=1, source_target_pairs={{0,192},{1,193},{2,194},{3,195},{4,196},{5,197},{6,198},{7,199},{1... | collective-permute-start | bytes 1572872 | tf_op jit(solution)/shard_map/ppermute | solution.py:53
  122.7 26.4 %collective-permute-start.18 = (bf16[256,1024]{1,0:T(8,128)(2,1)S(1)}, bf16[256,1024]{1,0:T(8,128)(2,1)S(1)}, u32[]{:S(2)}, u32[]{:S(2)}) collective-permute-start(bf16[256,1024]{1,0:T(8,128)(2,1)S(1)} %correlate.11), channel_id=1, source_target_pairs={{0,64},{1,65},{2,66},{3,67},{4,68},{5,69},{6,70},{7,71},{16,80},{1... | collective-permute-start | bytes 1572872 | tf_op jit(solution)/shard_map/ppermute | solution.py:53
  126.5 38.1 %collective-permute-start.19 = (bf16[256,1024]{1,0:T(8,128)(2,1)S(1)}, bf16[256,1024]{1,0:T(8,128)(2,1)S(1)}, u32[]{:S(2)}, u32[]{:S(2)}) collective-permute-start(bf16[256,1024]{1,0:T(8,128)(2,1)S(1)} %correlate.12), channel_id=1, source_target_pairs={{0,192},{1,193},{2,194},{3,195},{4,196},{5,197},{6,198},{7,199},{1... | collective-permute-start | bytes 1572872 | tf_op jit(solution)/shard_map/ppermute | solution.py:53
  132.3 36.6 %collective-permute-start.20 = (bf16[256,1024]{1,0:T(8,128)(2,1)S(1)}, bf16[256,1024]{1,0:T(8,128)(2,1)S(1)}, u32[]{:S(2)}, u32[]{:S(2)}) collective-permute-start(bf16[256,1024]{1,0:T(8,128)(2,1)S(1)} %correlate.13), channel_id=1, source_target_pairs={{0,64},{1,65},{2,66},{3,67},{4,68},{5,69},{6,70},{7,71},{16,80},{1... | collective-permute-start | bytes 1572872 | tf_op jit(solution)/shard_map/ppermute | solution.py:53
  (8 other events, 27.1 us)
